TPU v7x, 32 devices: a whole 2x2x4 slice. The times are simulated.
32 devices in a mesh: dp: 8 (over z, y), heads: 4 (over x, core).
Axes of the slice: x: 2, y: 2, z: 4, core: 2. Of those that a mesh axis runs over, the one named last changes fastest.
Arguments:
- inputs: bfloat16 [8, 4096, 768], P('dp', 'heads'), may hold values from -6 to 6
- doc_lengths: int32 [8], P('dp'), may hold values from 3073 to 4096, as said below
- random_blocks: int32 [8, 64, 3], P('dp'), may hold values from 0 to 63
- qkv_weight: bfloat16 [768, 2304], replicated, may hold values from -0.21875 to 0.21875
- query_bias: bfloat16 [768], replicated, may hold values from -3 to 3
- value_bias: bfloat16 [768], replicated, may hold values from -0.1796875 to 0.1796875
- proj_weight: bfloat16 [768, 768], replicated, may hold values from -2.5 to 2.5
- proj_bias: bfloat16 [768], replicated, may hold values from -3 to 3
- first_gain: bfloat16 [768], replicated, may hold values from 0.099609375 to 1.8984375
- first_shift: bfloat16 [768], replicated, may hold values from -3 to 3
- expand_weight: bfloat16 [768, 3072], replicated, may hold values from -0.21875 to 0.21875
- expand_bias: bfloat16 [3072], replicated, may hold values from -3 to 3
- shrink_weight: bfloat16 [3072, 768], replicated, may hold values from -0.109375 to 0.109375
- shrink_bias: bfloat16 [768], replicated, may hold values from -3 to 3
- second_gain: bfloat16 [768], replicated, may hold values from 0.099609375 to 1.8984375
- second_shift: bfloat16 [768], replicated, may hold values from -3 to 3
- cotangent: bfloat16 [8, 4096, 768], P('dp', 'heads'), may hold values from -6 to 6
Outputs:
- output: bfloat16 [8, 4096, 768], P('dp', 'heads')
- input_grad: float32 [8, 4096, 768], P('dp', 'heads')
- grad_qkv_weight: float32 [768, 2304], replicated
- grad_query_bias: float32 [768], replicated
- grad_value_bias: float32 [768], replicated
- grad_proj_weight: float32 [768, 768], replicated
- grad_proj_bias: float32 [768], replicated
- grad_first_gain: float32 [768], replicated
- grad_first_shift: float32 [768], replicated
- grad_expand_weight: float32 [768, 3072], replicated
- grad_expand_bias: float32 [3072], replicated
- grad_shrink_weight: float32 [3072, 768], replicated
- grad_shrink_bias: float32 [768], replicated
- grad_second_gain: float32 [768], replicated
- grad_second_shift: float32 [768], replicated
Inputs may be any that keep to these rules, and one draw needn't show every extreme that they name: `doc_lengths`: one document fills all 4096 slots and one has exactly the least length.
All inputs are finite; a program needn't handle non-finite values.
Results may differ from a plain program's by a relative error of at most 0.015.
Values may be sent and summed in bfloat16 or wider, within the bound.
No kernel may reach another device: no remote copies, remote signals or barrier semaphores. Data moves between devices by JAX's collectives and lax.ppermute only.
A program may use at most 320 MiB of HBM per device.

v0:
```python
from functools import partial

import jax
import jax.numpy as jnp
from jax import lax
from jax.sharding import PartitionSpec as P

D = 768
HEADS = 12
HEAD_DIM = 64
BLOCK = 64
LEN = 4096


norm_epsilon = 1e-12
masked_score = -1e30
slot_count = 8


def layer_norm(values, scaling, offset):
    center = values - jnp.mean(values, axis=-1, keepdims=True)
    spread = jnp.mean(center * center, axis=-1, keepdims=True)
    return center * lax.rsqrt(spread + norm_epsilon) * scaling + offset


def product_tn(left, right):
    return lax.dot_general(
        left, right, (((0,), (0,)), ((), ())), preferred_element_type=jnp.float32
    )


def product_nt(left, right):
    return lax.dot_general(
        left, right, (((1,), (1,)), ((), ())), preferred_element_type=jnp.float32
    )


def block_plan(length, randoms):
    blocks = LEN // BLOCK
    last = (length + BLOCK - 1) // BLOCK - 1
    places = jnp.arange(blocks, dtype=jnp.int32)
    zeros_col = jnp.zeros((blocks,), jnp.int32)
    candidates = jnp.stack(
        [
            places - 1,
            places,
            places + 1,
            zeros_col,
            zeros_col + last,
            randoms[:, 0],
            randoms[:, 1],
            randoms[:, 2],
        ],
        axis=1,
    )
    in_range = (candidates >= 0) & (candidates < blocks)
    fresh = []
    for slot in range(slot_count):
        keep = in_range[:, slot]
        for earlier in range(slot):
            keep = keep & (candidates[:, earlier] != candidates[:, slot])
        fresh.append(keep)
    usable = jnp.stack(fresh, axis=1)
    picked = jnp.clip(candidates, 0, blocks - 1)
    key_place = picked[:, :, None] * BLOCK + jnp.arange(BLOCK, dtype=jnp.int32)[None, None, :]
    key_ok = (usable[:, :, None] & (key_place < length)).reshape(blocks, slot_count * BLOCK)
    first_sel = (places == 0)[:, None, None, None]
    last_sel = (places == last)[:, None, None, None]
    return (picked, key_ok, first_sel, last_sel, last)


def doc_parts(block_data, picked):
    blocks = LEN // BLOCK
    group_heads = block_data.shape[2]
    shape_blocks = (blocks, BLOCK, group_heads, HEAD_DIM)
    query_blocks = block_data[:, 0].reshape(shape_blocks)
    key_blocks = block_data[:, 1].reshape(shape_blocks)
    value_blocks = block_data[:, 2].reshape(shape_blocks)
    shape_picked = (blocks, slot_count * BLOCK, group_heads, HEAD_DIM)
    key_picked = key_blocks[picked].reshape(shape_picked)
    value_picked = value_blocks[picked].reshape(shape_picked)
    return (query_blocks, key_blocks, value_blocks, key_picked, value_picked)


def sparse_scores(query_blocks, key_picked, key_ok):
    raw = jnp.einsum(
        "nqhd,nkhd->nhqk", query_blocks, key_picked, preferred_element_type=jnp.float32
    ) * HEAD_DIM ** (-0.5)
    return jnp.where(key_ok[:, None, None, :], raw, masked_score)


def global_queries(blocks_in, last):
    return jnp.concatenate(
        [blocks_in[0], lax.dynamic_index_in_dim(blocks_in, last, 0, keepdims=False)], axis=0
    )


def global_scores(query_rows, keys, length):
    raw = jnp.einsum(
        "qhd,khd->hqk", query_rows, keys, preferred_element_type=jnp.float32
    ) * HEAD_DIM ** (-0.5)
    live = jnp.arange(LEN, dtype=jnp.int32) < length
    return jnp.where(live[None, None, :], raw, masked_score)


def forward_doc(items):
    block_data, length, randoms = items
    picked, key_ok, first_sel, last_sel, last = block_plan(length, randoms)
    query_blocks, key_blocks, value_blocks, key_picked, value_picked = doc_parts(block_data, picked)
    scores = sparse_scores(query_blocks, key_picked, key_ok)
    largest = jnp.max(scores, axis=-1, keepdims=True)
    weights = jnp.exp(scores - largest)
    totals = jnp.sum(weights, axis=-1, keepdims=True)
    shares = weights / totals
    sparse_context = jnp.einsum(
        "nhqk,nkhd->nqhd",
        shares.astype(jnp.bfloat16),
        value_picked,
        preferred_element_type=jnp.float32,
    )
    sparse_logsum = (largest + jnp.log(totals))[..., 0]
    query_rows = global_queries(query_blocks, last)
    wide_scores = global_scores(query_rows, block_data[:, 1], length)
    wide_largest = jnp.max(wide_scores, axis=-1, keepdims=True)
    wide_weights = jnp.exp(wide_scores - wide_largest)
    wide_totals = jnp.sum(wide_weights, axis=-1, keepdims=True)
    wide_shares = wide_weights / wide_totals
    wide_context = jnp.einsum(
        "hqk,khd->qhd",
        wide_shares.astype(jnp.bfloat16),
        block_data[:, 2],
        preferred_element_type=jnp.float32,
    )
    wide_context = wide_context.reshape(2, BLOCK, wide_context.shape[1], HEAD_DIM)
    wide_logsum = (wide_largest + jnp.log(wide_totals))[..., 0]
    context = jnp.where(
        first_sel, wide_context[0][None], jnp.where(last_sel, wide_context[1][None], sparse_context)
    )
    return (
        context.astype(jnp.bfloat16).reshape(LEN, context.shape[2], HEAD_DIM),
        sparse_logsum,
        wide_logsum,
    )


def backward_doc(items):
    block_data, length, randoms, sparse_logsum, wide_logsum, back_context = items
    blocks = LEN // BLOCK
    group_heads = block_data.shape[2]
    scale = HEAD_DIM ** (-0.5)
    picked, key_ok, first_sel, last_sel, last = block_plan(length, randoms)
    query_blocks, key_blocks, value_blocks, key_picked, value_picked = doc_parts(block_data, picked)
    scores = sparse_scores(query_blocks, key_picked, key_ok)
    shares = jnp.exp(scores - sparse_logsum[..., None])
    back_blocks = back_context.reshape(blocks, BLOCK, group_heads, HEAD_DIM)
    global_row = first_sel | last_sel
    back_sparse = jnp.where(global_row, jnp.zeros_like(back_blocks), back_blocks)
    back_value_picked = jnp.einsum(
        "nhqk,nqhd->nkhd",
        shares.astype(jnp.bfloat16),
        back_sparse,
        preferred_element_type=jnp.float32,
    )
    back_shares = jnp.einsum(
        "nqhd,nkhd->nhqk", back_sparse, value_picked, preferred_element_type=jnp.float32
    )
    inner_sum = jnp.sum(shares * back_shares, axis=-1, keepdims=True)
    back_scores = (shares * (back_shares - inner_sum)).astype(jnp.bfloat16)
    back_query_blocks = (
        jnp.einsum("nhqk,nkhd->nqhd", back_scores, key_picked, preferred_element_type=jnp.float32)
        * scale
    )
    back_key_picked = (
        jnp.einsum("nhqk,nqhd->nkhd", back_scores, query_blocks, preferred_element_type=jnp.float32)
        * scale
    )
    spread_shape = (blocks, slot_count, BLOCK, group_heads, HEAD_DIM)
    empty = jnp.zeros((blocks, BLOCK, group_heads, HEAD_DIM), jnp.float32)
    back_key_blocks = empty.at[picked].add(back_key_picked.reshape(spread_shape))
    back_value_blocks = empty.at[picked].add(back_value_picked.reshape(spread_shape))
    query_rows = global_queries(query_blocks, last)
    back_rows = global_queries(back_blocks, last)
    wide_scores = global_scores(query_rows, block_data[:, 1], length)
    wide_shares = jnp.exp(wide_scores - wide_logsum[..., None])
    back_values = back_value_blocks.reshape(LEN, group_heads, HEAD_DIM) + jnp.einsum(
        "hqk,qhd->khd",
        wide_shares.astype(jnp.bfloat16),
        back_rows,
        preferred_element_type=jnp.float32,
    )
    wide_back_shares = jnp.einsum(
        "qhd,khd->hqk", back_rows, block_data[:, 2], preferred_element_type=jnp.float32
    )
    wide_inner = jnp.sum(wide_shares * wide_back_shares, axis=-1, keepdims=True)
    wide_back_scores = (wide_shares * (wide_back_shares - wide_inner)).astype(jnp.bfloat16)
    wide_back_queries = (
        jnp.einsum(
            "hqk,khd->qhd", wide_back_scores, block_data[:, 1], preferred_element_type=jnp.float32
        )
        * scale
    )
    wide_back_queries = wide_back_queries.reshape(2, BLOCK, group_heads, HEAD_DIM)
    back_keys = (
        back_key_blocks.reshape(LEN, group_heads, HEAD_DIM)
        + jnp.einsum(
            "hqk,qhd->khd", wide_back_scores, query_rows, preferred_element_type=jnp.float32
        )
        * scale
    )
    zero_rows = jnp.zeros_like(back_query_blocks)
    back_queries = (
        back_query_blocks
        + jnp.where(first_sel, wide_back_queries[0][None], zero_rows)
        + jnp.where(last_sel, wide_back_queries[1][None], zero_rows)
    )
    back_queries = back_queries.reshape(LEN, group_heads, HEAD_DIM)
    return jnp.stack(
        [
            back_queries.astype(jnp.bfloat16),
            back_keys.astype(jnp.bfloat16),
            back_values.astype(jnp.bfloat16),
        ],
        axis=1,
    )


def per_device(
    inputs,
    doc_lengths,
    random_blocks,
    qkv_weight,
    query_bias,
    value_bias,
    proj_weight,
    proj_bias,
    first_gain,
    first_shift,
    expand_weight,
    expand_bias,
    shrink_weight,
    shrink_bias,
    second_gain,
    second_shift,
    cotangent,
):
    parts = lax.axis_size("heads")
    group_width = D // parts
    group_heads = HEADS // parts
    local_docs = inputs.shape[0]
    doc_rows = inputs.shape[1]
    tokens = local_docs * doc_rows
    flat_inputs = inputs.reshape(tokens, D)
    joined = jnp.dot(flat_inputs, qkv_weight, preferred_element_type=jnp.float32)
    bias_row = jnp.concatenate(
        [
            query_bias.astype(jnp.float32),
            jnp.zeros((D,), jnp.float32),
            value_bias.astype(jnp.float32),
        ]
    )
    joined = (joined + bias_row).astype(jnp.bfloat16)
    outgoing = joined.reshape(local_docs, doc_rows, 3, parts, group_width)
    arrived = lax.all_to_all(outgoing, "heads", split_axis=3, concat_axis=1, tiled=True)
    arrived = arrived.reshape(local_docs, LEN, 3, group_heads, HEAD_DIM)
    context, sparse_logsum, wide_logsum = lax.map(
        forward_doc, (arrived, doc_lengths, random_blocks)
    )
    context = context.reshape(local_docs, LEN, 1, group_width)
    context_rows = lax.all_to_all(
        context, "heads", split_axis=1, concat_axis=2, tiled=True
    ).reshape(tokens, D)
    branch = jnp.dot(
        context_rows, proj_weight, preferred_element_type=jnp.float32
    ) + proj_bias.astype(jnp.float32)
    resid_one = flat_inputs.astype(jnp.float32) + branch
    hidden, first_pull = jax.vjp(
        layer_norm, resid_one, first_gain.astype(jnp.float32), first_shift.astype(jnp.float32)
    )
    hidden_low = hidden.astype(jnp.bfloat16)
    inner = jnp.dot(
        hidden_low, expand_weight, preferred_element_type=jnp.float32
    ) + expand_bias.astype(jnp.float32)
    active, gelu_pull = jax.vjp(partial(jax.nn.gelu, approximate=False), inner)
    active_low = active.astype(jnp.bfloat16)
    resid_two = (
        hidden
        + jnp.dot(active_low, shrink_weight, preferred_element_type=jnp.float32)
        + shrink_bias.astype(jnp.float32)
    )
    output, second_pull = jax.vjp(
        layer_norm, resid_two, second_gain.astype(jnp.float32), second_shift.astype(jnp.float32)
    )
    back_two, grad_second_gain, grad_second_shift = second_pull(
        cotangent.reshape(tokens, D).astype(jnp.float32)
    )
    back_ffn = back_two.astype(jnp.bfloat16)
    grad_shrink = product_tn(active_low, back_ffn)
    grad_shrink_bias = jnp.sum(back_ffn.astype(jnp.float32), axis=0)
    back_active = product_nt(back_ffn, shrink_weight)
    back_inner = gelu_pull(back_active)[0].astype(jnp.bfloat16)
    grad_expand = product_tn(hidden_low, back_inner)
    grad_expand_bias = jnp.sum(back_inner.astype(jnp.float32), axis=0)
    back_hidden = back_two + product_nt(back_inner, expand_weight)
    back_one, grad_first_gain, grad_first_shift = first_pull(back_hidden)
    back_branch = back_one.astype(jnp.bfloat16)
    grad_proj = product_tn(context_rows, back_branch)
    grad_proj_bias = jnp.sum(back_branch.astype(jnp.float32), axis=0)
    back_context = product_nt(back_branch, proj_weight).astype(jnp.bfloat16)
    back_context = back_context.reshape(local_docs, doc_rows, parts, group_width)
    back_heads = lax.all_to_all(back_context, "heads", split_axis=2, concat_axis=1, tiled=True)
    back_heads = back_heads.reshape(local_docs, LEN, group_heads, HEAD_DIM)
    back_stacked = lax.map(
        backward_doc, (arrived, doc_lengths, random_blocks, sparse_logsum, wide_logsum, back_heads)
    )
    back_stacked = back_stacked.reshape(local_docs, LEN, 3, 1, group_width)
    back_joined = lax.all_to_all(
        back_stacked, "heads", split_axis=1, concat_axis=3, tiled=True
    ).reshape(tokens, 3 * D)
    grad_joined = product_tn(flat_inputs, back_joined)
    back_sums = jnp.sum(back_joined.astype(jnp.float32), axis=0)
    grad_query_bias = back_sums[:D]
    grad_value_bias = back_sums[2 * D :]
    input_grad = back_one + product_nt(back_joined, qkv_weight)
    grads = (
        grad_joined,
        grad_query_bias,
        grad_value_bias,
        grad_proj,
        grad_proj_bias,
        grad_first_gain,
        grad_first_shift,
        grad_expand,
        grad_expand_bias,
        grad_shrink,
        grad_shrink_bias,
        grad_second_gain,
        grad_second_shift,
    )
    flat_grads = jnp.concatenate([member.reshape(-1) for member in grads])
    total_count = flat_grads.shape[0]
    device_count = lax.axis_size("dp") * parts
    lane_width = 128
    rows_each = -(-total_count // (lane_width * device_count))
    padded = jnp.pad(flat_grads, (0, rows_each * lane_width * device_count - total_count))
    spread = padded.reshape(rows_each * lane_width, device_count).T.reshape(
        device_count * rows_each, lane_width
    )
    partial_sum = lax.psum_scatter(spread, ("dp", "heads"), scatter_dimension=0, tiled=True)
    summed = lax.all_gather(
        partial_sum.astype(jnp.bfloat16), ("dp", "heads"), axis=0, tiled=True
    ).astype(partial_sum.dtype)
    summed = summed.reshape(device_count, rows_each * lane_width).T.reshape(-1)
    results = []
    start_at = 0
    for member in grads:
        extent = member.size
        results.append(summed[start_at : start_at + extent].reshape(member.shape))
        start_at += extent
    output_rows = output.astype(jnp.bfloat16).reshape(local_docs, doc_rows, D)
    input_rows = input_grad.reshape(local_docs, doc_rows, D)
    return (output_rows, input_rows) + tuple(results)


def solution(mesh):
    in_specs = (
        P("dp", "heads", None),
        P("dp"),
        P("dp", None, None),
        P(),
        P(),
        P(),
        P(),
        P(),
        P(),
        P(),
        P(),
        P(),
        P(),
        P(),
        P(),
        P(),
        P("dp", "heads", None),
    )
    out_specs = (
        P("dp", "heads", None),
        P("dp", "heads", None),
        P(),
        P(),
        P(),
        P(),
        P(),
        P(),
        P(),
        P(),
        P(),
        P(),
        P(),
        P(),
        P(),
    )
    return jax.shard_map(
        per_device, mesh=mesh, in_specs=in_specs, out_specs=out_specs, check_vma=False
    )
```

profile of v0, /device:TPU:0, one launch (start us, length us, event | category | flops | bytes accessed | tf_op | source)
XLA Modules:
  0.0 2480.9 jit_solution(11330320745470865450)
XLA Ops:
  49.4 38.5 %all-to-all-done = bf16[1,1024,3,4,192]{1,4,2,0,3:T(8,128)(2,1)} async-done(((bf16[1,1024,3,4,192]{1,4,2,0,3:T(8,128)(2,1)}), bf16[1,1024,3,4,192]{1,4,2,0,3:T(8,128)(2,1)}, u32[]{:S(2)}, u32[]{:S(2)}) %all-to-all-start) | async-done | bytes 4718624 | tf_op jit(solution)/shard_map/all_to_all | solution.py:263
  139.9 34.0 %copy.389 = bf16[512,64,3,64]{1,0,3,2:T(8,128)(2,1)} copy(bf16[512,64,3,64]{3,1,2,0:T(8,128)(2,1)} %gather_fusion.1) | data formatting | bytes 25165824 | tf_op jit(solution)/shard_map/while/body/eval_jaxpr/gather | solution.py:80
  173.8 33.1 %reshape.492 = bf16[64,512,3,64]{1,0,3,2:T(8,128)(2,1)} reshape(bf16[512,64,3,64]{1,0,3,2:T(8,128)(2,1)} %copy.389) | data formatting | bytes 25165824 | tf_op jit(solution)/shard_map/while/body/eval_jaxpr/reshape | solution.py:80
  258.5 34.0 %copy.385 = bf16[512,64,3,64]{1,0,3,2:T(8,128)(2,1)} copy(bf16[512,64,3,64]{3,1,2,0:T(8,128)(2,1)} %gather_fusion) | data formatting | bytes 25165824 | tf_op jit(solution)/shard_map/while/body/eval_jaxpr/gather | solution.py:81
  292.5 33.1 %reshape.491 = bf16[64,512,3,64]{1,0,3,2:T(8,128)(2,1)} reshape(bf16[512,64,3,64]{1,0,3,2:T(8,128)(2,1)} %copy.385) | data formatting | bytes 25165824 | tf_op jit(solution)/shard_map/while/body/eval_jaxpr/reshape | solution.py:81
  325.6 28.5 %fusion.20 = (f32[64,3,64]{2,1,0:T(4,128)}, f32[64,3,64,512]{3,2,1,0:T(8,128)}) fusion(pred[64,512]{1,0:T(8,128)(4,1)} %fusion.70, bf16[64,64,3,64]{3,1,2,0:T(8,128)(2,1)} %copy.381, bf16[64,512,3,64]{1,0,3,2:T(8,128)(2,1)} %reshape.492), kind=kOutput, calls=%fused_computation.42 | convolution fusion | flops 824168448 | bytes 39403520 | tf_op jit(solution)/shard_map/while/body/eval_jaxpr/nqhd,nkhd->nhqk/dot_general | solution.py:86
  494.4 38.7 %multiply_convert_fusion.1 = (bf16[1024,3072]{1,0:T(8,128)(2,1)}, f32[1024,3072]{1,0:T(8,128)}, f32[1024,3072]{1,0:T(8,128)}) fusion(f32[3072]{0:T(1024)S(1)} %copy-done.50, bf16[768,3072]{1,0:T(8,128)(2,1)} %param.27, f32[1024,768]{0,1:T(8,128)S(1)} %get-tuple-element.232, f32[768]{0:T(1024)S(1)} %copy-done.55, f32[768]{0:T(1024)S(1)} %convert_element_type.138, ...), kind=kOutput, calls=%fused_computation.20 | convolution fusion | flops 5043388416 | bytes 39348224 | tf_op jit(solution)/shard_map/dot_general | solution.py:280
  623.7 36.3 %multiply_reduce_fusion = (f32[64,3,64]{2,1,0:T(4,128)}, f32[64,3,64,512]{3,2,1,0:T(8,128)}) fusion(f32[64,3,64]{2,1,0:T(4,128)} %log_add_fusion, f32[64,3,64,512]{3,2,1,0:T(8,128)} %get-tuple-element.230, pred[64,512]{1,0:T(8,128)(4,1)} %fusion.70, bf16[64,512,3,64]{1,0,3,2:T(8,128)(2,1)} %reshape.491, bf16[64,64,3,64]{1,0,3,2:T(8,128)(2,1)} %broadcast_select_fusion), kind=kOutput, calls=%fused_computation.7 | convolution fusion | flops 836751360 | bytes 64618496 | tf_op jit(solution)/shard_map/while/body/eval_jaxpr/nqhd,nkhd->nhqk/dot_general | solution.py:164
  735.9 26.5 %fusion.25 = bf16[64,64,3,64]{1,3,2,0:T(8,128)(2,1)} fusion(f32[64,3,64]{0,2,1:T(8,128)} %get-tuple-element.214, f32[64,3,64]{0,2,1:T(8,128)} %get-tuple-element.213, pred[64]{0:T(512)(128)(4,1)S(1)} %copy-done.62, pred[64]{0:T(512)(128)(4,1)S(1)} %copy-done.60, bf16[64,3,64,512]{3,2,1,0:T(8,128)(2,1)} %multiply_convert_fusion, ...), kind=kOutput, calls=%fused_computation.48 | convolution fusion | flops 810024960 | bytes 26837120 | tf_op jit(solution)/shard_map/while/body/eval_jaxpr/nhqk,nkhd->nqhd/dot_general | solution.py:170
  797.9 36.4 %reshape.536 = f32[512,64,3,64]{1,0,3,2:T(8,128)} reshape(f32[64,512,3,64]{1,0,3,2:T(8,128)} %copy.409) | data formatting | bytes 50331648 | tf_op jit(solution)/shard_map/while/body/eval_jaxpr/reshape | solution.py:179
  834.3 52.2 %copy.411 = f32[512,64,3,64]{3,1,2,0:T(8,128)} copy(f32[512,64,3,64]{1,0,3,2:T(8,128)} %reshape.536) | data formatting | bytes 50331648 | tf_op jit(solution)/shard_map/while/body/eval_jaxpr/reshape | solution.py:179
  890.1 123.4 %scatter_fusion = f32[64,64,3,64]{3,1,2,0:T(8,128)} fusion(f32[64,64,3,64]{3,1,2,0:T(8,128)} %broadcast.407.clone2.1, s32[512]{0:T(512)S(1)} %copy-done.15, f32[512,64,3,64]{3,1,2,0:T(8,128)} %copy.411), kind=kCustom, calls=%fused_computation.2 | custom fusion | flops 6291456 | bytes 75499520 | tf_op jit(solution)/shard_map/while/body/eval_jaxpr/scatter-add | solution.py:179
  1056.0 36.4 %reshape.544 = f32[512,64,3,64]{1,0,3,2:T(8,128)} reshape(f32[64,512,3,64]{1,0,3,2:T(8,128)} %copy.414) | data formatting | bytes 50331648 | tf_op jit(solution)/shard_map/while/body/eval_jaxpr/reshape | solution.py:180
  1092.4 52.2 %copy.416 = f32[512,64,3,64]{3,1,2,0:T(8,128)} copy(f32[512,64,3,64]{1,0,3,2:T(8,128)} %reshape.544) | data formatting | bytes 50331648 | tf_op jit(solution)/shard_map/while/body/eval_jaxpr/reshape | solution.py:180
  1148.2 123.4 %scatter_fusion.1 = f32[64,64,3,64]{3,1,2,0:T(8,128)} fusion(f32[64,64,3,64]{3,1,2,0:T(8,128)} %broadcast.407.clone2, s32[512]{0:T(512)S(1)} %copy-done.15, f32[512,64,3,64]{3,1,2,0:T(8,128)} %copy.416), kind=kCustom, calls=%fused_computation.3 | custom fusion | flops 6291456 | bytes 75499520 | tf_op jit(solution)/shard_map/while/body/eval_jaxpr/scatter-add | solution.py:180
  1353.6 50.2 %all-to-all-done.3 = bf16[1,4096,3,1,192]{4,2,3,0,1:T(4,128)(2,1)} async-done(((bf16[1,4096,3,1,192]{4,2,3,0,1:T(4,128)(2,1)}), bf16[1,4096,3,1,192]{4,2,3,0,1:T(4,128)(2,1)}, u32[]{:S(2)}, u32[]{:S(2)}) %all-to-all-start.3) | async-done | bytes 4718624 | tf_op jit(solution)/shard_map/all_to_all | solution.py:316
  1484.8 80.3 %dynamic-update-slice.7 = f32[7087104]{0:T(1024)} dynamic-update-slice(f32[7087104]{0:T(1024)} %constant_dynamic-update-slice_fusion.11, f32[2359296]{0:T(1024)} %bitcast.229, s32[]{} %constant.208) | dynamic-update-slice | bytes 18874372
  1566.4 80.4 %dynamic-update-slice.9 = f32[7087104]{0:T(1024)} dynamic-update-slice(f32[7087104]{0:T(1024)} %constant_dynamic-update-slice_fusion.10, f32[2359296]{0:T(1024)} %reshape.507, s32[]{} %constant.210) | dynamic-update-slice | bytes 18874372
  1671.4 66.8 %reshape.508 = f32[221568,32]{1,0:T(8,128)} reshape(f32[7090176]{0:T(1024)} %pad.4) | data formatting | bytes 56721408 | tf_op jit(solution)/shard_map/reshape | solution.py:345
  1738.2 66.8 %copy.425 = f32[32,221568]{1,0:T(8,128)} copy(f32[32,221568]{0,1:T(8,128)} %bitcast.38) | data formatting | bytes 56721408 | tf_op jit(solution)/shard_map/transpose | solution.py:345
  1830.5 303.9 %fusion = f32[1744,128]{1,0:T(8,128)} fusion(f32[55392,128]{1,0:T(8,128)} %reshape.509), kind=kCustom, calls=%all-reduce-scatter | all-reduce-scatter fusion | flops 7143425 | bytes 29253632
  2161.1 97.9 %all-gather.3.cloned.1.call-done = bf16[32,1731,128]{2,1,0:T(8,128)(2,1)} async-done(((bf16[1,1731,128]{2,1,0:T(8,128)(2,1)}), bf16[32,1731,128]{2,1,0:T(8,128)(2,1)}) %all-gather.3.cloned.1.call-update) | async-done | bytes 14180368 | tf_op jit(solution)/shard_map/all_gather | solution.py:349
  2325.4 27.7 %reshape.513 = f32[768,3072]{1,0:T(8,128)} reshape(f32[73728,32]{1,0:T(8,128)} %copy.433) | data formatting | bytes 18874368 | tf_op jit(solution)/shard_map/reshape | solution.py:357
  2374.2 25.8 %reshape.514 = f32[3072,768]{1,0:T(8,128)} reshape(f32[73728,32]{1,0:T(8,128)} %copy.435) | data formatting | bytes 18874368 | tf_op jit(solution)/shard_map/reshape | solution.py:357
  (332 shorter events, 938.5 us)
Async XLA Ops:
  28.1 59.7 %all-to-all-start = ((bf16[1,1024,3,4,192]{1,4,2,0,3:T(8,128)(2,1)}), bf16[1,1024,3,4,192]{1,4,2,0,3:T(8,128)(2,1)}, u32[]{:S(2)}, u32[]{:S(2)}) async-start(bf16[1,1024,3,4,192]{1,4,2,0,3:T(8,128)(2,1)} %copy.379), calls=%async_computation | async-start | bytes 9437184 | tf_op jit(solution)/shard_map/all_to_all | solution.py:263
  46.6 58.2 %copy-start.14 = (s32[512]{0:T(512)}, s32[512]{0:T(512)S(1)}, u32[]{:S(2)}) copy-start(s32[512]{0:T(512)S(1)} %reshape.518) | copy-start | bytes 6148
  444.5 24.5 all-to-all-start.1
  452.7 125.0 %copy-start.44 = (f32[768]{0:T(1024)}, f32[768]{0:T(1024)S(1)}, u32[]{:S(2)}) copy-start(f32[768]{0:T(1024)S(1)} %convert_element_type.138) | copy-start | bytes 9220
  489.9 43.2 %slice-start = ((s8[4718592]{0:T(1024)(128)(4,1)}), s8[4194304]{0:T(1024)(128)(4,1)S(1)}, s32[]{:S(2)}) async-start(s8[4718592]{0:T(1024)(128)(4,1)} %bitcast.248), calls=%async_computation.5 | async-start | bytes 8388608
  493.9 39.2 %copy-start.8 = (f32[1024,768]{0,1:T(8,128)}, f32[1024,768]{0,1:T(8,128)S(1)}, u32[]{:S(2)}) copy-start(f32[1024,768]{0,1:T(8,128)S(1)} %get-tuple-element.232) | copy-start | bytes 9437188
  494.0 83.8 %copy-start.34 = (f32[1024]{0:T(1024)}, f32[1024]{0:T(1024)S(1)}, u32[]{:S(2)}) copy-start(f32[1024]{0:T(1024)S(1)} %broadcast_multiply_fusion.1) | copy-start | bytes 12292
  494.4 83.4 %copy-start.46 = (f32[1024]{0:T(1024)}, f32[1024]{0:T(1024)S(1)}, u32[]{:S(2)}) copy-start(f32[1024]{0:T(1024)S(1)} %fusion.71) | copy-start | bytes 12292
  494.4 38.7 %slice-start.1 = ((s8[4718592]{0:T(1024)(128)(4,1)}), s8[524288]{0:T(1024)(128)(4,1)S(1)}, s32[]{:S(2)}) async-start(s8[4718592]{0:T(1024)(128)(4,1)} %bitcast.248), calls=%async_computation.6 | async-start | bytes 1048576
  547.4 18.1 copy-start.21
  583.7 36.2 %copy-start.57 = (pred[64]{0:T(512)(128)(4,1)S(1)}, pred[64]{0:T(512)(128)(4,1)}, u32[]{:S(2)}) copy-start(pred[64]{0:T(512)(128)(4,1)} %get-tuple-element.244) | copy-start | bytes 196
  583.7 25.0 %all-to-all-start.2 = ((bf16[1,1024,4,192]{1,3,0,2:T(8,128)(2,1)}), bf16[1,1024,4,192]{1,3,0,2:T(8,128)(2,1)}, u32[]{:S(2)}, u32[]{:S(2)}) async-start(bf16[1,1024,4,192]{1,3,0,2:T(8,128)(2,1)} %bitcast.241), calls=%async_computation.2 | async-start | bytes 3145728 | tf_op jit(solution)/shard_map/all_to_all | solution.py:310
  588.6 98.5 %copy-start.36 = (f32[3,128]{1,0:T(4,128)}, f32[3,128]{1,0:T(4,128)S(1)}, u32[]{:S(2)}) copy-start(f32[3,128]{1,0:T(4,128)S(1)} %log_add_fusion.1) | copy-start | bytes 4612
  660.0 22.1 copy-start.31
  660.0 22.1 copy-start.30
  718.5 17.3 copy-start.62
  1304.9 98.9 %all-to-all-start.3 = ((bf16[1,4096,3,1,192]{4,2,3,0,1:T(4,128)(2,1)}), bf16[1,4096,3,1,192]{4,2,3,0,1:T(4,128)(2,1)}, u32[]{:S(2)}, u32[]{:S(2)}) async-start(bf16[1,4096,3,1,192]{4,2,3,0,1:T(4,128)(2,1)} %copy.418), calls=%async_computation.3 | async-start | bytes 16777216 | tf_op jit(solution)/shard_map/all_to_all | solution.py:316
  1310.6 948.4 %all-gather.3.cloned.1.call-start = ((), (), s32[]{:S(2)}) async-start(), calls=%async_computation.4 | async-start | bytes 14665728 | tf_op jit(solution)/shard_map/all_gather | solution.py:349
  1448.4 32.4 %copy-start.48 = (f32[768]{0:T(1024)S(1)}, f32[768]{0:T(1024)}, u32[]{:S(2)}) copy-start(f32[768]{0:T(1024)} %get-tuple-element.189) | copy-start | bytes 9220
  1484.7 80.3 %copy-start.49 = (f32[3072]{0:T(1024)S(1)}, f32[3072]{0:T(1024)}, u32[]{:S(2)}) copy-start(f32[3072]{0:T(1024)} %get-tuple-element.241) | copy-start | bytes 36868
  1566.4 80.4 %copy-start.43 = (f32[768]{0:T(1024)S(1)}, f32[768]{0:T(1024)}, u32[]{:S(2)}) copy-start(f32[768]{0:T(1024)} %get-tuple-element.187) | copy-start | bytes 9220
  1566.4 81.7 %copy-start.42 = (f32[768]{0:T(1024)S(1)}, f32[768]{0:T(1024)}, u32[]{:S(2)}) copy-start(f32[768]{0:T(1024)} %get-tuple-element.182) | copy-start | bytes 9220
  1830.5 319.1 %copy-start.41 = (f32[1024]{0:T(1024)S(1)}, f32[1024]{0:T(1024)}, u32[]{:S(2)}) copy-start(f32[1024]{0:T(1024)} %copy-done.40) | copy-start | bytes 12292
  2135.9 4.1 collective-permute-start
  (47 other events, 350.6 us)
Sparse Core Ops, SparseCore 0:
  2147.1 111.8 all-gather.2
where the time goes:
time: 2520 us; the launch traced here: 2480 us
  local copies, waits for them, and re-layouts  1270 us (50%)
  other arithmetic  346 us (14%)
  blocking collectives  304 us (12%)
  matrix products  302 us (12%)
  waiting for transfers between devices  215 us (9%)
    unnamed x1, blocking collectives  304 us
    unnamed x159, local copies, waits for them, and re-layouts  260 us
    scatter-add x1, other arithmetic, backward_doc(): empty.at[picked].add(back_key_picked.reshape(spread_shape))  123 us
    scatter-add x1, other arithmetic, backward_doc(): empty.at[picked].add(back_value_picked.reshape(spread_shape))  123 us
    slice x27, local copies, waits for them, and re-layouts, per_device(): results.append(summed[start_at:start_at + extent].reshape(member.shape))  115 us
    all_gather x1, waiting for transfers between devices, per_device(): lax.all_gather(partial_sum.astype(jnp.bfloat16), ('dp', 'heads'), axis=0,...  97.9 us
    reshape x2, local copies, waits for them, and re-layouts, per_device(): padded.reshape(rows_each * lane_width, device_count)  92.2 us
    reshape x2, local copies, waits for them, and re-layouts, backward_doc(): back_key_picked.reshape(spread_shape)  88.7 us
  transfers between devices with their start and end apart: 6, of which 6 were waited for; matrix products, arithmetic and copies ran while one was open for 3% of the time, Pallas kernels for 0%

commit v1 on v0

v1 whole, which is shorter than its diff:
```python
from functools import partial

import jax
import jax.numpy as jnp
from jax import lax
from jax.experimental import pallas as pl
from jax.experimental.pallas import tpu as pltpu
from jax.sharding import Mesh
from jax.sharding import PartitionSpec as P

D = 768
HEADS = 12
HEAD_DIM = 64
BLOCK = 64
SLOTS = 8
norm_epsilon = 1e-12
masked_score = -1e30
f32 = jnp.float32
bf16 = jnp.bfloat16


def dot_nn(left, right):
    return lax.dot_general(left, right, (((1,), (0,)), ((), ())), preferred_element_type=f32)


def dot_nt(left, right):
    return lax.dot_general(left, right, (((1,), (1,)), ((), ())), preferred_element_type=f32)


def dot_tn(left, right):
    return lax.dot_general(left, right, (((0,), (0,)), ((), ())), preferred_element_type=f32)


def layer_norm(values, scaling, offset):
    center = values - jnp.mean(values, axis=-1, keepdims=True)
    spread = jnp.mean(center * center, axis=-1, keepdims=True)
    return center * lax.rsqrt(spread + norm_epsilon) * scaling + offset


def block_plan(length, randoms, flip, query_blocks):
    blocks = randoms.shape[0]
    last = (length + BLOCK - 1) // BLOCK - 1
    places = jnp.arange(query_blocks, dtype=jnp.int32) ^ flip
    own_randoms = jnp.take_along_axis(randoms, places[:, None], axis=0)
    zero = jnp.zeros((query_blocks,), jnp.int32)
    candidates = jnp.concatenate(
        [
            jnp.stack([places - 1, places, places + 1, zero, zero + last], axis=1),
            own_randoms,
        ],
        axis=1,
    )
    usable = (candidates >= 0) & (candidates < blocks)
    same = candidates[:, :, None] == candidates[:, None, :]
    before = jnp.arange(SLOTS)[:, None] > jnp.arange(SLOTS)[None, :]
    usable = usable & ~jnp.any(same & before[None], axis=2)
    is_global = (places == 0) | (places == last)
    usable = usable & ~is_global[:, None]
    names = jnp.clip(candidates, 0, blocks - 1) ^ flip
    global_name = jnp.where((flip ^ last) < query_blocks, flip ^ last, flip)
    every = jnp.arange(blocks, dtype=jnp.int32).reshape(blocks // SLOTS, SLOTS)
    query_names = jnp.concatenate(
        [
            jnp.arange(query_blocks, dtype=jnp.int32),
            jnp.zeros((blocks // SLOTS,), jnp.int32) + global_name,
        ]
    )
    key_names = jnp.concatenate([names, every])
    bias_names = jnp.concatenate([jnp.where(usable, names, blocks), every])
    return query_names, key_names, bias_names, global_name.reshape(1)


def halves(pair):
    lane = lax.broadcasted_iota(jnp.int32, pair.shape, 1)
    zero = jnp.zeros_like(pair)
    return jnp.concatenate(
        [jnp.where(lane < HEAD_DIM, pair, zero), jnp.where(lane < HEAD_DIM, zero, pair)], axis=0
    )


def join_halves(stacked):
    lane = lax.broadcasted_iota(jnp.int32, (BLOCK, 2 * HEAD_DIM), 1)
    return jnp.where(lane < HEAD_DIM, stacked[:BLOCK], stacked[BLOCK:])


def block_rows(name):
    return pl.ds(pl.multiple_of(name * BLOCK, BLOCK), BLOCK)


def gather_blocks(ref, names):
    return jnp.concatenate([ref[block_rows(name), :] for name in names], axis=0)


def fill_length_bias(bias_scratch, length, flip):
    rows = bias_scratch.shape[0] - BLOCK
    place = lax.broadcasted_iota(jnp.int32, bias_scratch.shape, 0)
    token = (((place // BLOCK) ^ flip) * BLOCK) + place % BLOCK
    live = (token < length) & (place < rows)
    bias_scratch[...] = jnp.where(live, 0.0, masked_score)


def forward_kernel(
    key_names, bias_names, global_name, lengths, flips,
    q_ref, k_ref, v_ref, context_ref, logsum_ref, bias_scratch, score_scratch, *, unroll, query_blocks,
):
    @pl.when(pl.program_id(0) == 0)
    def _():
        fill_length_bias(bias_scratch, lengths[0], flips[0])

    def put(block, context, largest, total):
        context_ref[block_rows(block), :] = join_halves(context).astype(bf16)
        logsum_ref[0, pl.ds(block, 1), :] = largest + jnp.log(total)

    def one(block):
        queries = halves(q_ref[block_rows(block), :])
        names = [key_names[block, slot] for slot in range(SLOTS)]
        biases = [bias_names[block, slot] for slot in range(SLOTS)]
        scores = dot_nt(gather_blocks(k_ref, names), queries) + gather_blocks(bias_scratch, biases)
        largest = jnp.max(scores, axis=0, keepdims=True)
        weights = jnp.exp(scores - largest)
        total = jnp.sum(weights, axis=0, keepdims=True)
        shares = (weights * (1.0 / total)).astype(bf16)
        put(block, dot_tn(shares, gather_blocks(v_ref, names)), largest, total)

    def body(step, carry):
        for within in range(unroll):
            one(step * unroll + within)
        return carry

    lax.fori_loop(0, query_blocks // unroll, body, 0)
    block = global_name[0]
    queries = halves(q_ref[block_rows(block), :])
    tokens = k_ref.shape[0]
    chunk = SLOTS * BLOCK
    together = 4

    def score_chunk(step, largest):
        for within in range(together):
            rows = pl.ds(pl.multiple_of((step * together + within) * chunk, chunk), chunk)
            scores = dot_nt(k_ref[rows, :], queries) + bias_scratch[rows, :]
            score_scratch[rows, :] = scores
            largest = jnp.maximum(largest, jnp.max(scores, axis=0, keepdims=True))
        return largest

    steps = tokens // chunk // together
    lanes = 2 * BLOCK
    largest = lax.fori_loop(0, steps, score_chunk, jnp.full((1, lanes), masked_score, f32))

    def value_chunk(step, carry):
        total, context = carry
        for within in range(together):
            rows = pl.ds(pl.multiple_of((step * together + within) * chunk, chunk), chunk)
            weights = jnp.exp(score_scratch[rows, :] - largest)
            total = total + jnp.sum(weights, axis=0, keepdims=True)
            context = context + dot_tn(weights.astype(bf16), v_ref[rows, :])
        return total, context

    total, context = lax.fori_loop(
        0, steps, value_chunk, (jnp.zeros((1, lanes), f32), jnp.zeros((lanes, lanes), f32))
    )
    context = context * jnp.transpose(jnp.broadcast_to(1.0 / total, (lanes, lanes)))
    put(block, context, largest, total)


def attend(plan, length, flip, q, k, v):
    query_names, key_names, bias_names, global_name = plan
    query_rows, width = q.shape
    tokens = k.shape[0]
    pairs = width // 128
    query_blocks = query_rows // BLOCK
    q_spec = pl.BlockSpec((query_rows, 128), lambda pair, *_: (0, pair))
    k_spec = pl.BlockSpec((tokens, 128), lambda pair, *_: (0, pair))
    return pl.pallas_call(
        partial(forward_kernel, unroll=8, query_blocks=query_blocks),
        grid_spec=pltpu.PrefetchScalarGridSpec(
            num_scalar_prefetch=5,
            grid=(pairs,),
            in_specs=[q_spec, k_spec, k_spec],
            out_specs=[q_spec, pl.BlockSpec((1, query_blocks, 128), lambda pair, *_: (pair, 0, 0))],
            scratch_shapes=[
                pltpu.VMEM((tokens + BLOCK, 128), f32),
                pltpu.VMEM((tokens, 128), f32),
            ],
        ),
        out_shape=[
            jax.ShapeDtypeStruct(q.shape, bf16),
            jax.ShapeDtypeStruct((pairs, query_blocks, 128), f32),
        ],
        compiler_params=pltpu.CompilerParams(vmem_limit_bytes=48 << 20),
        cost_estimate=pl.CostEstimate(flops=40 * 10**9, bytes_accessed=10**7, transcendentals=10**7),
        name="attend_forward",
    )(key_names, bias_names, global_name, length, flip, q, k, v)


def backward_kernel(
    query_names, key_names, bias_names, lengths, flips,
    q_ref, k_ref, v_ref, back_ref, context_ref, logsum_ref,
    back_q_ref, back_k_ref, back_v_ref, bias_scratch, q_scratch, k_scratch, v_scratch, *, unroll, items,
):
    @pl.when(pl.program_id(0) == 0)
    def _():
        fill_length_bias(bias_scratch, lengths[0], flips[0])

    q_scratch[...] = jnp.zeros_like(q_scratch)
    k_scratch[...] = jnp.zeros_like(k_scratch)
    v_scratch[...] = jnp.zeros_like(v_scratch)
    ones = jnp.ones((16, 128), bf16)

    def one(item):
        block = query_names[item]
        rows = block_rows(block)
        queries = halves(q_ref[rows, :])
        back = back_ref[rows, :]
        backs = halves(back)
        product = (back.astype(f32) * context_ref[rows, :].astype(f32)).astype(bf16)
        inner = dot_nt(ones, halves(product))[0:1]
        logsum = logsum_ref[0, pl.ds(block, 1), :]
        names = [key_names[item, slot] for slot in range(SLOTS)]
        biases = [bias_names[item, slot] for slot in range(SLOTS)]
        keys = gather_blocks(k_ref, names)
        scores = dot_nt(keys, queries) + gather_blocks(bias_scratch, biases)
        shares = jnp.exp(scores - logsum)
        back_shares = dot_nt(gather_blocks(v_ref, names), backs)
        back_values = dot_nn(shares.astype(bf16), backs)
        back_scores = (shares * (back_shares - inner)).astype(bf16)
        back_keys = dot_nn(back_scores, queries)
        q_scratch[rows, :] += join_halves(dot_tn(back_scores, keys))
        for slot in range(SLOTS):
            part = slice(slot * BLOCK, (slot + 1) * BLOCK)
            v_scratch[block_rows(names[slot]), :] += back_values[part]
            k_scratch[block_rows(names[slot]), :] += back_keys[part]

    def body(step, carry):
        for within in range(unroll):
            one(step * unroll + within)
        return carry

    lax.fori_loop(0, items // unroll, body, 0)
    back_q_ref[...] = (q_scratch[...] * HEAD_DIM ** (-0.5)).astype(bf16)
    back_k_ref[...] = k_scratch[...].astype(bf16)
    back_v_ref[...] = v_scratch[...].astype(bf16)


def attend_back(plan, length, flip, q, k, v, back, context, logsum):
    query_names, key_names, bias_names, _ = plan
    query_rows, width = q.shape
    tokens = k.shape[0]
    pairs = width // 128
    query_blocks = query_rows // BLOCK
    q_spec = pl.BlockSpec((query_rows, 128), lambda pair, *_: (0, pair))
    k_spec = pl.BlockSpec((tokens, 128), lambda pair, *_: (0, pair))
    return pl.pallas_call(
        partial(backward_kernel, unroll=8, items=query_names.shape[0]),
        grid_spec=pltpu.PrefetchScalarGridSpec(
            num_scalar_prefetch=5,
            grid=(pairs,),
            in_specs=[
                q_spec, k_spec, k_spec, q_spec, q_spec,
                pl.BlockSpec((1, query_blocks, 128), lambda pair, *_: (pair, 0, 0)),
            ],
            out_specs=[q_spec, k_spec, k_spec],
            scratch_shapes=[
                pltpu.VMEM((tokens + BLOCK, 128), f32),
                pltpu.VMEM((query_rows, 128), f32),
                pltpu.VMEM((tokens, 128), f32),
                pltpu.VMEM((tokens, 128), f32),
            ],
        ),
        out_shape=[
            jax.ShapeDtypeStruct(q.shape, bf16),
            jax.ShapeDtypeStruct(k.shape, bf16),
            jax.ShapeDtypeStruct(k.shape, bf16),
        ],
        compiler_params=pltpu.CompilerParams(vmem_limit_bytes=56 << 20),
        cost_estimate=pl.CostEstimate(flops=60 * 10**9, bytes_accessed=10**7, transcendentals=10**7),
        name="attend_backward",
    )(query_names, key_names, bias_names, length, flip, q, k, v, back, context, logsum)


def swap(value, axis, bit=1):
    size = lax.axis_size(axis)
    return lax.ppermute(value, axis, [(place, place ^ bit) for place in range(size)])


def exchange_steps():
    steps = []
    bit = 1
    while bit < lax.axis_size("dp"):
        steps.append(("dp", bit))
        bit *= 2
    return steps


def sum_everywhere(value, steps):
    for axis, bit in steps:
        half = value.shape[0] // 2
        upper = (lax.axis_index(axis) & bit) // bit
        keep = lax.dynamic_slice_in_dim(value, upper * half, half, 0)
        send = lax.dynamic_slice_in_dim(value, (1 - upper) * half, half, 0)
        value = (keep.astype(f32) + swap(send, axis, bit).astype(f32)).astype(bf16)
    for axis, bit in reversed(steps):
        upper = (lax.axis_index(axis) & bit) // bit
        other = swap(value, axis, bit)
        value = jnp.where(
            upper == 0,
            jnp.concatenate([value, other], axis=0),
            jnp.concatenate([other, value], axis=0),
        )
    return value


def per_device(
    inputs, doc_lengths, random_blocks, qkv_weight, query_bias, value_bias, proj_weight, proj_bias,
    first_gain, first_shift, expand_weight, expand_bias, shrink_weight, shrink_bias,
    second_gain, second_shift, cotangent,
):
    hx = lax.axis_index("hx")
    hc = lax.axis_index("hc")
    docs, rows, _ = inputs.shape
    assert docs == 1 and lax.axis_size("hx") == 2 and lax.axis_size("hc") == 2
    half = D // 2
    x = inputs.reshape(rows, D)
    row_blocks = rows // BLOCK
    flip = (hx * 2 + hc).astype(jnp.int32) * row_blocks
    plan = block_plan(doc_lengths[0], random_blocks[0], flip, 2 * row_blocks)
    flip = flip.reshape(1)
    x_far = swap(x, "hx")
    x_near = swap(x, "hc")
    x_all = jnp.concatenate([x, x_near, x_far, swap(x_far, "hc")], axis=0)
    x_chip = x_all[: 2 * rows]

    def own_columns(array, start):
        return lax.dynamic_slice_in_dim(array, start + hc * half, half, array.ndim - 1)

    w_q = own_columns(qkv_weight, 0)
    w_k = own_columns(qkv_weight, D)
    w_v = own_columns(qkv_weight, 2 * D)
    w_proj = jnp.concatenate(
        [
            lax.dynamic_slice_in_dim(proj_weight, hc * half, half, 0),
            lax.dynamic_slice_in_dim(proj_weight, (1 - hc) * half, half, 0),
        ],
        axis=0,
    )
    q = (dot_nn(x_chip, w_q) + own_columns(query_bias, 0).astype(f32)).astype(bf16)
    q = q * jnp.asarray(HEAD_DIM ** (-0.5), bf16)
    k = dot_nn(x_all, w_k).astype(bf16)
    v = (dot_nn(x_all, w_v) + own_columns(value_bias, 0).astype(f32)).astype(bf16)
    context_chip, logsum = attend(plan, doc_lengths, flip, q, k, v)
    context = jnp.concatenate([context_chip[:rows], swap(context_chip[rows:], "hc")], axis=1)

    branch = dot_nn(context, w_proj) + proj_bias.astype(f32)
    resid_one = x.astype(f32) + branch
    hidden, first_pull = jax.vjp(
        layer_norm, resid_one, first_gain.astype(f32), first_shift.astype(f32)
    )
    hidden_low = hidden.astype(bf16)
    inner = dot_nn(hidden_low, expand_weight) + expand_bias.astype(f32)
    active, gelu_pull = jax.vjp(partial(jax.nn.gelu, approximate=False), inner)
    active_low = active.astype(bf16)
    resid_two = hidden + dot_nn(active_low, shrink_weight) + shrink_bias.astype(f32)
    output, second_pull = jax.vjp(
        layer_norm, resid_two, second_gain.astype(f32), second_shift.astype(f32)
    )
    back_two, grad_second_gain, grad_second_shift = second_pull(
        cotangent.reshape(rows, D).astype(f32)
    )
    back_ffn = back_two.astype(bf16)
    grad_shrink = dot_tn(active_low, back_ffn).astype(bf16)
    grad_shrink_bias = jnp.sum(back_ffn.astype(f32), axis=0)
    back_inner = gelu_pull(dot_nt(back_ffn, shrink_weight))[0].astype(bf16)
    grad_expand = dot_tn(hidden_low, back_inner).astype(bf16)
    grad_expand_bias = jnp.sum(back_inner.astype(f32), axis=0)
    back_hidden = back_two + dot_nt(back_inner, expand_weight)
    back_one, grad_first_gain, grad_first_shift = first_pull(back_hidden)
    back_branch = back_one.astype(bf16)
    grad_proj = dot_tn(context, back_branch).astype(bf16)
    grad_proj_bias = jnp.sum(back_branch.astype(f32), axis=0)
    back_context = dot_nt(back_branch, w_proj).astype(bf16)
    back_chip = jnp.concatenate([back_context[:, :half], swap(back_context[:, half:], "hc")], axis=0)

    back_q, back_k, back_v = attend_back(
        plan, doc_lengths, flip, q, k, v, back_chip, context_chip, logsum
    )
    steps = exchange_steps()
    all_steps = [("hc", 1)] + steps + [("hx", 1)]
    chip_steps = steps + [("hx", 1)]
    grad_shrink = sum_everywhere(grad_shrink, all_steps).astype(f32)
    grad_expand = sum_everywhere(grad_expand, all_steps).astype(f32)
    swapped = jnp.concatenate([grad_proj[half:], grad_proj[:half]], axis=0)
    grad_proj = jnp.where(hc == 0, grad_proj, swapped)
    grad_proj = sum_everywhere(grad_proj, all_steps).astype(f32)

    far = slice(2 * rows, 4 * rows)
    back_far = dot_nt(back_k[far], w_k) + dot_nt(back_v[far], w_v)
    back_near = (
        dot_nt(back_k[: 2 * rows], w_k)
        + dot_nt(back_v[: 2 * rows], w_v)
        + dot_nt(back_q, w_q)
    )
    far_own = back_far[:rows] + swap(back_far[rows:].astype(bf16), "hc").astype(f32)
    from_far = swap(far_own.astype(bf16), "hx")
    near_own = back_near[:rows] + swap(back_near[rows:].astype(bf16), "hc").astype(f32)
    input_grad = back_one + near_own + from_far.astype(f32)

    grad_joined = jnp.concatenate(
        [dot_tn(x_chip, back_q), dot_tn(x_all, back_k), dot_tn(x_all, back_v)], axis=1
    ).astype(bf16)
    grad_joined = sum_everywhere(grad_joined, chip_steps)
    other = swap(grad_joined, "hc")
    first = jnp.where(hc == 0, grad_joined, other).reshape(D, 3, half)
    second = jnp.where(hc == 0, other, grad_joined).reshape(D, 3, half)
    grad_qkv = jnp.concatenate([first, second], axis=2).reshape(D, 3 * D).astype(f32)

    sum_q = jnp.sum(back_q.astype(f32), axis=0)
    sum_v = jnp.sum(back_v.astype(f32), axis=0)
    empty = jnp.zeros_like(sum_q)
    vectors = [
        jnp.where(hc == 0, jnp.concatenate([sum_q, empty]), jnp.concatenate([empty, sum_q])),
        jnp.where(hc == 0, jnp.concatenate([sum_v, empty]), jnp.concatenate([empty, sum_v])),
        grad_proj_bias, grad_first_gain, grad_first_shift, grad_expand_bias,
        grad_shrink_bias, grad_second_gain, grad_second_shift,
    ]
    sizes = [member.shape[0] for member in vectors]
    summed = lax.psum(jnp.concatenate(vectors), ("dp", "hx", "hc"))
    parts = []
    at = 0
    for size in sizes:
        parts.append(summed[at : at + size])
        at += size
    return (
        output.astype(bf16).reshape(docs, rows, D),
        input_grad.reshape(docs, rows, D),
        grad_qkv, parts[0], parts[1], grad_proj, parts[2], parts[3], parts[4],
        grad_expand, parts[5], grad_shrink, parts[6], parts[7], parts[8],
    )


def solution(mesh):
    dp = mesh.shape["dp"]
    heads = mesh.shape["heads"]
    split = Mesh(mesh.devices.reshape(dp, heads // 2, 2), ("dp", "hx", "hc"))
    rows = P("dp", ("hx", "hc"), None)
    in_specs = (rows, P("dp"), P("dp", None, None)) + (P(),) * 13 + (rows,)
    out_specs = (rows, rows) + (P(),) * 13
    return jax.shard_map(
        per_device, mesh=split, in_specs=in_specs, out_specs=out_specs, check_vma=False
    )
```

time: 2520 us -> 654 us (0.26); the launches traced: 2480 us -> 644 us
  local copies, waits for them, and re-layouts: 1270 us -> 79.5 us
  blocking collectives: 304 us -> 44.2 us
  other arithmetic: 346 us -> 106 us
  matrix products: 302 us -> 147 us
  waiting for transfers between devices: 215 us -> 143 us
  Pallas kernels: 0 us -> 71.5 us
  starting transfers between devices: 23.8 us -> 50 us
    reshape x21 -> x0, local copies, waits for them, and re-layouts: 484 us -> none  [the longest x2 92.2 us: per_device(): padded.reshape(rows_each * lane_width, device_count)]
    unnamed x1 -> x0, blocking collectives: 304 us -> none
    scatter-add x2 -> x0, other arithmetic: 247 us -> none  [the longest x1 123 us: backward_doc(): empty.at[picked].add(back_key_picked.reshape(spread_shape))]
    unnamed x159 -> x144, local copies, waits for them, and re-layouts: 260 us -> 41.1 us
    dot_general x24 -> x20, matrix products: 302 us -> 147 us  [the longest x6 67.5 us: dot_nn(): lax.dot_general(left, right, (((1,), (0,)), ((), ())), preferred_element_...]
    ppermute x0 -> x47, waiting for transfers between devices: none -> 143 us  [swap(): lax.ppermute(value, axis, [(place, place ^ bit) for place in range(size)])]
    slice x36 -> x7, local copies, waits for them, and re-layouts: 127 us -> 8.63 us  [the longest x1 3.33 us: per_device(): back_near[rows:].astype(bf16)]
    all_to_all x4 -> x0, waiting for transfers between devices: 117 us -> none  [the longest x1 50.2 us: per_device(): lax.all_to_all(back_stacked, 'heads', split_axis=1, concat_axis=3, tiled=...]
  transfers between devices with their start and end apart: 6 -> 47, of which waited for: 6 -> 18; matrix products, arithmetic and copies ran while one was open for 3% -> 29% of each run, Pallas kernels for 0% -> 7%
where the time goes in v1:
time: 654 us; the launch traced here: 644 us
  matrix products  147 us (22%)
  waiting for transfers between devices  143 us (22%)
  other arithmetic  106 us (16%)
  local copies, waits for them, and re-layouts  79.5 us (12%)
  Pallas kernels  71.5 us (11%)
  starting transfers between devices  50 us (8%)
  blocking collectives  44.2 us (7%)
    ppermute x47, waiting for transfers between devices, swap(): lax.ppermute(value, axis, [(place, place ^ bit) for place in range(size)])  143 us
    dot_general x6, matrix products, dot_nn(): lax.dot_general(left, right, (((1,), (0,)), ((), ())), preferred_element_...  67.5 us
    ppermute x47, starting transfers between devices, swap(): lax.ppermute(value, axis, [(place, place ^ bit) for place in range(size)])  50 us
    pallas_call x1, Pallas kernels, attend_back(): pl.pallas_call(partial(backward_kernel, unroll=8, items=query_names.shape...  45.6 us
    dot_general x8, matrix products, dot_nt(): lax.dot_general(left, right, (((1,), (1,)), ((), ())), preferred_element_...  45 us
    psum x1, blocking collectives, per_device(): summed = lax.psum(jnp.concatenate(vectors), ('dp', 'hx', 'hc'))  44.2 us
    unnamed x144, local copies, waits for them, and re-layouts  41.1 us
    dot_general x6, matrix products, dot_tn(): lax.dot_general(left, right, (((0,), (0,)), ((), ())), preferred_element_...  34.7 us
  transfers between devices with their start and end apart: 47, of which 18 were waited for; matrix products, arithmetic and copies ran while one was open for 29% of the time, Pallas kernels for 7%

profile of v1, /device:TPU:0, one launch (start us, length us, event | category | flops | bytes accessed | tf_op | source)
XLA Modules:
  0.0 643.6 jit_solution(18238343468275515520)
XLA Ops:
  8.4 32.7 %collective-permute-done.1 = bf16[1024,768]{0,1:T(8,128)(2,1)} collective-permute-done((bf16[1024,768]{0,1:T(8,128)(2,1)}, bf16[1024,768]{0,1:T(8,128)(2,1)}, u32[]{:S(2)}, u32[]{:S(2)}) %collective-permute-start.1) | collective-permute-done | bytes 1572896 | tf_op jit(solution)/shard_map/ppermute | solution.py:282
  56.7 8.6 %convolution_convert_fusion.k_ref = bf16[4096,384]{1,0:T(8,128)(2,1)} fusion(bf16[768,2304]{1,0:T(8,128)(2,1)S(1)} %copy-done, s32[]{:T(128)S(6)} %select_n.367, bf16[1024,768]{0,1:T(8,128)(2,1)} %collective-permute-done.2, bf16[1024,768]{0,1:T(8,128)(2,1)} %collective-permute-done.1, bf16[1024,768]{0,1:T(8,128)(2,1)} %collective-permute-done, ...), kind=kOutput, calls=%fused_computation.23 | convolution fusion | flops 2442657792 | bytes 10027012 | tf_op jit(solution)/shard_map/dot_general | solution.py:23
  65.3 8.4 %add_convert_fusion.1.v_ref = bf16[4096,384]{1,0:T(8,128)(2,1)} fusion(f32[384]{0:T(512)S(1)} %get-tuple-element.154, bf16[768,2304]{1,0:T(8,128)(2,1)S(1)} %copy-done, s32[]{:T(128)S(6)} %select_n.368, bf16[1024,768]{0,1:T(8,128)(2,1)} %collective-permute-done.2, bf16[1024,768]{0,1:T(8,128)(2,1)} %collective-permute-done.1, ...), kind=kOutput, calls=%fused_computation.22 | convolution fusion | flops 2444230656 | bytes 10029060 | tf_op jit(solution)/shard_map/dot_general | solution.py:23
  73.8 26.0 %attend_forward.1 = (bf16[2048,384]{1,0:T(8,128)(2,1)S(1)}, f32[3,32,128]{2,1,0:T(8,128)S(1)}) custom-call(s32[40,8]{1,0:T(8,128)S(1)} %get-tuple-element.139.key_names, s32[40,8]{1,0:T(8,128)S(1)} %get-tuple-element.138.bias_names, s32[1]{0:T(128)} %bitcast.3.global_name, s32[1]{0:T(128)S(6)} %copy.141.lengths, s32[1]{0:T(128)} %bitcast.4.flips, ...), custom_call_target="tpu_custom_call" | custom-call | flops 40000000000 | bytes 10000000 | tf_op jit(solution)/shard_map/attend_forward/pallas_call | solution.py:173
  117.3 35.9 %multiply_convert_fusion = (bf16[1024,3072]{1,0:T(8,128)(2,1)}, f32[1024,3072]{1,0:T(8,128)}, f32[1024,3072]{1,0:T(8,128)}) fusion(f32[3072]{0:T(1024)S(1)} %copy-done.49, bf16[768,3072]{1,0:T(8,128)(2,1)S(1)} %bitcast.70, f32[1024,768]{0,1:T(8,128)S(1)} %get-tuple-element.141, f32[768]{0:T(1024)S(1)} %convert_element_type.299, ...), kind=kOutput, calls=%fused_computation.5 | convolution fusion | flops 5043388416 | bytes 39348224 | tf_op jit(solution)/shard_map/dot_general | solution.py:23
  153.2 7.8 %fusion.68 = (f32[1024]{0:T(1024)S(1)}, f32[1024,768]{0,1:T(8,128)S(1)}) fusion(f32[768]{0:T(1024)S(1)} %copy-done.52, bf16[1024,3072]{1,0:T(8,128)(2,1)} %get-tuple-element.113, bf16[3072,768]{1,0:T(8,128)(2,1)S(1)} %bitcast.68, f32[768]{0:T(1024)S(1)} %convert_element_type.299, f32[768]{0:T(1024)S(1)} %convert_element_type.298, f32[1024]{0:T(1024)S(1)} %fusion.50, ...), kind=kOutput, calls=%fused_computation.216 | convolution fusion | flops 4837342208 | bytes 17323008 | tf_op jit(solution)/shard_map/dot_general | solution.py:23
  167.4 17.5 %convert_reduce_fusion = (f32[3072]{0:T(1024)}, bf16[1024,3072]{1,0:T(8,128)(2,1)}) fusion(f32[1024,3072]{1,0:T(8,128)} %get-tuple-element.114, bf16[1024,768]{0,1:T(8,128)(2,1)S(1)} %get-tuple-element.108, bf16[3072,768]{1,0:T(8,128)(2,1)} %param.29, f32[1024,3072]{1,0:T(8,128)} %get-tuple-element.142, f32[3072]{0:T(1024)} %convert_element_type.301), kind=kOutput, calls=%fused_computation.3 | convolution fusion | flops 4885312512 | bytes 37773312 | tf_op jit(solution)/shard_map/dot_general | solution.py:27
  184.9 12.5 %multiply_reduce_fusion = (f32[768]{0:T(1024)}, f32[1024]{0:T(1024)S(1)}, f32[768]{0:T(1024)}, f32[1024,768]{0,1:T(8,128)S(1)}) fusion(f32[1024,768]{0,1:T(8,128)} %copy-done.12, f32[1024]{0:T(1024)S(1)} %fusion.50, f32[1024]{0:T(1024)S(1)} %broadcast_multiply_fusion.1, f32[768]{0:T(1024)S(1)} %convert_element_type.298, ...), kind=kOutput, calls=%fused_computation.55 | convolution fusion | flops 4845204480 | bytes 22061056 | tf_op jit(solution)/shard_map/dot_general | solution.py:27
  203.1 11.9 %convolution_convert_fusion.1 = bf16[3072,768]{1,0:T(8,128)(2,1)} fusion(bf16[1024,3072]{1,0:T(8,128)(2,1)} %get-tuple-element.113, bf16[1024,768]{0,1:T(8,128)(2,1)S(1)} %get-tuple-element.108), kind=kOutput, calls=%fused_computation.24 | convolution fusion | flops 4834197504 | bytes 12582912 | tf_op jit(solution)/shard_map/dot_general | solution.py:31
  240.4 45.6 %attend_backward.1 = (bf16[2048,384]{1,0:T(8,128)(2,1)}, bf16[4096,384]{1,0:T(8,128)(2,1)}, bf16[4096,384]{1,0:T(8,128)(2,1)}) custom-call(s32[40]{0:T(128)} %concatenate.173.query_names, s32[40,8]{1,0:T(8,128)} %copy-done.3, s32[40,8]{1,0:T(8,128)} %copy-done.2, s32[1]{0:T(128)S(6)} %copy.141.lengths, s32[1]{0:T(128)} %bitcast.4.flips, ...), custom_call_target="tpu_custom_call" | custom-call | flops 60000002048 | bytes 10000000 | tf_op jit(solution)/shard_map/attend_backward/pallas_call | solution.py:252
  306.0 6.0 convolution_convert_fusion.6
  362.8 10.1 %collective-permute-done.10 = bf16[96,1152]{0,1:T(8,128)(2,1)S(1)} collective-permute-done((bf16[96,1152]{0,1:T(8,128)(2,1)S(1)}, bf16[96,1152]{0,1:T(8,128)(2,1)S(1)}, u32[]{:S(2)}, u32[]{:S(2)}) %collective-permute-start.10) | collective-permute-done | bytes 221216 | tf_op jit(solution)/shard_map/ppermute | solution.py:282
  382.9 5.9 collective-permute-done.12
  391.2 6.0 collective-permute-start.24
  433.3 13.4 %collective-permute-done.38 = bf16[768,768]{1,0:T(8,128)(2,1)} collective-permute-done((bf16[768,768]{1,0:T(8,128)(2,1)}, bf16[768,768]{1,0:T(8,128)(2,1)}, u32[]{:S(2)}, u32[]{:S(2)}) %collective-permute-start.38) | collective-permute-done | bytes 1179680 | tf_op jit(solution)/shard_map/ppermute | solution.py:282
  449.8 11.5 %collective-permute-done.39 = bf16[384,768]{1,0:T(8,128)(2,1)S(1)} collective-permute-done((bf16[384,768]{1,0:T(8,128)(2,1)S(1)}, bf16[384,768]{1,0:T(8,128)(2,1)S(1)}, u32[]{:S(2)}, u32[]{:S(2)}) %collective-permute-start.39) | collective-permute-done | bytes 589856 | tf_op jit(solution)/shard_map/ppermute | solution.py:282
  466.5 12.6 %collective-permute-done.40 = bf16[192,768]{1,0:T(8,128)(2,1)S(1)} collective-permute-done((bf16[192,768]{1,0:T(8,128)(2,1)S(1)}, bf16[192,768]{1,0:T(8,128)(2,1)S(1)}, u32[]{:S(2)}, u32[]{:S(2)}) %collective-permute-start.40) | collective-permute-done | bytes 294944 | tf_op jit(solution)/shard_map/ppermute | solution.py:282
  485.6 6.9 %collective-permute-done.33 = bf16[48,3072]{1,0:T(8,128)(2,1)S(1)} collective-permute-done((bf16[48,3072]{1,0:T(8,128)(2,1)S(1)}, bf16[48,3072]{1,0:T(8,128)(2,1)S(1)}, u32[]{:S(2)}, u32[]{:S(2)}) %collective-permute-start.33) | collective-permute-done | bytes 294944 | tf_op jit(solution)/shard_map/ppermute | solution.py:282
  502.2 13.2 %collective-permute-done.43 = bf16[192,768]{1,0:T(8,128)(2,1)S(1)} collective-permute-done((bf16[192,768]{1,0:T(8,128)(2,1)S(1)}, bf16[192,768]{1,0:T(8,128)(2,1)S(1)}, u32[]{:S(2)}, u32[]{:S(2)}) %collective-permute-start.43) | collective-permute-done | bytes 294944 | tf_op jit(solution)/shard_map/ppermute | solution.py:282
  527.0 44.2 %psum.7 = f32[9216]{0:T(1024)} all-reduce(f32[9216]{0:T(1024)} %constant_dynamic-update-slice_fusion), channel_id=1, replica_groups=mesh['dp'=8,'hx'=2,'hc'=2] {'dp','hx','hc'}, use_global_device_ids=true, to_apply=%region_18.19 | all-reduce | flops 9216 | bytes 73728 | tf_op jit(solution)/shard_map/psum | solution.py:425
  597.9 9.2 %collective-permute-done.45 = bf16[768,768]{1,0:T(8,128)(2,1)} collective-permute-done((bf16[768,768]{1,0:T(8,128)(2,1)}, bf16[768,768]{1,0:T(8,128)(2,1)}, u32[]{:S(2)}, u32[]{:S(2)}) %collective-permute-start.45) | collective-permute-done | bytes 1179680 | tf_op jit(solution)/shard_map/ppermute | solution.py:282
  617.0 8.0 %copy.125 = f32[768,2304]{1,0:T(8,128)} copy(f32[768,2304]{0,1:T(8,128)} %bitcast_convert_fusion) | data formatting | bytes 14155776
  625.0 9.5 %fusion.6 = f32[768,3072]{1,0:T(8,128)} fusion(bf16[384,3072]{1,0:T(8,128)(2,1)} %collective-permute-done.36, bf16[384,3072]{1,0:T(8,128)(2,1)} %maximum_select_fusion.2, pred[]{:T(512)S(6)} %eq.75), kind=kLoop, calls=%fused_computation.29 | loop fusion | flops 23592960 | bytes 14155777 | tf_op jit(solution)/shard_map/convert_element_type | solution.py:389
  634.5 8.7 %fusion.7 = f32[3072,768]{1,0:T(8,128)} fusion(bf16[1536,768]{1,0:T(8,128)(2,1)} %collective-permute-done.46, bf16[1536,768]{1,0:T(8,128)(2,1)} %maximum_select_fusion.3, pred[]{:T(512)S(6)} %eq.75), kind=kLoop, calls=%fused_computation.31 | loop fusion | flops 23592960 | bytes 14155777 | tf_op jit(solution)/shard_map/convert_element_type | solution.py:388
  (363 shorter events, 268.8 us)
Async XLA Ops:
  3.4 37.6 %collective-permute-start.1 = (bf16[1024,768]{0,1:T(8,128)(2,1)}, bf16[1024,768]{0,1:T(8,128)(2,1)}, u32[]{:S(2)}, u32[]{:S(2)}) collective-permute-start(bf16[1024,768]{0,1:T(8,128)(2,1)} %bitcast.58), channel_id=1, source_target_pairs={{0,2},{2,0},{1,3},{3,1},{4,6},{6,4},{5,7},{7,5},{8,10},{10,8},{9,1... | collective-permute-start | bytes 4718600 | tf_op jit(solution)/shard_map/ppermute | solution.py:282
  6.3 46.5 %collective-permute-start = (bf16[1024,768]{0,1:T(8,128)(2,1)}, bf16[1024,768]{0,1:T(8,128)(2,1)}, u32[]{:S(2)}, u32[]{:S(2)}) collective-permute-start(bf16[1024,768]{0,1:T(8,128)(2,1)} %bitcast.59), channel_id=1, source_target_pairs={{0,1},{1,0},{2,3},{3,2},{4,5},{5,4},{6,7},{7,6},{8,9},{9,8},{10,11... | collective-permute-start | bytes 4718600 | tf_op jit(solution)/shard_map/ppermute | solution.py:282
  230.3 144.5 %collective-permute-start.27 = (bf16[384,3072]{1,0:T(8,128)(2,1)}, bf16[384,3072]{1,0:T(8,128)(2,1)}, u32[]{:S(2)}, u32[]{:S(2)}) collective-permute-start(bf16[384,3072]{1,0:T(8,128)(2,1)} %constant_dynamic-slice_fusion.9), channel_id=1, source_target_pairs={{0,1},{1,0},{2,3},{3,2},{4,5},{5,4},{6,7},{7,6},{8,9},{9,8},{10,11... | collective-permute-start | bytes 7077896 | tf_op jit(solution)/shard_map/ppermute | solution.py:282
  233.8 178.3 %collective-permute-start.37 = (bf16[1536,768]{1,0:T(8,128)(2,1)}, bf16[1536,768]{1,0:T(8,128)(2,1)}, u32[]{:S(2)}, u32[]{:S(2)}) collective-permute-start(bf16[1536,768]{1,0:T(8,128)(2,1)} %constant_dynamic-slice_fusion.4), channel_id=1, source_target_pairs={{0,1},{1,0},{2,3},{3,2},{4,5},{5,4},{6,7},{7,6},{8,9},{9,8},{10,11... | collective-permute-start | bytes 7077896 | tf_op jit(solution)/shard_map/ppermute | solution.py:282
  236.2 86.8 %collective-permute-start.18 = (bf16[192,768]{1,0:T(8,128)(2,1)}, bf16[192,768]{1,0:T(8,128)(2,1)}, u32[]{:S(2)}, u32[]{:S(2)}) collective-permute-start(bf16[192,768]{1,0:T(8,128)(2,1)} %constant_dynamic-slice_fusion.13), channel_id=1, source_target_pairs={{0,4},{4,0},{8,12},{12,8},{16,20},{20,16},{24,28},{28,24},{1,5},{5... | collective-permute-start | bytes 884744 | tf_op jit(solution)/shard_map/ppermute | solution.py:282
  300.3 198.5 %collective-permute-start.6 = (bf16[1024,768]{0,1:T(8,128)(2,1)}, bf16[1024,768]{0,1:T(8,128)(2,1)}, u32[]{:S(2)}, u32[]{:S(2)}) collective-permute-start(bf16[1024,768]{0,1:T(8,128)(2,1)} %slice.135), channel_id=1, source_target_pairs={{0,1},{1,0},{2,3},{3,2},{4,5},{5,4},{6,7},{7,6},{8,9},{9,8},{10,11... | collective-permute-start | bytes 4718600 | tf_op jit(solution)/shard_map/ppermute | solution.py:282
  315.2 22.1 %collective-permute-start.8 = (bf16[384,1152]{0,1:T(8,128)(2,1)S(1)}, bf16[384,1152]{0,1:T(8,128)(2,1)S(1)}, u32[]{:S(2)}, u32[]{:S(2)}) collective-permute-start(bf16[384,1152]{0,1:T(8,128)(2,1)S(1)} %constant_dynamic-slice_fusion.18), channel_id=1, source_target_pairs={{0,4},{4,0},{8,12},{12,8},{16,20},{20,16},{24,28},{28,24},{1,5},{5... | collective-permute-start | bytes 2654216 | tf_op jit(solution)/shard_map/ppermute | solution.py:282
  361.2 21.6 %collective-permute-start.22 = (bf16[24,768]{1,0:T(8,128)(2,1)S(1)}, bf16[24,768]{1,0:T(8,128)(2,1)S(1)}, u32[]{:S(2)}, u32[]{:S(2)}) collective-permute-start(bf16[24,768]{1,0:T(8,128)(2,1)S(1)} %add_convert_fusion.24), channel_id=1, source_target_pairs={{0,2},{2,0},{1,3},{3,1},{4,6},{6,4},{5,7},{7,5},{8,10},{10,8},{9,1... | collective-permute-start | bytes 110600 | tf_op jit(solution)/shard_map/ppermute | solution.py:282
  380.5 26.8 %collective-permute-start.28 = (bf16[192,3072]{1,0:T(8,128)(2,1)}, bf16[192,3072]{1,0:T(8,128)(2,1)}, u32[]{:S(2)}, u32[]{:S(2)}) collective-permute-start(bf16[192,3072]{1,0:T(8,128)(2,1)} %constant_dynamic-slice_fusion.8), channel_id=1, source_target_pairs={{0,4},{4,0},{8,12},{12,8},{16,20},{20,16},{24,28},{28,24},{1,5},{5... | collective-permute-start | bytes 3538952 | tf_op jit(solution)/shard_map/ppermute | solution.py:282
  391.2 31.6 %collective-permute-start.24 = (bf16[96,768]{1,0:T(8,128)(2,1)}, bf16[96,768]{1,0:T(8,128)(2,1)}, u32[]{:S(2)}, u32[]{:S(2)}) collective-permute-start(bf16[96,768]{1,0:T(8,128)(2,1)} %maximum_select_fusion.18), channel_id=1, source_target_pairs={{0,8},{4,12},{8,0},{12,4},{16,24},{20,28},{24,16},{28,20},{1,9},{5... | collective-permute-start | bytes 442376 | tf_op jit(solution)/shard_map/ppermute | solution.py:282
  417.5 29.2 %collective-permute-start.38 = (bf16[768,768]{1,0:T(8,128)(2,1)}, bf16[768,768]{1,0:T(8,128)(2,1)}, u32[]{:S(2)}, u32[]{:S(2)}) collective-permute-start(bf16[768,768]{1,0:T(8,128)(2,1)} %constant_dynamic-slice_fusion.3), channel_id=1, source_target_pairs={{0,4},{4,0},{8,12},{12,8},{16,20},{20,16},{24,28},{28,24},{1,5},{5... | collective-permute-start | bytes 3538952 | tf_op jit(solution)/shard_map/ppermute | solution.py:282
  422.9 165.9 %collective-permute-start.5 = (bf16[1024,768]{0,1:T(8,128)(2,1)}, bf16[1024,768]{0,1:T(8,128)(2,1)}, u32[]{:S(2)}, u32[]{:S(2)}) collective-permute-start(bf16[1024,768]{0,1:T(8,128)(2,1)} %slice.136), channel_id=1, source_target_pairs={{0,1},{1,0},{2,3},{3,2},{4,5},{5,4},{6,7},{7,6},{8,9},{9,8},{10,11... | collective-permute-start | bytes 4718600 | tf_op jit(solution)/shard_map/ppermute | solution.py:282
  424.8 95.7 %collective-permute-start.25 = (bf16[192,768]{1,0:T(8,128)(2,1)}, bf16[192,768]{1,0:T(8,128)(2,1)}, u32[]{:S(2)}, u32[]{:S(2)}) collective-permute-start(bf16[192,768]{1,0:T(8,128)(2,1)} %maximum_select_fusion.15), channel_id=1, source_target_pairs={{0,4},{4,0},{8,12},{12,8},{16,20},{20,16},{24,28},{28,24},{1,5},{5... | collective-permute-start | bytes 884744 | tf_op jit(solution)/shard_map/ppermute | solution.py:282
  429.9 19.1 %collective-permute-start.30 = (bf16[48,3072]{1,0:T(8,128)(2,1)S(1)}, bf16[48,3072]{1,0:T(8,128)(2,1)S(1)}, u32[]{:S(2)}, u32[]{:S(2)}) collective-permute-start(bf16[48,3072]{1,0:T(8,128)(2,1)S(1)} %constant_dynamic-slice_fusion.6), channel_id=1, source_target_pairs={{0,16},{4,20},{8,24},{12,28},{16,0},{20,4},{24,8},{28,12},{1,17},{... | collective-permute-start | bytes 884744 | tf_op jit(solution)/shard_map/ppermute | solution.py:282
  484.9 38.6 %collective-permute-start.15 = (bf16[384,1152]{0,1:T(8,128)(2,1)S(1)}, bf16[384,1152]{0,1:T(8,128)(2,1)S(1)}, u32[]{:S(2)}, u32[]{:S(2)}) collective-permute-start(bf16[384,1152]{0,1:T(8,128)(2,1)S(1)} %maximum_select_fusion.9), channel_id=1, source_target_pairs={{0,4},{4,0},{8,12},{12,8},{16,20},{20,16},{24,28},{28,24},{1,5},{5... | collective-permute-start | bytes 2654216 | tf_op jit(solution)/shard_map/ppermute | solution.py:282
  498.7 18.8 %collective-permute-start.34 = (bf16[96,3072]{1,0:T(8,128)(2,1)S(1)}, bf16[96,3072]{1,0:T(8,128)(2,1)S(1)}, u32[]{:S(2)}, u32[]{:S(2)}) collective-permute-start(bf16[96,3072]{1,0:T(8,128)(2,1)S(1)} %maximum_select_fusion.12), channel_id=1, source_target_pairs={{0,8},{4,12},{8,0},{12,4},{16,24},{20,28},{24,16},{28,20},{1,9},{5... | collective-permute-start | bytes 1769480 | tf_op jit(solution)/shard_map/ppermute | solution.py:282
  515.3 73.4 %collective-permute-start.7 = (bf16[1024,768]{0,1:T(8,128)(2,1)}, bf16[1024,768]{0,1:T(8,128)(2,1)}, u32[]{:S(2)}, u32[]{:S(2)}) collective-permute-start(bf16[1024,768]{0,1:T(8,128)(2,1)} %fusion.14), channel_id=1, source_target_pairs={{0,2},{2,0},{1,3},{3,1},{4,6},{6,4},{5,7},{7,5},{8,10},{10,8},{9,1... | collective-permute-start | bytes 4718600 | tf_op jit(solution)/shard_map/ppermute | solution.py:282
  517.5 57.5 %collective-permute-start.44 = (bf16[384,768]{1,0:T(8,128)(2,1)}, bf16[384,768]{1,0:T(8,128)(2,1)}, u32[]{:S(2)}, u32[]{:S(2)}) collective-permute-start(bf16[384,768]{1,0:T(8,128)(2,1)} %maximum_select_fusion.13), channel_id=1, source_target_pairs={{0,8},{4,12},{8,0},{12,4},{16,24},{20,28},{24,16},{28,20},{1,9},{5... | collective-permute-start | bytes 1769480 | tf_op jit(solution)/shard_map/ppermute | solution.py:282
  520.5 64.3 %collective-permute-start.35 = (bf16[192,3072]{1,0:T(8,128)(2,1)}, bf16[192,3072]{1,0:T(8,128)(2,1)}, u32[]{:S(2)}, u32[]{:S(2)}) collective-permute-start(bf16[192,3072]{1,0:T(8,128)(2,1)} %maximum_select_fusion.7), channel_id=1, source_target_pairs={{0,4},{4,0},{8,12},{12,8},{16,20},{20,16},{24,28},{28,24},{1,5},{5... | collective-permute-start | bytes 3538952 | tf_op jit(solution)/shard_map/ppermute | solution.py:282
  524.5 53.5 %collective-permute-start.26 = (bf16[384,768]{1,0:T(8,128)(2,1)}, bf16[384,768]{1,0:T(8,128)(2,1)}, u32[]{:S(2)}, u32[]{:S(2)}) collective-permute-start(bf16[384,768]{1,0:T(8,128)(2,1)} %maximum_select_fusion.11), channel_id=1, source_target_pairs={{0,1},{1,0},{2,3},{3,2},{4,5},{5,4},{6,7},{7,6},{8,9},{9,8},{10,11... | collective-permute-start | bytes 1769480 | tf_op jit(solution)/shard_map/ppermute | solution.py:282
  575.0 35.8 %collective-permute-start.16 = (bf16[768,1152]{0,1:T(8,128)(2,1)}, bf16[768,1152]{0,1:T(8,128)(2,1)}, u32[]{:S(2)}, u32[]{:S(2)}) collective-permute-start(bf16[768,1152]{0,1:T(8,128)(2,1)} %maximum_select_fusion.4), channel_id=1, source_target_pairs={{0,1},{1,0},{2,3},{3,2},{4,5},{5,4},{6,7},{7,6},{8,9},{9,8},{10,11... | collective-permute-start | bytes 5308424 | tf_op jit(solution)/shard_map/ppermute | solution.py:282
  577.9 29.2 %collective-permute-start.45 = (bf16[768,768]{1,0:T(8,128)(2,1)}, bf16[768,768]{1,0:T(8,128)(2,1)}, u32[]{:S(2)}, u32[]{:S(2)}) collective-permute-start(bf16[768,768]{1,0:T(8,128)(2,1)} %maximum_select_fusion.8), channel_id=1, source_target_pairs={{0,4},{4,0},{8,12},{12,8},{16,20},{20,16},{24,28},{28,24},{1,5},{5... | collective-permute-start | bytes 3538952 | tf_op jit(solution)/shard_map/ppermute | solution.py:282
  588.6 36.5 %collective-permute-start.36 = (bf16[384,3072]{1,0:T(8,128)(2,1)}, bf16[384,3072]{1,0:T(8,128)(2,1)}, u32[]{:S(2)}, u32[]{:S(2)}) collective-permute-start(bf16[384,3072]{1,0:T(8,128)(2,1)} %maximum_select_fusion.2), channel_id=1, source_target_pairs={{0,1},{1,0},{2,3},{3,2},{4,5},{5,4},{6,7},{7,6},{8,9},{9,8},{10,11... | collective-permute-start | bytes 7077896 | tf_op jit(solution)/shard_map/ppermute | solution.py:282
  610.8 23.7 %collective-permute-start.46 = (bf16[1536,768]{1,0:T(8,128)(2,1)}, bf16[1536,768]{1,0:T(8,128)(2,1)}, u32[]{:S(2)}, u32[]{:S(2)}) collective-permute-start(bf16[1536,768]{1,0:T(8,128)(2,1)} %maximum_select_fusion.3), channel_id=1, source_target_pairs={{0,1},{1,0},{2,3},{3,2},{4,5},{5,4},{6,7},{7,6},{8,9},{9,8},{10,11... | collective-permute-start | bytes 7077896 | tf_op jit(solution)/shard_map/ppermute | solution.py:282
  (89 other events, 1115.3 us)

commit v2 on v1

--- a/solution.py
+++ b/solution.py
@@ -241,24 +241,25 @@
     back_v_ref[...] = v_scratch[...].astype(bf16)
 
 
-def attend_back(plan, length, flip, q, k, v, back, context, logsum):
+def attend_back(plan, length, flip, pair, q, k, v, back, context, logsum):
     query_names, key_names, bias_names, _ = plan
-    query_rows, width = q.shape
+    query_rows = q.shape[0]
     tokens = k.shape[0]
-    pairs = width // 128
     query_blocks = query_rows // BLOCK
-    q_spec = pl.BlockSpec((query_rows, 128), lambda pair, *_: (0, pair))
-    k_spec = pl.BlockSpec((tokens, 128), lambda pair, *_: (0, pair))
+    q_in = pl.BlockSpec((query_rows, 128), lambda step, *_: (0, pair))
+    k_in = pl.BlockSpec((tokens, 128), lambda step, *_: (0, pair))
+    q_out = pl.BlockSpec((query_rows, 128), lambda step, *_: (0, 0))
+    k_out = pl.BlockSpec((tokens, 128), lambda step, *_: (0, 0))
     return pl.pallas_call(
         partial(backward_kernel, unroll=8, items=query_names.shape[0]),
         grid_spec=pltpu.PrefetchScalarGridSpec(
             num_scalar_prefetch=5,
-            grid=(pairs,),
+            grid=(1,),
             in_specs=[
-                q_spec, k_spec, k_spec, q_spec, q_spec,
-                pl.BlockSpec((1, query_blocks, 128), lambda pair, *_: (pair, 0, 0)),
+                q_in, k_in, k_in, q_in, q_in,
+                pl.BlockSpec((1, query_blocks, 128), lambda step, *_: (pair, 0, 0)),
             ],
-            out_specs=[q_spec, k_spec, k_spec],
+            out_specs=[q_out, k_out, k_out],
             scratch_shapes=[
                 pltpu.VMEM((tokens + BLOCK, 128), f32),
                 pltpu.VMEM((query_rows, 128), f32),
@@ -267,14 +268,545 @@
             ],
         ),
         out_shape=[
-            jax.ShapeDtypeStruct(q.shape, bf16),
-            jax.ShapeDtypeStruct(k.shape, bf16),
-            jax.ShapeDtypeStruct(k.shape, bf16),
+            jax.ShapeDtypeStruct((query_rows, 128), bf16),
+            jax.ShapeDtypeStruct((tokens, 128), bf16),
+            jax.ShapeDtypeStruct((tokens, 128), bf16),
         ],
-        compiler_params=pltpu.CompilerParams(vmem_limit_bytes=56 << 20),
-        cost_estimate=pl.CostEstimate(flops=60 * 10**9, bytes_accessed=10**7, transcendentals=10**7),
+        compiler_params=pltpu.CompilerParams(vmem_limit_bytes=40 << 20),
+        cost_estimate=pl.CostEstimate(flops=16 * 10**9, bytes_accessed=10**6, transcendentals=10**6),
         name="attend_backward",
     )(query_names, key_names, bias_names, length, flip, q, k, v, back, context, logsum)
+
+
+def project_kernel(core, x_ref, x_near_ref, w_q, w_k, w_v, b_q, b_v, q_ref, k_ref, v_ref):
+    step = pl.program_id(0)
+
+    def project(tile):
+        q = (dot_nn(tile, w_q[...]) + b_q[...]).astype(bf16)
+        q_ref[...] = q * jnp.asarray(HEAD_DIM ** (-0.5), bf16)
+        k_ref[...] = dot_nn(tile, w_k[...]).astype(bf16)
+        v_ref[...] = (dot_nn(tile, w_v[...]) + b_v[...]).astype(bf16)
+
+    @pl.when(step < pl.num_programs(0) // 2)
+    def _():
+        project(x_ref[...])
+
+    @pl.when(step >= pl.num_programs(0) // 2)
+    def _():
+        project(x_near_ref[...])
+
+
+def project_far_kernel(core, x_ref, x_near_ref, w_k, w_v, b_v, k_old, v_old, k_ref, v_ref):
+    step = pl.program_id(0)
+
+    def project(tile):
+        k_ref[...] = dot_nn(tile, w_k[...]).astype(bf16)
+        v_ref[...] = (dot_nn(tile, w_v[...]) + b_v[...]).astype(bf16)
+
+    @pl.when(step < pl.num_programs(0) // 2)
+    def _():
+        project(x_ref[...])
+
+    @pl.when(step >= pl.num_programs(0) // 2)
+    def _():
+        project(x_near_ref[...])
+
+
+TILE = 512
+
+
+def piece_spec(piece, per, width):
+    return pl.BlockSpec((TILE, width), lambda step, *_: (jnp.clip(step - piece * per, 0, per - 1), 0))
+
+
+def own_weight(which):
+    return pl.BlockSpec((D, D // 2), lambda step, core, *_: (0, 2 * which + core[0]))
+
+
+def own_bias():
+    return pl.BlockSpec((1, D // 2), lambda step, core, *_: (0, core[0]))
+
+
+def project_chip(core, x, x_near, qkv_weight, query_bias, value_bias):
+    rows = x.shape[0]
+    half = D // 2
+    per = rows // TILE
+    out = pl.BlockSpec((TILE, half), lambda step, *_: (step, 0))
+    return pl.pallas_call(
+        project_kernel,
+        grid_spec=pltpu.PrefetchScalarGridSpec(
+            num_scalar_prefetch=1,
+            grid=(2 * per,),
+            in_specs=[piece_spec(0, per, D), piece_spec(1, per, D)]
+            + [own_weight(0), own_weight(1), own_weight(2), own_bias(), own_bias()],
+            out_specs=[out, out, out],
+        ),
+        out_shape=[
+            jax.ShapeDtypeStruct((2 * rows, half), bf16),
+            jax.ShapeDtypeStruct((4 * rows, half), bf16),
+            jax.ShapeDtypeStruct((4 * rows, half), bf16),
+        ],
+        compiler_params=pltpu.CompilerParams(vmem_limit_bytes=32 << 20),
+        cost_estimate=pl.CostEstimate(flops=4 * 10**9, bytes_accessed=10**7, transcendentals=0),
+        name="project_chip",
+    )(core, x, x_near, qkv_weight, qkv_weight, qkv_weight, query_bias, value_bias)
+
+
+def project_far(core, x_far, x_far_near, qkv_weight, value_bias, k, v):
+    rows = x_far.shape[0]
+    half = D // 2
+    per = rows // TILE
+    out = pl.BlockSpec((TILE, half), lambda step, *_: (2 * per + step, 0))
+    kept = pl.BlockSpec(memory_space=pl.ANY)
+    return pl.pallas_call(
+        project_far_kernel,
+        grid_spec=pltpu.PrefetchScalarGridSpec(
+            num_scalar_prefetch=1,
+            grid=(2 * per,),
+            in_specs=[piece_spec(0, per, D), piece_spec(1, per, D)]
+            + [own_weight(1), own_weight(2), own_bias(), kept, kept],
+            out_specs=[out, out],
+        ),
+        out_shape=[jax.ShapeDtypeStruct(k.shape, bf16), jax.ShapeDtypeStruct(v.shape, bf16)],
+        input_output_aliases={6: 0, 7: 1},
+        compiler_params=pltpu.CompilerParams(vmem_limit_bytes=32 << 20),
+        cost_estimate=pl.CostEstimate(flops=3 * 10**9, bytes_accessed=10**7, transcendentals=0),
+        name="project_far",
+    )(core, x_far, x_far_near, qkv_weight, qkv_weight, value_bias, k, v)
+
+
+def gelu_pair(x):
+    t = 1.0 / (1.0 + (0.3275911 * 0.5**0.5) * jnp.abs(x))
+    bell = jnp.exp(-0.5 * x * x)
+    poly = 0.7107068705 + t * (-0.7265760135 + t * 0.5307027145)
+    tail = t * (0.127414796 + t * (-0.142248368 + t * poly)) * bell
+    cdf = jnp.where(x < 0, tail, 1.0 - tail)
+    return x * cdf, cdf + x * bell * 0.3989422804014327
+
+
+def norm_parts(value):
+    center = value - jnp.mean(value, axis=-1, keepdims=True)
+    spread = jnp.mean(center * center, axis=-1, keepdims=True)
+    scale = lax.rsqrt(spread + norm_epsilon)
+    return center * scale, scale
+
+
+def norm_back(slope, normed, scale):
+    along = jnp.mean(slope * normed, axis=-1, keepdims=True)
+    return scale * (slope - jnp.mean(slope, axis=-1, keepdims=True) - normed * along)
+
+
+def column_sum(value):
+    return jnp.sum(value, axis=0, keepdims=True)
+
+
+PIECES = 32
+STAGES = 8
+VECTOR_ROWS = 256
+
+
+def middle_kernel(
+    places, core,
+    own_ref, other_ref, x_ref, cot_ref, vector_ref, expand_bias_ref, proj_hbm, expand_hbm, shrink_hbm,
+    output_ref, back_one_ref, back_own_ref, back_other_ref, keep_ref, send_ref,
+    proj_w, expand_w, shrink_w, active_s, slope_s, shrink_g, expand_g, proj_g, vector_g, bias_g, stage,
+    weight_sems, sems, *, chunk,
+):
+    step = pl.program_id(0)
+    half = D // 2
+    ff = expand_w.shape[1]
+    chunks = ff // chunk
+    hc = core[0]
+    loads = [
+        pltpu.make_async_copy(proj_hbm.at[pl.ds(hc * half, half)], proj_w.at[pl.ds(0, half)], weight_sems.at[0]),
+        pltpu.make_async_copy(
+            proj_hbm.at[pl.ds((1 - hc) * half, half)], proj_w.at[pl.ds(half, half)], weight_sems.at[1]
+        ),
+        pltpu.make_async_copy(expand_hbm, expand_w, weight_sems.at[2]),
+        pltpu.make_async_copy(shrink_hbm, shrink_w, weight_sems.at[3]),
+    ]
+
+    @pl.when(step == 0)
+    def _():
+        for load in loads:
+            load.start()
+        for total in (shrink_g, expand_g, proj_g, vector_g, bias_g):
+            total[...] = jnp.zeros_like(total)
+        loads[0].wait()
+        loads[1].wait()
+
+    def vector(row):
+        return vector_ref[pl.ds(row, 1), :]
+
+    context = jnp.concatenate([own_ref[...], other_ref[...]], axis=1)
+    resid = x_ref[...].astype(f32) + dot_nn(context, proj_w[...]) + vector(0)
+    normed_one, scale_one = norm_parts(resid)
+    hidden = normed_one * vector(1) + vector(2)
+    low = hidden.astype(bf16)
+    resid_two = hidden + vector(3)
+
+    @pl.when(step == 0)
+    def _():
+        loads[2].wait()
+        loads[3].wait()
+
+    for part in range(chunks):
+        cols = slice(part * chunk, (part + 1) * chunk)
+        inner = dot_nn(low, expand_w[:, cols]) + expand_bias_ref[:, cols]
+        active, slope = gelu_pair(inner)
+        active = active.astype(bf16)
+        active_s[:, cols] = active
+        slope_s[:, cols] = slope.astype(bf16)
+        resid_two = resid_two + dot_nn(active, shrink_w[cols, :])
+    normed_two, scale_two = norm_parts(resid_two)
+    output_ref[...] = (normed_two * vector(4) + vector(5)).astype(bf16)
+    cot = cot_ref[...].astype(f32)
+    back_two = norm_back(vector(4) * cot, normed_two, scale_two)
+    low_two = back_two.astype(bf16)
+    vector_g[3:4, :] += column_sum(low_two.astype(f32))
+    vector_g[4:5, :] += column_sum(cot * normed_two)
+    vector_g[5:6, :] += column_sum(cot)
+    back = back_two
+    for part in range(chunks):
+        cols = slice(part * chunk, (part + 1) * chunk)
+        back_inner = (dot_nt(low_two, shrink_w[cols, :]) * slope_s[:, cols].astype(f32)).astype(bf16)
+        bias_g[:, cols] += column_sum(back_inner.astype(f32))
+        back = back + dot_nt(back_inner, expand_w[:, cols])
+        shrink_g[cols, :] += dot_tn(active_s[:, cols], low_two)
+        expand_g[:, cols] += dot_tn(low, back_inner)
+    vector_g[1:2, :] += column_sum(back * normed_one)
+    vector_g[2:3, :] += column_sum(back)
+    back_one = norm_back(vector(1) * back, normed_one, scale_one)
+    back_one_ref[...] = back_one
+    low_one = back_one.astype(bf16)
+    vector_g[0:1, :] += column_sum(low_one.astype(f32))
+    proj_g[:D, :] += dot_tn(context, low_one)
+    back_context = dot_nt(low_one, proj_w[...]).astype(bf16)
+    back_own_ref[...] = back_context[:, :half]
+    back_other_ref[...] = back_context[:, half:]
+
+    @pl.when(step == pl.num_programs(0) - 1)
+    def _():
+        proj_g[D:, :] = jnp.zeros((proj_g.shape[0] - D, D), f32)
+        proj_g[D : D + 8, :] = vector_g[...]
+        for part in range(ff // D):
+            proj_g[D + 8 + part : D + 9 + part, :] = bias_g[:, part * D : (part + 1) * D]
+        kept = PIECES // 2
+        rows = ff // PIECES
+        extra = proj_g.shape[0] // (2 * PIECES)
+        wide = ff // D
+        half_chunks = half // extra
+
+        def wait(color, slot):
+            pltpu.make_async_copy(stage.at[color, slot], keep_ref.at[0], sems.at[color, slot]).wait()
+
+        def put(piece, carry):
+            slot = lax.rem(piece, STAGES)
+
+            @pl.when(piece >= STAGES)
+            def _():
+                wait(0, slot)
+                wait(1, slot)
+
+            first = piece ^ places[0]
+            second = piece ^ places[1]
+
+            def extra_rows(place):
+                turned = lax.rem(place + half_chunks * hc, 2 * half_chunks)
+                place = jnp.where(place < 2 * half_chunks, turned, place)
+                return proj_g[pl.ds(pl.multiple_of(place * extra, extra), extra), :].astype(bf16)
+
+            stage[0, slot, :rows, :] = shrink_g[pl.ds(pl.multiple_of(first * rows, rows), rows), :].astype(bf16)
+            stage[0, slot, rows:, :] = extra_rows(first)
+            down = pl.ds(pl.multiple_of((second // wide) * rows, rows), rows)
+            across = pl.ds(pl.multiple_of((second % wide) * D, D), D)
+            stage[1, slot, :rows, :] = expand_g[down, across].astype(bf16)
+            stage[1, slot, rows:, :] = extra_rows(PIECES + second)
+            place = lax.rem(piece, kept)
+            for color in range(2):
+                source = stage.at[color, slot]
+
+                @pl.when(piece < kept)
+                def _():
+                    pltpu.make_async_copy(source, keep_ref.at[color * kept + place], sems.at[color, slot]).start()
+
+                @pl.when(piece >= kept)
+                def _():
+                    pltpu.make_async_copy(source, send_ref.at[color * kept + place], sems.at[color, slot]).start()
+
+            return carry
+
+        lax.fori_loop(0, PIECES, put, 0)
+        for slot in range(STAGES):
+            wait(0, slot)
+            wait(1, slot)
+
+
+def middle(places, core, own, other, x, cot, vectors, expand_bias, proj_weight, expand_weight, shrink_weight):
+    rows = x.shape[0]
+    ff = expand_weight.shape[1]
+    half = D // 2
+    tile = 256
+    piece_rows = ff // PIECES + (D + VECTOR_ROWS) // (2 * PIECES)
+
+    def row(width):
+        return pl.BlockSpec((tile, width), lambda step, *_: (step, 0))
+
+    def whole(array):
+        return pl.BlockSpec(array.shape, lambda step, *_: (0, 0))
+
+    kept = pl.BlockSpec(memory_space=pl.ANY)
+    packed = jax.ShapeDtypeStruct((PIECES, piece_rows, D), bf16)
+    return pl.pallas_call(
+        partial(middle_kernel, chunk=D),
+        grid_spec=pltpu.PrefetchScalarGridSpec(
+            num_scalar_prefetch=2,
+            grid=(rows // tile,),
+            in_specs=[row(half), row(half), row(D), row(D), whole(vectors), whole(expand_bias), kept, kept, kept],
+            out_specs=[row(D), row(D), row(half), row(half), kept, kept],
+            scratch_shapes=[
+                pltpu.VMEM((D, D), bf16),
+                pltpu.VMEM((D, ff), bf16),
+                pltpu.VMEM((ff, D), bf16),
+                pltpu.VMEM((tile, ff), bf16),
+                pltpu.VMEM((tile, ff), bf16),
+                pltpu.VMEM((ff, D), f32),
+                pltpu.VMEM((D, ff), f32),
+                pltpu.VMEM((D + VECTOR_ROWS, D), f32),
+                pltpu.VMEM((8, D), f32),
+                pltpu.VMEM((1, ff), f32),
+                pltpu.VMEM((2, STAGES, piece_rows, D), bf16),
+                pltpu.SemaphoreType.DMA((4,)),
+                pltpu.SemaphoreType.DMA((2, STAGES)),
+            ],
+        ),
+        out_shape=[
+            jax.ShapeDtypeStruct((rows, D), bf16),
+            jax.ShapeDtypeStruct((rows, D), f32),
+            jax.ShapeDtypeStruct((rows, half), bf16),
+            jax.ShapeDtypeStruct((rows, half), bf16),
+            packed,
+            packed,
+        ],
+        compiler_params=pltpu.CompilerParams(vmem_limit_bytes=60 << 20),
+        cost_estimate=pl.CostEstimate(flops=60 * 10**9, bytes_accessed=10**7, transcendentals=10**7),
+        name="middle",
+    )(places, core, own, other, x, cot, vectors, expand_bias, proj_weight, expand_weight, shrink_weight)
+
+
+def input_far_kernel(core, *refs):
+    w_k, w_v, out = refs[0], refs[1], refs[-1]
+    arrays = refs[2:-1]
+    pairs = len(arrays) // 2
+    back_k = jnp.concatenate([ref[...] for ref in arrays[:pairs]], axis=1)
+    back_v = jnp.concatenate([ref[...] for ref in arrays[pairs:]], axis=1)
+    out[...] = (dot_nt(back_k, w_k[...]) + dot_nt(back_v, w_v[...])).astype(bf16)
+
+
+def input_far(core, qkv_weight, back_ks, back_vs, rows):
+    first = 2 * rows // TILE
+    token = pl.BlockSpec((TILE, 128), lambda step, *_: (first + step, 0))
+    arrays = list(back_ks) + list(back_vs)
+    return pl.pallas_call(
+        input_far_kernel,
+        grid_spec=pltpu.PrefetchScalarGridSpec(
+            num_scalar_prefetch=1,
+            grid=(2 * rows // TILE,),
+            in_specs=[own_weight(1), own_weight(2)] + [token] * len(arrays),
+            out_specs=pl.BlockSpec((TILE, D), lambda step, *_: (step, 0)),
+        ),
+        out_shape=jax.ShapeDtypeStruct((2 * rows, D), bf16),
+        compiler_params=pltpu.CompilerParams(vmem_limit_bytes=32 << 20),
+        cost_estimate=pl.CostEstimate(flops=3 * 10**9, bytes_accessed=10**7, transcendentals=0),
+        name="input_far",
+    )(core, qkv_weight, qkv_weight, *arrays)
+
+
+QKV_PIECES = 16
+
+
+def joined_kernel(places, core, *refs, tiles, pairs):
+    w_q, w_k, w_v = refs[:3]
+    x_refs = refs[3:7]
+    arrays = refs[7 : 7 + 3 * pairs]
+    near_ref, first_ref, second_ref = refs[7 + 3 * pairs : 10 + 3 * pairs]
+    q_g, k_g, v_g, b_g = refs[10 + 3 * pairs :]
+    step = pl.program_id(0)
+    half = D // 2
+    per = tiles // 4
+
+    @pl.when(step == 0)
+    def _():
+        for total in (q_g, k_g, v_g, b_g):
+            total[...] = jnp.zeros_like(total)
+
+    def joined(which):
+        return jnp.concatenate([ref[...] for ref in arrays[which * pairs : (which + 1) * pairs]], axis=1)
+
+    ones = jnp.ones((TILE, 128), bf16)
+    for piece in range(4):
+
+        @pl.when((step >= piece * per) & (step < (piece + 1) * per))
+        def _():
+            x = x_refs[piece][...]
+            back_k = joined(1)
+            back_v = joined(2)
+            k_g[...] += dot_tn(x, back_k)
+            v_g[...] += dot_tn(x, back_v)
+            b_g[half:, :] += dot_tn(back_v, ones)
+            if piece < 2:
+                back_q = joined(0)
+                q_g[...] += dot_tn(x, back_q)
+                b_g[:half, :] += dot_tn(back_q, ones)
+                near_ref[...] = (
+                    dot_nt(back_q, w_q[...]) + dot_nt(back_k, w_k[...]) + dot_nt(back_v, w_v[...])
+                ).astype(bf16)
+
+    @pl.when(step == tiles - 1)
+    def _():
+        rows = D // QKV_PIECES
+        for piece in range(QKV_PIECES):
+            part = pl.ds(pl.multiple_of((piece ^ places[0]) * rows, rows), rows)
+            first_ref[piece, :, :half] = q_g[part, :].astype(bf16)
+            first_ref[piece, :, half:] = k_g[part, :256].astype(bf16)
+            part = pl.ds(pl.multiple_of((piece ^ places[1]) * rows, rows), rows)
+            second_ref[piece, :, :128] = k_g[part, 256:].astype(bf16)
+            second_ref[piece, :, 128 : 128 + half] = v_g[part, :].astype(bf16)
+            second_ref[piece, :, 128 + half :] = b_g[part, :].astype(bf16)
+
+
+def joined_grads(places, core, qkv_weight, xs, back_qs, back_ks, back_vs):
+    rows = xs[0].shape[0]
+    pairs = len(back_qs)
+    per = rows // TILE
+    tiles = 4 * per
+    half = D // 2
+    width = half + 256
+    token = pl.BlockSpec((TILE, 128), lambda step, *_: (step, 0))
+    query = pl.BlockSpec((TILE, 128), lambda step, *_: (jnp.minimum(step, 2 * per - 1), 0))
+    weights = [
+        pl.BlockSpec((D, half), lambda step, places, core, which=which: (0, 2 * which + core[0]))
+        for which in range(3)
+    ]
+    packed = pl.BlockSpec((QKV_PIECES, D // QKV_PIECES, width), lambda step, *_: (0, 0, 0))
+    packed_shape = jax.ShapeDtypeStruct((QKV_PIECES, D // QKV_PIECES, width), bf16)
+    return pl.pallas_call(
+        partial(joined_kernel, tiles=tiles, pairs=pairs),
+        grid_spec=pltpu.PrefetchScalarGridSpec(
+            num_scalar_prefetch=2,
+            grid=(tiles,),
+            in_specs=weights
+            + [piece_spec(piece, per, D) for piece in range(4)]
+            + [query] * pairs
+            + [token] * (2 * pairs),
+            out_specs=[
+                pl.BlockSpec((TILE, D), lambda step, *_: (jnp.minimum(step, 2 * per - 1), 0)),
+                packed,
+                packed,
+            ],
+            scratch_shapes=[pltpu.VMEM((D, half), f32)] * 3 + [pltpu.VMEM((D, 128), f32)],
+        ),
+        out_shape=[jax.ShapeDtypeStruct((2 * rows, D), bf16), packed_shape, packed_shape],
+        compiler_params=pltpu.CompilerParams(vmem_limit_bytes=48 << 20),
+        cost_estimate=pl.CostEstimate(flops=10 * 10**9, bytes_accessed=10**7, transcendentals=0),
+        name="joined_grads",
+    )(places, core, qkv_weight, qkv_weight, qkv_weight, *xs, *back_qs, *back_ks, *back_vs)
+
+
+def unpack_kernel(places, first_own, first_other, second_own, second_other, shrink_ref, expand_ref, low_ref, high_ref, *, rows):
+    step = pl.program_id(0)
+    kept = PIECES // 2
+
+    def put(first, second):
+        shrink_ref[...] = first[0, :rows, :].astype(f32)
+        expand_ref[...] = second[0, :rows, :].astype(f32)
+        low_ref[...] = first[0, rows:, :].astype(f32)
+        high_ref[...] = second[0, rows:, :].astype(f32)
+
+    @pl.when(step < kept)
+    def _():
+        put(first_own, second_own)
+
+    @pl.when(step >= kept)
+    def _():
+        put(first_other, second_other)
+
+
+def unpack(places, first_own, first_other, second_own, second_other, ff):
+    kept, piece_rows, _ = first_own.shape
+    rows = ff // PIECES
+    extra = piece_rows - rows
+    wide = ff // D
+    own = pl.BlockSpec((1, piece_rows, D), lambda step, *_: (jnp.minimum(step, kept - 1), 0, 0))
+    other = pl.BlockSpec((1, piece_rows, D), lambda step, *_: (jnp.maximum(step - kept, 0), 0, 0))
+    return pl.pallas_call(
+        partial(unpack_kernel, rows=rows),
+        grid_spec=pltpu.PrefetchScalarGridSpec(
+            num_scalar_prefetch=1,
+            grid=(PIECES,),
+            in_specs=[own, other, own, other],
+            out_specs=[
+                pl.BlockSpec((rows, D), lambda step, places: (step ^ places[0], 0)),
+                pl.BlockSpec((rows, D), lambda step, places: ((step ^ places[1]) // wide, (step ^ places[1]) % wide)),
+                pl.BlockSpec((extra, D), lambda step, places: (step ^ places[0], 0)),
+                pl.BlockSpec((extra, D), lambda step, places: (step ^ places[1], 0)),
+            ],
+        ),
+        out_shape=[
+            jax.ShapeDtypeStruct((ff, D), f32),
+            jax.ShapeDtypeStruct((D, ff), f32),
+            jax.ShapeDtypeStruct((extra * PIECES, D), f32),
+            jax.ShapeDtypeStruct((extra * PIECES, D), f32),
+        ],
+        compiler_params=pltpu.CompilerParams(vmem_limit_bytes=32 << 20),
+        cost_estimate=pl.CostEstimate(flops=10**6, bytes_accessed=42 * 10**6, transcendentals=0),
+        name="unpack",
+    )(places, first_own, first_other, second_own, second_other)
+
+
+def unpack_joined_kernel(places, core, first_own, second_own, first_other, second_other, out_ref, bias_ref):
+    half = D // 2
+
+    def put(first, second, place):
+        def at(which):
+            return slice(which * D + place * half, which * D + (place + 1) * half)
+
+        out_ref[:, at(0)] = first[0, :, :half].astype(f32)
+        out_ref[:, at(1)] = jnp.concatenate([first[0, :, half:], second[0, :, :128]], axis=1).astype(f32)
+        out_ref[:, at(2)] = second[0, :, 128 : 128 + half].astype(f32)
+        bias_ref[:, place * 128 : (place + 1) * 128] = second[0, :, 128 + half :].astype(f32)
+
+    @pl.when(core[0] == 0)
+    def _():
+        put(first_own, second_own, 0)
+        put(first_other, second_other, 1)
+
+    @pl.when(core[0] != 0)
+    def _():
+        put(first_own, second_own, 1)
+        put(first_other, second_other, 0)
+
+
+def unpack_joined(places, core, first_own, second_own, first_other, second_other):
+    count, rows, width = first_own.shape
+    first = pl.BlockSpec((1, rows, width), lambda step, places, core: (step ^ places[0], 0, 0))
+    second = pl.BlockSpec((1, rows, width), lambda step, places, core: (step ^ places[1], 0, 0))
+    return pl.pallas_call(
+        unpack_joined_kernel,
+        grid_spec=pltpu.PrefetchScalarGridSpec(
+            num_scalar_prefetch=2,
+            grid=(count,),
+            in_specs=[first, second, first, second],
+            out_specs=[
+                pl.BlockSpec((rows, 3 * D), lambda step, *_: (step, 0)),
+                pl.BlockSpec((rows, 256), lambda step, *_: (step, 0)),
+            ],
+        ),
+        out_shape=[jax.ShapeDtypeStruct((D, 3 * D), f32), jax.ShapeDtypeStruct((D, 256), f32)],
+        compiler_params=pltpu.CompilerParams(vmem_limit_bytes=32 << 20),
+        cost_estimate=pl.CostEstimate(flops=10**6, bytes_accessed=10**7, transcendentals=0),
+        name="unpack_joined",
+    )(places, core, first_own, second_own, first_other, second_other)
 
 
 def swap(value, axis, bit=1):
@@ -282,31 +814,37 @@
     return lax.ppermute(value, axis, [(place, place ^ bit) for place in range(size)])
 
 
-def exchange_steps():
-    steps = []
-    bit = 1
+def place_of(order):
+    number = jnp.zeros((), jnp.int32)
+    for axis, bit in order:
+        number = 2 * number + ((lax.axis_index(axis) & bit) // bit).astype(jnp.int32)
+    return number
+
+
+def add_low(left, right):
+    return (left.astype(f32) + right.astype(f32)).astype(bf16)
+
+
+def scatter_sum(keep, arrived, order):
+    for axis, bit in order:
+        half = keep.shape[0] // 2
+        if arrived is None:
+            send, keep = keep[half:], keep[:half]
+        else:
+            send, keep = add_low(keep[half:], arrived[half:]), add_low(keep[:half], arrived[:half])
+        arrived = swap(send, axis, bit)
+    total = add_low(keep, arrived)
+    bit = 8
     while bit < lax.axis_size("dp"):
-        steps.append(("dp", bit))
+        total = add_low(total, swap(total, "dp", bit))
         bit *= 2
-    return steps
-
-
-def sum_everywhere(value, steps):
-    for axis, bit in steps:
-        half = value.shape[0] // 2
-        upper = (lax.axis_index(axis) & bit) // bit
-        keep = lax.dynamic_slice_in_dim(value, upper * half, half, 0)
-        send = lax.dynamic_slice_in_dim(value, (1 - upper) * half, half, 0)
-        value = (keep.astype(f32) + swap(send, axis, bit).astype(f32)).astype(bf16)
-    for axis, bit in reversed(steps):
-        upper = (lax.axis_index(axis) & bit) // bit
-        other = swap(value, axis, bit)
-        value = jnp.where(
-            upper == 0,
-            jnp.concatenate([value, other], axis=0),
-            jnp.concatenate([other, value], axis=0),
-        )
-    return value
+    return total
+
+
+def gather_sum(piece, order):
+    for axis, bit in reversed(order):
+        piece = jnp.concatenate([piece, swap(piece, axis, bit)], axis=0)
+    return piece
 
 
 def per_device(
@@ -319,120 +857,76 @@
     docs, rows, _ = inputs.shape
     assert docs == 1 and lax.axis_size("hx") == 2 and lax.axis_size("hc") == 2
     half = D // 2
+    ff = expand_weight.shape[1]
+    pairs = half // 128
     x = inputs.reshape(rows, D)
+    x_far = swap(x, "hx")
+    x_near = swap(x, "hc")
     row_blocks = rows // BLOCK
     flip = (hx * 2 + hc).astype(jnp.int32) * row_blocks
     plan = block_plan(doc_lengths[0], random_blocks[0], flip, 2 * row_blocks)
     flip = flip.reshape(1)
-    x_far = swap(x, "hx")
-    x_near = swap(x, "hc")
-    x_all = jnp.concatenate([x, x_near, x_far, swap(x_far, "hc")], axis=0)
-    x_chip = x_all[: 2 * rows]
-
-    def own_columns(array, start):
-        return lax.dynamic_slice_in_dim(array, start + hc * half, half, array.ndim - 1)
-
-    w_q = own_columns(qkv_weight, 0)
-    w_k = own_columns(qkv_weight, D)
-    w_v = own_columns(qkv_weight, 2 * D)
-    w_proj = jnp.concatenate(
-        [
-            lax.dynamic_slice_in_dim(proj_weight, hc * half, half, 0),
-            lax.dynamic_slice_in_dim(proj_weight, (1 - hc) * half, half, 0),
-        ],
-        axis=0,
-    )
-    q = (dot_nn(x_chip, w_q) + own_columns(query_bias, 0).astype(f32)).astype(bf16)
-    q = q * jnp.asarray(HEAD_DIM ** (-0.5), bf16)
-    k = dot_nn(x_all, w_k).astype(bf16)
-    v = (dot_nn(x_all, w_v) + own_columns(value_bias, 0).astype(f32)).astype(bf16)
-    context_chip, logsum = attend(plan, doc_lengths, flip, q, k, v)
-    context = jnp.concatenate([context_chip[:rows], swap(context_chip[rows:], "hc")], axis=1)
-
-    branch = dot_nn(context, w_proj) + proj_bias.astype(f32)
-    resid_one = x.astype(f32) + branch
-    hidden, first_pull = jax.vjp(
-        layer_norm, resid_one, first_gain.astype(f32), first_shift.astype(f32)
-    )
-    hidden_low = hidden.astype(bf16)
-    inner = dot_nn(hidden_low, expand_weight) + expand_bias.astype(f32)
-    active, gelu_pull = jax.vjp(partial(jax.nn.gelu, approximate=False), inner)
-    active_low = active.astype(bf16)
-    resid_two = hidden + dot_nn(active_low, shrink_weight) + shrink_bias.astype(f32)
-    output, second_pull = jax.vjp(
-        layer_norm, resid_two, second_gain.astype(f32), second_shift.astype(f32)
-    )
-    back_two, grad_second_gain, grad_second_shift = second_pull(
-        cotangent.reshape(rows, D).astype(f32)
-    )
-    back_ffn = back_two.astype(bf16)
-    grad_shrink = dot_tn(active_low, back_ffn).astype(bf16)
-    grad_shrink_bias = jnp.sum(back_ffn.astype(f32), axis=0)
-    back_inner = gelu_pull(dot_nt(back_ffn, shrink_weight))[0].astype(bf16)
-    grad_expand = dot_tn(hidden_low, back_inner).astype(bf16)
-    grad_expand_bias = jnp.sum(back_inner.astype(f32), axis=0)
-    back_hidden = back_two + dot_nt(back_inner, expand_weight)
-    back_one, grad_first_gain, grad_first_shift = first_pull(back_hidden)
-    back_branch = back_one.astype(bf16)
-    grad_proj = dot_tn(context, back_branch).astype(bf16)
-    grad_proj_bias = jnp.sum(back_branch.astype(f32), axis=0)
-    back_context = dot_nt(back_branch, w_proj).astype(bf16)
-    back_chip = jnp.concatenate([back_context[:, :half], swap(back_context[:, half:], "hc")], axis=0)
-
-    back_q, back_k, back_v = attend_back(
-        plan, doc_lengths, flip, q, k, v, back_chip, context_chip, logsum
-    )
-    steps = exchange_steps()
-    all_steps = [("hc", 1)] + steps + [("hx", 1)]
-    chip_steps = steps + [("hx", 1)]
-    grad_shrink = sum_everywhere(grad_shrink, all_steps).astype(f32)
-    grad_expand = sum_everywhere(grad_expand, all_steps).astype(f32)
-    swapped = jnp.concatenate([grad_proj[half:], grad_proj[:half]], axis=0)
-    grad_proj = jnp.where(hc == 0, grad_proj, swapped)
-    grad_proj = sum_everywhere(grad_proj, all_steps).astype(f32)
-
-    far = slice(2 * rows, 4 * rows)
-    back_far = dot_nt(back_k[far], w_k) + dot_nt(back_v[far], w_v)
-    back_near = (
-        dot_nt(back_k[: 2 * rows], w_k)
-        + dot_nt(back_v[: 2 * rows], w_v)
-        + dot_nt(back_q, w_q)
-    )
-    far_own = back_far[:rows] + swap(back_far[rows:].astype(bf16), "hc").astype(f32)
-    from_far = swap(far_own.astype(bf16), "hx")
-    near_own = back_near[:rows] + swap(back_near[rows:].astype(bf16), "hc").astype(f32)
-    input_grad = back_one + near_own + from_far.astype(f32)
-
-    grad_joined = jnp.concatenate(
-        [dot_tn(x_chip, back_q), dot_tn(x_all, back_k), dot_tn(x_all, back_v)], axis=1
-    ).astype(bf16)
-    grad_joined = sum_everywhere(grad_joined, chip_steps)
-    other = swap(grad_joined, "hc")
-    first = jnp.where(hc == 0, grad_joined, other).reshape(D, 3, half)
-    second = jnp.where(hc == 0, other, grad_joined).reshape(D, 3, half)
-    grad_qkv = jnp.concatenate([first, second], axis=2).reshape(D, 3 * D).astype(f32)
-
-    sum_q = jnp.sum(back_q.astype(f32), axis=0)
-    sum_v = jnp.sum(back_v.astype(f32), axis=0)
-    empty = jnp.zeros_like(sum_q)
-    vectors = [
-        jnp.where(hc == 0, jnp.concatenate([sum_q, empty]), jnp.concatenate([empty, sum_q])),
-        jnp.where(hc == 0, jnp.concatenate([sum_v, empty]), jnp.concatenate([empty, sum_v])),
-        grad_proj_bias, grad_first_gain, grad_first_shift, grad_expand_bias,
-        grad_shrink_bias, grad_second_gain, grad_second_shift,
-    ]
-    sizes = [member.shape[0] for member in vectors]
-    summed = lax.psum(jnp.concatenate(vectors), ("dp", "hx", "hc"))
-    parts = []
-    at = 0
-    for size in sizes:
-        parts.append(summed[at : at + size])
-        at += size
+    core = hc.astype(jnp.int32).reshape(1)
+    first_order = [("dp", 1), ("dp", 2), ("dp", 4), ("hx", 1)]
+    second_order = [("hx", 1), ("dp", 1), ("dp", 2), ("dp", 4)]
+    core_order = [("hc", 1)]
+    places = jnp.stack([place_of(core_order + first_order), place_of(core_order + second_order)])
+    chip_places = jnp.stack([place_of(first_order), place_of(second_order)])
+
+    bias_q = query_bias.astype(f32).reshape(1, D)
+    bias_v = value_bias.astype(f32).reshape(1, D)
+    q, k, v = project_chip(core, x, x_near, qkv_weight, bias_q, bias_v)
+    x_far_near = swap(x_far, "hc")
+    k, v = project_far(core, x_far, x_far_near, qkv_weight, bias_v, k, v)
+    context, logsum = attend(plan, doc_lengths, flip, q, k, v)
+    other_context = swap(context[rows:], "hc")
+    empty = jnp.zeros((D,), bf16)
+    vectors = jnp.stack(
+        [proj_bias, first_gain, first_shift, shrink_bias, second_gain, second_shift, empty, empty]
+    ).astype(f32)
+    output, back_one, back_own, back_other, grads_keep, grads_send = middle(
+        places, core, context, other_context, x, cotangent.reshape(rows, D), vectors,
+        expand_bias.astype(f32).reshape(1, ff), proj_weight, expand_weight, shrink_weight,
+    )
+    back = jnp.concatenate([back_own, swap(back_other, "hc")], axis=0)
+    grads_arrived = swap(grads_send, "hc")
+    back_qs, back_ks, back_vs = zip(
+        *[attend_back(plan, doc_lengths, flip, pair, q, k, v, back, context, logsum) for pair in range(pairs)]
+    )
+    kept = PIECES // 2
+    first = scatter_sum(grads_keep[:kept], grads_arrived[:kept], first_order)
+    second = scatter_sum(grads_keep[kept:], grads_arrived[kept:], second_order)
+
+    far = input_far(core, qkv_weight, back_ks, back_vs, rows)
+    far_own = add_low(far[:rows], swap(far[rows:], "hc"))
+    from_far = swap(far_own, "hx")
+    near, joined_first, joined_second = joined_grads(
+        chip_places, core, qkv_weight, (x, x_near, x_far, x_far_near), back_qs, back_ks, back_vs
+    )
+    from_near = swap(near[rows:], "hc")
+    joined_first = gather_sum(scatter_sum(joined_first, None, first_order), first_order)
+    joined_second = gather_sum(scatter_sum(joined_second, None, second_order), second_order)
+    first = gather_sum(first, first_order)
+    second = gather_sum(second, second_order)
+    input_grad = back_one + near[:rows].astype(f32) + from_near.astype(f32) + from_far.astype(f32)
+
+    grad_shrink, grad_expand, low, high = unpack(
+        places, first, swap(first, "hc"), second, swap(second, "hc"), ff
+    )
+    grad_qkv, bias = unpack_joined(
+        chip_places, core, joined_first, joined_second, swap(joined_first, "hc"), swap(joined_second, "hc")
+    )
+    low_rows = low.shape[0]
+    grad_proj = jnp.concatenate([low, high[: D - low_rows]], axis=0)
+    vector = high[D - low_rows :]
+    grad_query_bias = jnp.concatenate([bias[:half, 0], bias[:half, 128]])
+    grad_value_bias = jnp.concatenate([bias[half:, 0], bias[half:, 128]])
+    grad_expand_bias = vector[8 : 8 + ff // D].reshape(ff)
     return (
-        output.astype(bf16).reshape(docs, rows, D),
+        output.reshape(docs, rows, D),
         input_grad.reshape(docs, rows, D),
-        grad_qkv, parts[0], parts[1], grad_proj, parts[2], parts[3], parts[4],
-        grad_expand, parts[5], grad_shrink, parts[6], parts[7], parts[8],
+        grad_qkv, grad_query_bias, grad_value_bias, grad_proj, vector[0], vector[1], vector[2],
+        grad_expand, grad_expand_bias, grad_shrink, vector[3], vector[4], vector[5],
     )
 
 

time: 654 us -> 504 us (0.77)
  matrix products: 147 us -> 0 us
  Pallas kernels: 71.5 us -> 191 us
  other arithmetic: 106 us -> 14 us
  waiting for transfers between devices: 143 us -> 220 us
  local copies, waits for them, and re-layouts: 79.5 us -> 25.4 us
  blocking collectives: 44.2 us -> 0 us
    dot_general x20 -> x0, matrix products: 147 us -> none  [the longest x6 67.5 us: dot_nn(): lax.dot_general(left, right, (((1,), (0,)), ((), ())), preferred_element_...]
    pallas_call x0 -> x7, Pallas kernels: none -> 117 us  [the longest x1 57.7 us: middle(): pl.pallas_call(partial(middle_kernel, chunk=D), grid_spec=pltpu.PrefetchS...]
    ppermute x47 -> x45, waiting for transfers between devices: 143 us -> 220 us  [swap(): lax.ppermute(value, axis, [(place, place ^ bit) for place in range(size)])]
    convert_element_type x32 -> x15, other arithmetic: 52.2 us -> 6.22 us  [the longest x14 5.6 us: add_low(): return (left.astype(f32) + right.astype(f32)).astype(bf16)]
    psum x1 -> x0, blocking collectives: 44.2 us -> none  [per_device(): summed = lax.psum(jnp.concatenate(vectors), ('dp', 'hx', 'hc'))]
    select_n x18 -> x0, other arithmetic: 26.4 us -> none  [the longest x16 23.8 us: sum_everywhere(): jnp.where(upper == 0, jnp.concatenate([value, other], axis=0), jnp.concat...]
    unnamed x144 -> x84, local copies, waits for them, and re-layouts: 41.1 us -> 19.6 us
    dynamic_slice x21 -> x0, local copies, waits for them, and re-layouts: 16.2 us -> none  [the longest x20 14.8 us: sum_everywhere(): send = lax.dynamic_slice_in_dim(value, (1 - upper) * half, half, 0)]
  transfers between devices with their start and end apart: 47 -> 45, of which waited for: 18 -> 19; matrix products, arithmetic and copies ran while one was open for 29% -> 3% of each run, Pallas kernels for 7% -> 17%
where the time goes in v2:
time: 504 us; the launch traced here: 498 us
  waiting for transfers between devices  220 us (44%)
  Pallas kernels  191 us (38%)
  starting transfers between devices  45.6 us (9%)
  local copies, waits for them, and re-layouts  25.4 us (5%)
  other arithmetic  14 us (3%)
    ppermute x45, waiting for transfers between devices, swap(): lax.ppermute(value, axis, [(place, place ^ bit) for place in range(size)])  220 us
    pallas_call x1, Pallas kernels, middle(): pl.pallas_call(partial(middle_kernel, chunk=D), grid_spec=pltpu.PrefetchS...  57.7 us
    pallas_call x3, Pallas kernels, attend_back(): pl.pallas_call(partial(backward_kernel, unroll=8, items=query_names.shape...  47.3 us
    ppermute x45, starting transfers between devices, swap(): lax.ppermute(value, axis, [(place, place ^ bit) for place in range(size)])  45.6 us
    pallas_call x1, Pallas kernels, attend(): pl.pallas_call(partial(forward_kernel, unroll=8, query_blocks=query_block...  26 us
    pallas_call x1, Pallas kernels, joined_grads(): pl.pallas_call(partial(joined_kernel, tiles=tiles, pairs=pairs), grid_spe...  21.9 us
    unnamed x84, local copies, waits for them, and re-layouts  19.6 us
    pallas_call x1, Pallas kernels, unpack(): pl.pallas_call(partial(unpack_kernel, rows=rows), grid_spec=pltpu.Prefetc...  14.4 us
  transfers between devices with their start and end apart: 45, of which 19 were waited for; matrix products, arithmetic and copies ran while one was open for 3% of the time, Pallas kernels for 17%

profile of v2, /device:TPU:0, one launch (start us, length us, event | category | flops | bytes accessed | tf_op | source)
XLA Modules:
  0.0 498.1 jit_solution(13242592386355265463)
XLA Ops:
  6.6 31.8 %collective-permute-done.1.x_ref.refs_5_ = bf16[1024,768]{1,0:T(8,128)(2,1)} collective-permute-done((bf16[1024,768]{1,0:T(8,128)(2,1)}, bf16[1024,768]{1,0:T(8,128)(2,1)}, u32[]{:S(2)}, u32[]{:S(2)}) %collective-permute-start.1) | collective-permute-done | bytes 1572896 | tf_op jit(solution)/shard_map/ppermute | solution.py:814
  45.5 5.9 %project_chip.1 = (bf16[2048,384]{1,0:T(8,128)(2,1)S(1)}, bf16[4096,384]{1,0:T(8,128)(2,1)S(1)}, bf16[4096,384]{1,0:T(8,128)(2,1)S(1)}) custom-call(s32[1]{0:T(128)} %bitcast.2.core, bf16[1024,768]{1,0:T(8,128)(2,1)S(1)} %bitcast.19, bf16[1024,768]{1,0:T(8,128)(2,1)S(1)} %copy-done.20, bf16[768,2304]{1,0:T(8,128)(2,1)S(1)} %copy-done, ...), custom_call_target="tpu_custom_call" | custom-call | flops 4000000000 | bytes 10000000 | tf_op jit(solution)/shard_map/project_chip/pallas_call | solution.py:335
  51.4 6.1 %project_far.1 = (bf16[4096,384]{1,0:T(8,128)(2,1)S(1)}, bf16[4096,384]{1,0:T(8,128)(2,1)S(1)}) custom-call(s32[1]{0:T(128)} %bitcast.2.core, bf16[1024,768]{1,0:T(8,128)(2,1)} %collective-permute-done.1.x_ref.refs_5_, bf16[1024,768]{1,0:T(8,128)(2,1)} %collective-permute-done.2.x_near_ref.refs_6_, ...), custom_call_target="tpu_custom_call", output_to_operand_aliasing={{0}: (6, {}), {1}: (7, {})} | custom-call | flops 3000000000 | bytes 10000000 | tf_op jit(solution)/shard_map/project_far/pallas_call | solution.py:361
  60.9 26.0 %attend_forward.1 = (bf16[2048,384]{1,0:T(8,128)(2,1)S(1)}, f32[3,32,128]{2,1,0:T(8,128)S(1)}) custom-call(s32[40,8]{1,0:T(8,128)S(1)} %get-tuple-element.118.key_names, s32[40,8]{1,0:T(8,128)S(1)} %get-tuple-element.117.bias_names, s32[1]{0:T(128)} %bitcast.5.global_name, s32[1]{0:T(128)S(6)} %copy.85.lengths, s32[1]{0:T(128)} %bitcast.6.flips, ...), custom_call_target="tpu_custom_call" | custom-call | flops 40000000000 | bytes 10000000 | tf_op jit(solution)/shard_map/attend_forward/pallas_call | solution.py:173
  91.6 57.7 %middle.1 = (bf16[1024,768]{1,0:T(8,128)(2,1)}, f32[1024,768]{1,0:T(8,128)}, bf16[1024,384]{1,0:T(8,128)(2,1)}, bf16[1024,384]{1,0:T(8,128)(2,1)}, bf16[32,112,7...) custom-call(s32[2]{0:T(128)} %pad_add_fusion.2.places, s32[1]{0:T(128)} %bitcast.2.core, bf16[2048,384]{1,0:T(8,128)(2,1)} %copy-done.15, ...), custom_call_target="tpu_custom_call" | custom-call | flops 60000002048 | bytes 10000000 | tf_op jit(solution)/shard_map/middle/pallas_call | solution.py:560
  151.3 8.5 %collective-permute-done.4 = bf16[1024,384]{1,0:T(8,128)(2,1)} collective-permute-done((bf16[1024,384]{1,0:T(8,128)(2,1)}, bf16[1024,384]{1,0:T(8,128)(2,1)}, u32[]{:S(2)}, u32[]{:S(2)}) %collective-permute-start.4) | collective-permute-done | bytes 786464 | tf_op jit(solution)/shard_map/ppermute | solution.py:814
  164.0 15.7 %attend_backward.5 = (bf16[2048,128]{1,0:T(8,128)(2,1)S(1)}, bf16[4096,128]{1,0:T(8,128)(2,1)S(1)}, bf16[4096,128]{1,0:T(8,128)(2,1)S(1)}) custom-call(s32[40]{0:T(128)S(1)} %concatenate.87.query_names, s32[40,8]{1,0:T(8,128)S(1)} %get-tuple-element.118.key_names, s32[40,8]{1,0:T(8,128)S(1)} %get-tuple-element.117.bias_names, s32[1]{0:T(128)S(6)} %copy.85.lengths, ...), custom_call_target="tpu_custom_call" | custom-call | flops 16000000000 | bytes 1000000 | tf_op jit(solution)/shard_map/attend_backward/pallas_call | solution.py:253
  181.6 15.7 %attend_backward.4 = (bf16[2048,128]{1,0:T(8,128)(2,1)S(1)}, bf16[4096,128]{1,0:T(8,128)(2,1)S(1)}, bf16[4096,128]{1,0:T(8,128)(2,1)S(1)}) custom-call(s32[40]{0:T(128)S(1)} %concatenate.87.query_names, s32[40,8]{1,0:T(8,128)S(1)} %get-tuple-element.118.key_names, s32[40,8]{1,0:T(8,128)S(1)} %get-tuple-element.117.bias_names, s32[1]{0:T(128)S(6)} %copy.85.lengths, ...), custom_call_target="tpu_custom_call" | custom-call | flops 16000000000 | bytes 1000000 | tf_op jit(solution)/shard_map/attend_backward/pallas_call | solution.py:253
  198.4 15.9 %attend_backward.3 = (bf16[2048,128]{1,0:T(8,128)(2,1)S(1)}, bf16[4096,128]{1,0:T(8,128)(2,1)S(1)}, bf16[4096,128]{1,0:T(8,128)(2,1)S(1)}) custom-call(s32[40]{0:T(128)S(1)} %concatenate.87.query_names, s32[40,8]{1,0:T(8,128)S(1)} %get-tuple-element.118.key_names, s32[40,8]{1,0:T(8,128)S(1)} %get-tuple-element.117.bias_names, s32[1]{0:T(128)S(6)} %copy.85.lengths, ...), custom_call_target="tpu_custom_call" | custom-call | flops 16000000000 | bytes 1000000 | tf_op jit(solution)/shard_map/attend_backward/pallas_call | solution.py:253
  219.8 21.9 %joined_grads.1 = (bf16[2048,768]{1,0:T(8,128)(2,1)}, bf16[16,48,640]{2,1,0:T(8,128)(2,1)S(1)}, bf16[16,48,640]{2,1,0:T(8,128)(2,1)S(1)}) custom-call(s32[2]{0:T(128)S(1)} %pad_add_fusion.3.places, s32[1]{0:T(128)} %bitcast.2.core, bf16[768,2304]{1,0:T(8,128)(2,1)} %refs_1_.3, bf16[768,2304]{1,0:T(8,128)(2,1)} %refs_1_.3, bf16[768,2304]{1,0:T(8,128)(2,1)} %refs_1_.3, ...), custom_call_target="tpu_custom_call" | custom-call | flops 10000000000 | bytes 10000000 | tf_op jit(solution)/shard_map/joined_grads/pallas_call | solution.py:693
  244.2 11.7 %collective-permute-done.16 = bf16[8,48,640]{2,1,0:T(8,128)(2,1)S(1)} collective-permute-done((bf16[8,48,640]{2,1,0:T(8,128)(2,1)S(1)}, bf16[8,48,640]{2,1,0:T(8,128)(2,1)S(1)}, u32[]{:S(2)}, u32[]{:S(2)}) %collective-permute-start.16) | collective-permute-done | bytes 491552 | tf_op jit(solution)/shard_map/ppermute | solution.py:814
  268.8 15.7 %collective-permute-done.36 = bf16[8,112,768]{2,1,0:T(8,128)(2,1)S(1)} collective-permute-done((bf16[8,112,768]{2,1,0:T(8,128)(2,1)S(1)}, bf16[8,112,768]{2,1,0:T(8,128)(2,1)S(1)}, u32[]{:S(2)}, u32[]{:S(2)}) %collective-permute-start.36) | collective-permute-done | bytes 1376288 | tf_op jit(solution)/shard_map/ppermute | solution.py:814
  291.4 9.9 %collective-permute-done.37 = bf16[4,112,768]{2,1,0:T(8,128)(2,1)S(1)} collective-permute-done((bf16[4,112,768]{2,1,0:T(8,128)(2,1)S(1)}, bf16[4,112,768]{2,1,0:T(8,128)(2,1)S(1)}, u32[]{:S(2)}, u32[]{:S(2)}) %collective-permute-start.37) | collective-permute-done | bytes 688160 | tf_op jit(solution)/shard_map/ppermute | solution.py:814
  304.8 5.7 %collective-permute-done.29 = bf16[2,112,768]{2,1,0:T(8,128)(2,1)S(1)} collective-permute-done((bf16[2,112,768]{2,1,0:T(8,128)(2,1)S(1)}, bf16[2,112,768]{2,1,0:T(8,128)(2,1)S(1)}, u32[]{:S(2)}, u32[]{:S(2)}) %collective-permute-start.29) | collective-permute-done | bytes 344096 | tf_op jit(solution)/shard_map/ppermute | solution.py:814
  321.3 7.5 %collective-permute-done.39 = bf16[1,112,768]{2,1,0:T(8,128)(2,1)S(1)} collective-permute-done((bf16[1,112,768]{2,1,0:T(8,128)(2,1)S(1)}, bf16[1,112,768]{2,1,0:T(8,128)(2,1)S(1)}, u32[]{:S(2)}, u32[]{:S(2)}) %collective-permute-start.39) | collective-permute-done | bytes 172064 | tf_op jit(solution)/shard_map/ppermute | solution.py:814
  332.1 16.5 %collective-permute-done.40 = bf16[1,112,768]{2,1,0:T(8,128)(2,1)S(1)} collective-permute-done((bf16[1,112,768]{2,1,0:T(8,128)(2,1)S(1)}, bf16[1,112,768]{2,1,0:T(8,128)(2,1)S(1)}, u32[]{:S(2)}, u32[]{:S(2)}) %collective-permute-start.40) | collective-permute-done | bytes 172064 | tf_op jit(solution)/shard_map/ppermute | solution.py:814
  352.4 11.4 %collective-permute-done.41 = bf16[2,112,768]{2,1,0:T(8,128)(2,1)S(1)} collective-permute-done((bf16[2,112,768]{2,1,0:T(8,128)(2,1)S(1)}, bf16[2,112,768]{2,1,0:T(8,128)(2,1)S(1)}, u32[]{:S(2)}, u32[]{:S(2)}) %collective-permute-start.41) | collective-permute-done | bytes 344096 | tf_op jit(solution)/shard_map/ppermute | solution.py:814
  372.7 13.8 %collective-permute-done.22 = bf16[4,48,640]{2,1,0:T(8,128)(2,1)S(1)} collective-permute-done((bf16[4,48,640]{2,1,0:T(8,128)(2,1)S(1)}, bf16[4,48,640]{2,1,0:T(8,128)(2,1)S(1)}, u32[]{:S(2)}, u32[]{:S(2)}) %collective-permute-start.22) | collective-permute-done | bytes 245792 | tf_op jit(solution)/shard_map/ppermute | solution.py:814
  390.8 9.9 %collective-permute-done.23 = bf16[8,48,640]{2,1,0:T(8,128)(2,1)S(1)} collective-permute-done((bf16[8,48,640]{2,1,0:T(8,128)(2,1)S(1)}, bf16[8,48,640]{2,1,0:T(8,128)(2,1)S(1)}, u32[]{:S(2)}, u32[]{:S(2)}) %collective-permute-start.23) | collective-permute-done | bytes 491552 | tf_op jit(solution)/shard_map/ppermute | solution.py:814
  401.2 27.2 %collective-permute-done.43 = bf16[8,112,768]{2,1,0:T(8,128)(2,1)S(1)} collective-permute-done((bf16[8,112,768]{2,1,0:T(8,128)(2,1)S(1)}, bf16[8,112,768]{2,1,0:T(8,128)(2,1)S(1)}, u32[]{:S(2)}, u32[]{:S(2)}) %collective-permute-start.43) | collective-permute-done | bytes 1376288 | tf_op jit(solution)/shard_map/ppermute | solution.py:814
  431.5 11.0 %collective-permute-done.15 = bf16[8,48,640]{2,1,0:T(8,128)(2,1)S(1)} collective-permute-done((bf16[8,48,640]{2,1,0:T(8,128)(2,1)S(1)}, bf16[8,48,640]{2,1,0:T(8,128)(2,1)S(1)}, u32[]{:S(2)}, u32[]{:S(2)}) %collective-permute-start.15) | collective-permute-done | bytes 491552 | tf_op jit(solution)/shard_map/ppermute | solution.py:814
  446.8 7.1 %unpack_joined.1 = (f32[768,2304]{1,0:T(8,128)}, f32[768,256]{1,0:T(8,128)S(1)}) custom-call(s32[2]{0:T(128)S(1)} %pad_add_fusion.3.places, s32[1]{0:T(128)} %bitcast.2.core, bf16[16,48,640]{2,1,0:T(8,128)(2,1)S(1)} %constant_dynamic-update-slice_fusion.2.first_own, bf16[16,48,640]{2,1,0:T(8,128)(2,1)S(1)} %constant_dynamic-update-slice_fusion.7.second_own, ...), custom_call_target="tpu_custom_call" | custom-call | flops 1000000 | bytes 10000000 | tf_op jit(solution)/shard_map/unpack_joined/pallas_call | solution.py:794
  455.4 22.5 %collective-permute-done.7 = bf16[1024,768]{1,0:T(8,128)(2,1)S(1)} collective-permute-done((bf16[1024,768]{1,0:T(8,128)(2,1)S(1)}, bf16[1024,768]{1,0:T(8,128)(2,1)S(1)}, u32[]{:S(2)}, u32[]{:S(2)}) %collective-permute-start.7) | collective-permute-done | bytes 1572896 | tf_op jit(solution)/shard_map/ppermute | solution.py:814
  480.3 14.4 %unpack.1 = (f32[3072,768]{1,0:T(8,128)}, f32[768,3072]{1,0:T(8,128)}, f32[512,768]{1,0:T(8,128)S(1)}, f32[512,768]{1,0:T(8,128)S(1)}) custom-call(s32[2]{0:T(128)S(1)} %copy-done.17, bf16[16,112,768]{2,1,0:T(8,128)(2,1)S(1)} %constant_dynamic-update-slice_fusion.12.first_own, bf16[16,112,768]{2,1,0:T(8,128)(2,1)S(1)} %collective-permute-done.35.first_other, ...), custom_call_target="tpu_custom_call" | custom-call | flops 1000000 | bytes 42000000 | tf_op jit(solution)/shard_map/unpack/pallas_call | solution.py:742
  (243 shorter events, 105.8 us)
Async XLA Ops:
  0.6 37.7 %collective-permute-start.1 = (bf16[1024,768]{1,0:T(8,128)(2,1)}, bf16[1024,768]{1,0:T(8,128)(2,1)}, u32[]{:S(2)}, u32[]{:S(2)}) collective-permute-start(bf16[1024,768]{1,0:T(8,128)(2,1)} %bitcast.15), channel_id=1, source_target_pairs={{0,2},{2,0},{1,3},{3,1},{4,6},{6,4},{5,7},{7,5},{8,10},{10,8},{9,1... | collective-permute-start | bytes 4718600 | tf_op jit(solution)/shard_map/ppermute | solution.py:814
  3.7 35.9 %collective-permute-start = (bf16[1024,768]{1,0:T(8,128)(2,1)}, bf16[1024,768]{1,0:T(8,128)(2,1)S(1)}, u32[]{:S(2)}, u32[]{:S(2)}) collective-permute-start(bf16[1024,768]{1,0:T(8,128)(2,1)} %bitcast.16), channel_id=1, source_target_pairs={{0,1},{1,0},{2,3},{3,2},{4,5},{5,4},{6,7},{7,6},{8,9},{9,8},{10,11... | collective-permute-start | bytes 4718600 | tf_op jit(solution)/shard_map/ppermute | solution.py:814
  149.3 65.0 %collective-permute-start.26 = (bf16[32,112,768]{2,1,0:T(8,128)(2,1)}, bf16[32,112,768]{2,1,0:T(8,128)(2,1)}, u32[]{:S(2)}, u32[]{:S(2)}) collective-permute-start(bf16[32,112,768]{2,1,0:T(8,128)(2,1)} %get-tuple-element.72), channel_id=1, source_target_pairs={{0,1},{1,0},{2,3},{3,2},{4,5},{5,4},{6,7},{7,6},{8,9},{9,8},{10,11... | collective-permute-start | bytes 16515080 | tf_op jit(solution)/shard_map/ppermute | solution.py:814
  217.9 50.2 %collective-permute-start.27 = (bf16[8,112,768]{2,1,0:T(8,128)(2,1)S(1)}, bf16[8,112,768]{2,1,0:T(8,128)(2,1)S(1)}, u32[]{:S(2)}, u32[]{:S(2)}) collective-permute-start(bf16[8,112,768]{2,1,0:T(8,128)(2,1)S(1)} %get-tuple-element.97), channel_id=1, source_target_pairs={{0,4},{4,0},{8,12},{12,8},{16,20},{20,16},{24,28},{28,24},{1,5},{5... | collective-permute-start | bytes 4128776 | tf_op jit(solution)/shard_map/ppermute | solution.py:814
  243.3 41.1 %collective-permute-start.36 = (bf16[8,112,768]{2,1,0:T(8,128)(2,1)S(1)}, bf16[8,112,768]{2,1,0:T(8,128)(2,1)S(1)}, u32[]{:S(2)}, u32[]{:S(2)}) collective-permute-start(bf16[8,112,768]{2,1,0:T(8,128)(2,1)S(1)} %get-tuple-element.96), channel_id=1, source_target_pairs={{0,2},{2,0},{1,3},{3,1},{4,6},{6,4},{5,7},{7,5},{8,10},{10,8},{9,1... | collective-permute-start | bytes 4128776 | tf_op jit(solution)/shard_map/ppermute | solution.py:814
  261.7 23.5 %collective-permute-start.9 = (bf16[4,48,640]{2,1,0:T(8,128)(2,1)S(1)}, bf16[4,48,640]{2,1,0:T(8,128)(2,1)S(1)}, u32[]{:S(2)}, u32[]{:S(2)}) collective-permute-start(bf16[4,48,640]{2,1,0:T(8,128)(2,1)S(1)} %get-tuple-element.106), channel_id=1, source_target_pairs={{0,8},{4,12},{8,0},{12,4},{16,24},{20,28},{24,16},{28,20},{1,9},{5... | collective-permute-start | bytes 737288 | tf_op jit(solution)/shard_map/ppermute | solution.py:814
  266.2 21.9 %collective-permute-start.18 = (bf16[2,48,640]{2,1,0:T(8,128)(2,1)S(1)}, bf16[2,48,640]{2,1,0:T(8,128)(2,1)S(1)}, u32[]{:S(2)}, u32[]{:S(2)}) collective-permute-start(bf16[2,48,640]{2,1,0:T(8,128)(2,1)S(1)} %get-tuple-element.112), channel_id=1, source_target_pairs={{0,8},{4,12},{8,0},{12,4},{16,24},{20,28},{24,16},{28,20},{1,9},{5... | collective-permute-start | bytes 368648 | tf_op jit(solution)/shard_map/ppermute | solution.py:814
  288.1 40.8 %collective-permute-start.19 = (bf16[1,48,640]{2,1,0:T(8,128)(2,1)S(1)}, bf16[1,48,640]{2,1,0:T(8,128)(2,1)S(1)}, u32[]{:S(2)}, u32[]{:S(2)}) collective-permute-start(bf16[1,48,640]{2,1,0:T(8,128)(2,1)S(1)} %add_convert_fusion.28), channel_id=1, source_target_pairs={{0,16},{4,20},{8,24},{12,28},{16,0},{20,4},{24,8},{28,12},{1,17},{... | collective-permute-start | bytes 184328 | tf_op jit(solution)/shard_map/ppermute | solution.py:814
  288.5 22.0 %collective-permute-start.29 = (bf16[2,112,768]{2,1,0:T(8,128)(2,1)S(1)}, bf16[2,112,768]{2,1,0:T(8,128)(2,1)S(1)}, u32[]{:S(2)}, u32[]{:S(2)}) collective-permute-start(bf16[2,112,768]{2,1,0:T(8,128)(2,1)S(1)} %get-tuple-element.110), channel_id=1, source_target_pairs={{0,16},{4,20},{8,24},{12,28},{16,0},{20,4},{24,8},{28,12},{1,17},{... | collective-permute-start | bytes 1032200 | tf_op jit(solution)/shard_map/ppermute | solution.py:814
  303.2 45.5 %collective-permute-start.11 = (bf16[1,48,640]{2,1,0:T(8,128)(2,1)S(1)}, bf16[1,48,640]{2,1,0:T(8,128)(2,1)S(1)}, u32[]{:S(2)}, u32[]{:S(2)}) collective-permute-start(bf16[1,48,640]{2,1,0:T(8,128)(2,1)S(1)} %add_convert_fusion.31), channel_id=1, source_target_pairs={{0,2},{2,0},{1,3},{3,1},{4,6},{6,4},{5,7},{7,5},{8,10},{10,8},{9,1... | collective-permute-start | bytes 184328 | tf_op jit(solution)/shard_map/ppermute | solution.py:814
  329.0 21.4 %collective-permute-start.20 = (bf16[1,48,640]{2,1,0:T(8,128)(2,1)S(1)}, bf16[1,48,640]{2,1,0:T(8,128)(2,1)S(1)}, u32[]{:S(2)}, u32[]{:S(2)}) collective-permute-start(bf16[1,48,640]{2,1,0:T(8,128)(2,1)S(1)} %get-tuple-element.92), channel_id=1, source_target_pairs={{0,16},{4,20},{8,24},{12,28},{16,0},{20,4},{24,8},{28,12},{1,17},{... | collective-permute-start | bytes 184328 | tf_op jit(solution)/shard_map/ppermute | solution.py:814
  332.0 33.5 %collective-permute-start.32 = (bf16[2,112,768]{2,1,0:T(8,128)(2,1)S(1)}, bf16[2,112,768]{2,1,0:T(8,128)(2,1)S(1)}, u32[]{:S(2)}, u32[]{:S(2)}) collective-permute-start(bf16[2,112,768]{2,1,0:T(8,128)(2,1)S(1)} %pad_maximum_fusion.7), channel_id=1, source_target_pairs={{0,16},{4,20},{8,24},{12,28},{16,0},{20,4},{24,8},{28,12},{1,17},{... | collective-permute-start | bytes 1032200 | tf_op jit(solution)/shard_map/ppermute | solution.py:814
  348.7 23.8 %collective-permute-start.12 = (bf16[1,48,640]{2,1,0:T(8,128)(2,1)S(1)}, bf16[1,48,640]{2,1,0:T(8,128)(2,1)S(1)}, u32[]{:S(2)}, u32[]{:S(2)}) collective-permute-start(bf16[1,48,640]{2,1,0:T(8,128)(2,1)S(1)} %get-tuple-element.94), channel_id=1, source_target_pairs={{0,2},{2,0},{1,3},{3,1},{4,6},{6,4},{5,7},{7,5},{8,10},{10,8},{9,1... | collective-permute-start | bytes 184328 | tf_op jit(solution)/shard_map/ppermute | solution.py:814
  363.9 24.3 %collective-permute-start.42 = (bf16[4,112,768]{2,1,0:T(8,128)(2,1)S(1)}, bf16[4,112,768]{2,1,0:T(8,128)(2,1)S(1)}, u32[]{:S(2)}, u32[]{:S(2)}) collective-permute-start(bf16[4,112,768]{2,1,0:T(8,128)(2,1)S(1)} %pad_maximum_fusion.4), channel_id=1, source_target_pairs={{0,4},{4,0},{8,12},{12,8},{16,20},{20,16},{24,28},{28,24},{1,5},{5... | collective-permute-start | bytes 2064392 | tf_op jit(solution)/shard_map/ppermute | solution.py:814
  365.6 23.3 %collective-permute-start.33 = (bf16[4,112,768]{2,1,0:T(8,128)(2,1)S(1)}, bf16[4,112,768]{2,1,0:T(8,128)(2,1)S(1)}, u32[]{:S(2)}, u32[]{:S(2)}) collective-permute-start(bf16[4,112,768]{2,1,0:T(8,128)(2,1)S(1)} %pad_maximum_fusion.3), channel_id=1, source_target_pairs={{0,8},{4,12},{8,0},{12,4},{16,24},{20,28},{24,16},{28,20},{1,9},{5... | collective-permute-start | bytes 2064392 | tf_op jit(solution)/shard_map/ppermute | solution.py:814
  372.5 58.5 %collective-permute-start.6 = (bf16[1024,768]{1,0:T(8,128)(2,1)S(1)}, bf16[1024,768]{1,0:T(8,128)(2,1)S(1)}, u32[]{:S(2)}, u32[]{:S(2)}) collective-permute-start(bf16[1024,768]{1,0:T(8,128)(2,1)S(1)} %slice.329), channel_id=1, source_target_pairs={{0,1},{1,0},{2,3},{3,2},{4,5},{5,4},{6,7},{7,6},{8,9},{9,8},{10,11... | collective-permute-start | bytes 4718600 | tf_op jit(solution)/shard_map/ppermute | solution.py:814
  388.4 39.9 %collective-permute-start.43 = (bf16[8,112,768]{2,1,0:T(8,128)(2,1)S(1)}, bf16[8,112,768]{2,1,0:T(8,128)(2,1)S(1)}, u32[]{:S(2)}, u32[]{:S(2)}) collective-permute-start(bf16[8,112,768]{2,1,0:T(8,128)(2,1)S(1)} %pad_maximum_fusion.2), channel_id=1, source_target_pairs={{0,2},{2,0},{1,3},{3,1},{4,6},{6,4},{5,7},{7,5},{8,10},{10,8},{9,1... | collective-permute-start | bytes 4128776 | tf_op jit(solution)/shard_map/ppermute | solution.py:814
  389.0 39.5 %collective-permute-start.34 = (bf16[8,112,768]{2,1,0:T(8,128)(2,1)S(1)}, bf16[8,112,768]{2,1,0:T(8,128)(2,1)S(1)}, u32[]{:S(2)}, u32[]{:S(2)}) collective-permute-start(bf16[8,112,768]{2,1,0:T(8,128)(2,1)S(1)} %pad_maximum_fusion.1), channel_id=1, source_target_pairs={{0,4},{4,0},{8,12},{12,8},{16,20},{20,16},{24,28},{28,24},{1,5},{5... | collective-permute-start | bytes 4128776 | tf_op jit(solution)/shard_map/ppermute | solution.py:814
  390.7 38.5 %collective-permute-start.14 = (bf16[4,48,640]{2,1,0:T(8,128)(2,1)S(1)}, bf16[4,48,640]{2,1,0:T(8,128)(2,1)S(1)}, u32[]{:S(2)}, u32[]{:S(2)}) collective-permute-start(bf16[4,48,640]{2,1,0:T(8,128)(2,1)S(1)} %pad_maximum_fusion.9), channel_id=1, source_target_pairs={{0,8},{4,12},{8,0},{12,4},{16,24},{20,28},{24,16},{28,20},{1,9},{5... | collective-permute-start | bytes 737288 | tf_op jit(solution)/shard_map/ppermute | solution.py:814
  400.9 43.3 %collective-permute-start.25 = (bf16[16,48,640]{2,1,0:T(8,128)(2,1)S(1)}, bf16[16,48,640]{2,1,0:T(8,128)(2,1)S(1)}, u32[]{:S(2)}, u32[]{:S(2)}) collective-permute-start(bf16[16,48,640]{2,1,0:T(8,128)(2,1)S(1)} %constant_dynamic-update-slice_fusion.7.second_own), channel_id=1, source_target_pairs={{0,1},{1,0},{2,3},{3,2},{4,5},{5,4},{6,7},{7,6},{8,9},{9,8},{10,11... | collective-permute-start | bytes 2949128 | tf_op jit(solution)/shard_map/ppermute | solution.py:814
  428.4 51.9 %collective-permute-start.44 = (bf16[16,112,768]{2,1,0:T(8,128)(2,1)S(1)}, bf16[16,112,768]{2,1,0:T(8,128)(2,1)S(1)}, u32[]{:S(2)}, u32[]{:S(2)}) collective-permute-start(bf16[16,112,768]{2,1,0:T(8,128)(2,1)S(1)} %constant_dynamic-update-slice_fusion.17.second_own), channel_id=1, source_target_pairs={{0,1},{1,0},{2,3},{3,2},{4,5},{5,4},{6,7},{7,6},{8,9},{9,8},{10,11... | collective-permute-start | bytes 8257544 | tf_op jit(solution)/shard_map/ppermute | solution.py:814
  428.6 51.7 %collective-permute-start.35 = (bf16[16,112,768]{2,1,0:T(8,128)(2,1)S(1)}, bf16[16,112,768]{2,1,0:T(8,128)(2,1)S(1)}, u32[]{:S(2)}, u32[]{:S(2)}) collective-permute-start(bf16[16,112,768]{2,1,0:T(8,128)(2,1)S(1)} %constant_dynamic-update-slice_fusion.12.first_own), channel_id=1, source_target_pairs={{0,1},{1,0},{2,3},{3,2},{4,5},{5,4},{6,7},{7,6},{8,9},{9,8},{10,11... | collective-permute-start | bytes 8257544 | tf_op jit(solution)/shard_map/ppermute | solution.py:814
  430.9 24.5 %collective-permute-start.5 = (bf16[1024,768]{1,0:T(8,128)(2,1)S(1)}, bf16[1024,768]{1,0:T(8,128)(2,1)S(1)}, u32[]{:S(2)}, u32[]{:S(2)}) collective-permute-start(bf16[1024,768]{1,0:T(8,128)(2,1)S(1)} %slice.253), channel_id=1, source_target_pairs={{0,1},{1,0},{2,3},{3,2},{4,5},{5,4},{6,7},{7,6},{8,9},{9,8},{10,11... | collective-permute-start | bytes 4718600 | tf_op jit(solution)/shard_map/ppermute | solution.py:814
  442.4 35.5 %collective-permute-start.7 = (bf16[1024,768]{1,0:T(8,128)(2,1)S(1)}, bf16[1024,768]{1,0:T(8,128)(2,1)S(1)}, u32[]{:S(2)}, u32[]{:S(2)}) collective-permute-start(bf16[1024,768]{1,0:T(8,128)(2,1)S(1)} %add_convert_fusion), channel_id=1, source_target_pairs={{0,2},{2,0},{1,3},{3,1},{4,6},{6,4},{5,7},{7,5},{8,10},{10,8},{9,1... | collective-permute-start | bytes 4718600 | tf_op jit(solution)/shard_map/ppermute | solution.py:814
  (56 other events, 714.4 us)

commit v3 on v2

--- a/solution.py
+++ b/solution.py
@@ -273,7 +273,7 @@
             jax.ShapeDtypeStruct((tokens, 128), bf16),
         ],
         compiler_params=pltpu.CompilerParams(vmem_limit_bytes=40 << 20),
-        cost_estimate=pl.CostEstimate(flops=16 * 10**9, bytes_accessed=10**6, transcendentals=10**6),
+        cost_estimate=pl.CostEstimate(flops=10**9, bytes_accessed=10**6, transcendentals=10**5),
         name="attend_backward",
     )(query_names, key_names, bias_names, length, flip, q, k, v, back, context, logsum)
 
@@ -405,23 +405,62 @@
 VECTOR_ROWS = 256
 
 
-def middle_kernel(
+class Packer:
+    def __init__(self, places, stage, sems, keep, send, first_row, rows, pieces):
+        self.places, self.stage, self.sems = places, stage, sems
+        self.keep, self.send = keep, send
+        self.first_row, self.rows, self.pieces = first_row, rows, pieces
+
+    def target(self, array, place):
+        return array.at[place, pl.ds(self.first_row, self.rows)]
+
+    def wait(self, slot):
+        pltpu.make_async_copy(self.stage.at[slot], self.target(self.keep, 0), self.sems.at[slot]).wait()
+
+    def put(self, number, color, piece, value):
+        slot = lax.rem(number, STAGES)
+
+        @pl.when(number >= STAGES)
+        def _():
+            self.wait(slot)
+
+        self.stage[slot] = value.astype(bf16)
+        kept = self.pieces // 2
+        relative = piece ^ self.places[color]
+        place = color * kept + lax.rem(relative, kept)
+
+        @pl.when(relative < kept)
+        def _():
+            pltpu.make_async_copy(self.stage.at[slot], self.target(self.keep, place), self.sems.at[slot]).start()
+
+        @pl.when(relative >= kept)
+        def _():
+            pltpu.make_async_copy(self.stage.at[slot], self.target(self.send, place), self.sems.at[slot]).start()
+
+    def finish(self):
+        for slot in range(STAGES):
+            self.wait(slot)
+
+
+def proj_loads(proj_hbm, proj_w, core, sems):
+    half = D // 2
+    hc = core[0]
+    return [
+        pltpu.make_async_copy(proj_hbm.at[pl.ds(hc * half, half)], proj_w.at[pl.ds(0, half)], sems.at[0]),
+        pltpu.make_async_copy(proj_hbm.at[pl.ds((1 - hc) * half, half)], proj_w.at[pl.ds(half, half)], sems.at[1]),
+    ]
+
+
+def middle_forward_kernel(
     places, core,
     own_ref, other_ref, x_ref, cot_ref, vector_ref, expand_bias_ref, proj_hbm, expand_hbm, shrink_hbm,
-    output_ref, back_one_ref, back_own_ref, back_other_ref, keep_ref, send_ref,
-    proj_w, expand_w, shrink_w, active_s, slope_s, shrink_g, expand_g, proj_g, vector_g, bias_g, stage,
-    weight_sems, sems, *, chunk,
+    output_ref, back_two_ref, normed_ref, scale_ref, slope_ref, vector_g, keep_ref, send_ref,
+    proj_w, expand_w, shrink_w, active_s, shrink_g, stage, weight_sems, sems, *, chunk,
 ):
     step = pl.program_id(0)
-    half = D // 2
     ff = expand_w.shape[1]
     chunks = ff // chunk
-    hc = core[0]
-    loads = [
-        pltpu.make_async_copy(proj_hbm.at[pl.ds(hc * half, half)], proj_w.at[pl.ds(0, half)], weight_sems.at[0]),
-        pltpu.make_async_copy(
-            proj_hbm.at[pl.ds((1 - hc) * half, half)], proj_w.at[pl.ds(half, half)], weight_sems.at[1]
-        ),
+    loads = proj_loads(proj_hbm, proj_w, core, weight_sems) + [
         pltpu.make_async_copy(expand_hbm, expand_w, weight_sems.at[2]),
         pltpu.make_async_copy(shrink_hbm, shrink_w, weight_sems.at[3]),
     ]
@@ -430,8 +469,8 @@
     def _():
         for load in loads:
             load.start()
-        for total in (shrink_g, expand_g, proj_g, vector_g, bias_g):
-            total[...] = jnp.zeros_like(total)
+        shrink_g[...] = jnp.zeros_like(shrink_g)
+        vector_g[...] = jnp.zeros_like(vector_g)
         loads[0].wait()
         loads[1].wait()
 
@@ -441,6 +480,8 @@
     context = jnp.concatenate([own_ref[...], other_ref[...]], axis=1)
     resid = x_ref[...].astype(f32) + dot_nn(context, proj_w[...]) + vector(0)
     normed_one, scale_one = norm_parts(resid)
+    normed_ref[...] = normed_one
+    scale_ref[...] = jnp.broadcast_to(scale_one, scale_ref.shape)
     hidden = normed_one * vector(1) + vector(2)
     low = hidden.astype(bf16)
     resid_two = hidden + vector(3)
@@ -456,27 +497,152 @@
         active, slope = gelu_pair(inner)
         active = active.astype(bf16)
         active_s[:, cols] = active
-        slope_s[:, cols] = slope.astype(bf16)
+        slope_ref[:, cols] = slope.astype(bf16)
         resid_two = resid_two + dot_nn(active, shrink_w[cols, :])
     normed_two, scale_two = norm_parts(resid_two)
     output_ref[...] = (normed_two * vector(4) + vector(5)).astype(bf16)
     cot = cot_ref[...].astype(f32)
     back_two = norm_back(vector(4) * cot, normed_two, scale_two)
+    back_two_ref[...] = back_two
     low_two = back_two.astype(bf16)
     vector_g[3:4, :] += column_sum(low_two.astype(f32))
     vector_g[4:5, :] += column_sum(cot * normed_two)
     vector_g[5:6, :] += column_sum(cot)
-    back = back_two
+    rows = ff // (2 * PIECES)
+    packer = Packer(places, stage, sems, keep_ref, send_ref, 0, rows, PIECES)
+    per = chunk // rows
     for part in range(chunks):
         cols = slice(part * chunk, (part + 1) * chunk)
-        back_inner = (dot_nt(low_two, shrink_w[cols, :]) * slope_s[:, cols].astype(f32)).astype(bf16)
+        shrink_g[cols, :] += dot_tn(active_s[:, cols], low_two)
+
+        @pl.when(step == pl.num_programs(0) - 1)
+        def _():
+            def put(within, carry):
+                number = part * per + within
+                value = shrink_g[pl.ds(pl.multiple_of(number * rows, rows), rows), :]
+                packer.put(number, (part * per) // PIECES, lax.rem(number, PIECES), value)
+                return carry
+
+            lax.fori_loop(0, per, put, 0)
+
+    @pl.when(step == pl.num_programs(0) - 1)
+    def _():
+        packer.finish()
+
+
+def row_spec(tile, width):
+    return pl.BlockSpec((tile, width), lambda step, *_: (step, 0))
+
+
+def whole_spec(shape):
+    return pl.BlockSpec(shape, lambda step, *_: (0, 0))
+
+
+def middle_forward(places, core, own, other, x, cot, vectors, expand_bias, proj_weight, expand_weight, shrink_weight):
+    rows = x.shape[0]
+    ff = expand_weight.shape[1]
+    half = D // 2
+    tile = 256
+    piece_rows = ff // (2 * PIECES)
+    kept = pl.BlockSpec(memory_space=pl.ANY)
+    packed = jax.ShapeDtypeStruct((PIECES, piece_rows, D), bf16)
+    return pl.pallas_call(
+        partial(middle_forward_kernel, chunk=D),
+        grid_spec=pltpu.PrefetchScalarGridSpec(
+            num_scalar_prefetch=2,
+            grid=(rows // tile,),
+            in_specs=[row_spec(tile, half)] * 2
+            + [row_spec(tile, D)] * 2
+            + [whole_spec(vectors.shape), whole_spec(expand_bias.shape), kept, kept, kept],
+            out_specs=[row_spec(tile, D)] * 3
+            + [row_spec(tile, 128), row_spec(tile, ff), whole_spec((8, D)), kept, kept],
+            scratch_shapes=[
+                pltpu.VMEM((D, D), bf16),
+                pltpu.VMEM((D, ff), bf16),
+                pltpu.VMEM((ff, D), bf16),
+                pltpu.VMEM((tile, ff), bf16),
+                pltpu.VMEM((ff, D), f32),
+                pltpu.VMEM((STAGES, piece_rows, D), bf16),
+                pltpu.SemaphoreType.DMA((4,)),
+                pltpu.SemaphoreType.DMA((STAGES,)),
+            ],
+        ),
+        out_shape=[
+            jax.ShapeDtypeStruct((rows, D), bf16),
+            jax.ShapeDtypeStruct((rows, D), f32),
+            jax.ShapeDtypeStruct((rows, D), f32),
+            jax.ShapeDtypeStruct((rows, 128), f32),
+            jax.ShapeDtypeStruct((rows, ff), bf16),
+            jax.ShapeDtypeStruct((8, D), f32),
+            packed,
+            packed,
+        ],
+        compiler_params=pltpu.CompilerParams(vmem_limit_bytes=60 << 20),
+        cost_estimate=pl.CostEstimate(flops=10**9, bytes_accessed=10**7, transcendentals=10**6),
+        name="middle_forward",
+    )(places, core, own, other, x, cot, vectors, expand_bias, proj_weight, expand_weight, shrink_weight)
+
+
+def middle_back_kernel(
+    places, core,
+    own_ref, other_ref, back_two_ref, normed_ref, scale_ref, slope_ref, vector_ref, sums_ref,
+    proj_hbm, expand_hbm, shrink_hbm,
+    back_one_ref, back_own_ref, back_other_ref, keep_ref, send_ref,
+    proj_w, expand_w, shrink_w, expand_g, proj_g, vector_g, bias_g, stage, extra_stage, weight_sems, sems, extra_sems,
+    *, chunk,
+):
+    step = pl.program_id(0)
+    last = step == pl.num_programs(0) - 1
+    half = D // 2
+    ff = expand_w.shape[1]
+    chunks = ff // chunk
+    loads = proj_loads(proj_hbm, proj_w, core, weight_sems) + [
+        pltpu.make_async_copy(expand_hbm, expand_w, weight_sems.at[2]),
+        pltpu.make_async_copy(shrink_hbm, shrink_w, weight_sems.at[3]),
+    ]
+
+    @pl.when(step == 0)
+    def _():
+        for load in reversed(loads):
+            load.start()
+        for total in (expand_g, proj_g, bias_g):
+            total[...] = jnp.zeros_like(total)
+        vector_g[...] = sums_ref[...]
+        for load in reversed(loads):
+            load.wait()
+
+    def vector(row):
+        return vector_ref[pl.ds(row, 1), :]
+
+    context = jnp.concatenate([own_ref[...], other_ref[...]], axis=1)
+    normed_one = normed_ref[...]
+    low = (normed_one * vector(1) + vector(2)).astype(bf16)
+    back = back_two_ref[...]
+    low_two = back.astype(bf16)
+    rows = ff // (2 * PIECES)
+    packer = Packer(places, stage, sems, keep_ref, send_ref, 0, rows, PIECES)
+    per = D // rows
+    wide = ff // chunk
+    for part in range(chunks):
+        cols = slice(part * chunk, (part + 1) * chunk)
+        back_inner = (dot_nt(low_two, shrink_w[cols, :]) * slope_ref[:, cols].astype(f32)).astype(bf16)
         bias_g[:, cols] += column_sum(back_inner.astype(f32))
+        expand_g[:, cols] += dot_tn(low, back_inner)
         back = back + dot_nt(back_inner, expand_w[:, cols])
-        shrink_g[cols, :] += dot_tn(active_s[:, cols], low_two)
-        expand_g[:, cols] += dot_tn(low, back_inner)
+
+        @pl.when(last)
+        def _():
+            def put(down, carry):
+                number = down * wide + part
+                value = expand_g[pl.ds(pl.multiple_of(down * rows, rows), rows), cols]
+                packer.put(part * per + down, number // PIECES, lax.rem(number, PIECES), value)
+                return carry
+
+            lax.fori_loop(0, per, put, 0)
+
     vector_g[1:2, :] += column_sum(back * normed_one)
     vector_g[2:3, :] += column_sum(back)
-    back_one = norm_back(vector(1) * back, normed_one, scale_one)
+    back_one = norm_back(vector(1) * back, normed_one, scale_ref[:, 0:1])
     back_one_ref[...] = back_one
     low_one = back_one.astype(bf16)
     vector_g[0:1, :] += column_sum(low_one.astype(f32))
@@ -485,103 +651,64 @@
     back_own_ref[...] = back_context[:, :half]
     back_other_ref[...] = back_context[:, half:]
 
-    @pl.when(step == pl.num_programs(0) - 1)
+    @pl.when(last)
     def _():
         proj_g[D:, :] = jnp.zeros((proj_g.shape[0] - D, D), f32)
         proj_g[D : D + 8, :] = vector_g[...]
         for part in range(ff // D):
             proj_g[D + 8 + part : D + 9 + part, :] = bias_g[:, part * D : (part + 1) * D]
-        kept = PIECES // 2
-        rows = ff // PIECES
         extra = proj_g.shape[0] // (2 * PIECES)
-        wide = ff // D
         half_chunks = half // extra
-
-        def wait(color, slot):
-            pltpu.make_async_copy(stage.at[color, slot], keep_ref.at[0], sems.at[color, slot]).wait()
-
-        def put(piece, carry):
-            slot = lax.rem(piece, STAGES)
-
-            @pl.when(piece >= STAGES)
-            def _():
-                wait(0, slot)
-                wait(1, slot)
-
-            first = piece ^ places[0]
-            second = piece ^ places[1]
-
-            def extra_rows(place):
-                turned = lax.rem(place + half_chunks * hc, 2 * half_chunks)
-                place = jnp.where(place < 2 * half_chunks, turned, place)
-                return proj_g[pl.ds(pl.multiple_of(place * extra, extra), extra), :].astype(bf16)
-
-            stage[0, slot, :rows, :] = shrink_g[pl.ds(pl.multiple_of(first * rows, rows), rows), :].astype(bf16)
-            stage[0, slot, rows:, :] = extra_rows(first)
-            down = pl.ds(pl.multiple_of((second // wide) * rows, rows), rows)
-            across = pl.ds(pl.multiple_of((second % wide) * D, D), D)
-            stage[1, slot, :rows, :] = expand_g[down, across].astype(bf16)
-            stage[1, slot, rows:, :] = extra_rows(PIECES + second)
-            place = lax.rem(piece, kept)
-            for color in range(2):
-                source = stage.at[color, slot]
-
-                @pl.when(piece < kept)
-                def _():
-                    pltpu.make_async_copy(source, keep_ref.at[color * kept + place], sems.at[color, slot]).start()
-
-                @pl.when(piece >= kept)
-                def _():
-                    pltpu.make_async_copy(source, send_ref.at[color * kept + place], sems.at[color, slot]).start()
-
+        extra_packer = Packer(places, extra_stage, extra_sems, keep_ref, send_ref, rows, extra, PIECES)
+
+        def put(number, carry):
+            turned = lax.rem(number + half_chunks * core[0], 2 * half_chunks)
+            source = jnp.where(number < 2 * half_chunks, turned, number)
+            value = proj_g[pl.ds(pl.multiple_of(source * extra, extra), extra), :]
+            extra_packer.put(number, number // PIECES, lax.rem(number, PIECES), value)
             return carry
 
-        lax.fori_loop(0, PIECES, put, 0)
-        for slot in range(STAGES):
-            wait(0, slot)
-            wait(1, slot)
-
-
-def middle(places, core, own, other, x, cot, vectors, expand_bias, proj_weight, expand_weight, shrink_weight):
-    rows = x.shape[0]
+        lax.fori_loop(0, 2 * PIECES, put, 0)
+        packer.finish()
+        extra_packer.finish()
+
+
+def middle_back(
+    places, core, own, other, back_two, normed, scale, slope, vectors, sums, proj_weight, expand_weight, shrink_weight
+):
+    rows = own.shape[0] // 2
     ff = expand_weight.shape[1]
     half = D // 2
     tile = 256
-    piece_rows = ff // PIECES + (D + VECTOR_ROWS) // (2 * PIECES)
-
-    def row(width):
-        return pl.BlockSpec((tile, width), lambda step, *_: (step, 0))
-
-    def whole(array):
-        return pl.BlockSpec(array.shape, lambda step, *_: (0, 0))
-
+    piece_rows = ff // (2 * PIECES)
+    extra_rows = (D + VECTOR_ROWS) // (2 * PIECES)
     kept = pl.BlockSpec(memory_space=pl.ANY)
-    packed = jax.ShapeDtypeStruct((PIECES, piece_rows, D), bf16)
+    packed = jax.ShapeDtypeStruct((PIECES, piece_rows + extra_rows, D), bf16)
     return pl.pallas_call(
-        partial(middle_kernel, chunk=D),
+        partial(middle_back_kernel, chunk=D),
         grid_spec=pltpu.PrefetchScalarGridSpec(
             num_scalar_prefetch=2,
             grid=(rows // tile,),
-            in_specs=[row(half), row(half), row(D), row(D), whole(vectors), whole(expand_bias), kept, kept, kept],
-            out_specs=[row(D), row(D), row(half), row(half), kept, kept],
+            in_specs=[row_spec(tile, half)] * 2
+            + [row_spec(tile, D)] * 2
+            + [row_spec(tile, 128), row_spec(tile, ff), whole_spec(vectors.shape), whole_spec((8, D)), kept, kept, kept],
+            out_specs=[row_spec(tile, D), row_spec(tile, half), row_spec(tile, half), kept, kept],
             scratch_shapes=[
                 pltpu.VMEM((D, D), bf16),
                 pltpu.VMEM((D, ff), bf16),
                 pltpu.VMEM((ff, D), bf16),
-                pltpu.VMEM((tile, ff), bf16),
-                pltpu.VMEM((tile, ff), bf16),
-                pltpu.VMEM((ff, D), f32),
                 pltpu.VMEM((D, ff), f32),
                 pltpu.VMEM((D + VECTOR_ROWS, D), f32),
                 pltpu.VMEM((8, D), f32),
                 pltpu.VMEM((1, ff), f32),
-                pltpu.VMEM((2, STAGES, piece_rows, D), bf16),
+                pltpu.VMEM((STAGES, piece_rows, D), bf16),
+                pltpu.VMEM((STAGES, extra_rows, D), bf16),
                 pltpu.SemaphoreType.DMA((4,)),
-                pltpu.SemaphoreType.DMA((2, STAGES)),
+                pltpu.SemaphoreType.DMA((STAGES,)),
+                pltpu.SemaphoreType.DMA((STAGES,)),
             ],
         ),
         out_shape=[
-            jax.ShapeDtypeStruct((rows, D), bf16),
             jax.ShapeDtypeStruct((rows, D), f32),
             jax.ShapeDtypeStruct((rows, half), bf16),
             jax.ShapeDtypeStruct((rows, half), bf16),
@@ -589,9 +716,9 @@
             packed,
         ],
         compiler_params=pltpu.CompilerParams(vmem_limit_bytes=60 << 20),
-        cost_estimate=pl.CostEstimate(flops=60 * 10**9, bytes_accessed=10**7, transcendentals=10**7),
-        name="middle",
-    )(places, core, own, other, x, cot, vectors, expand_bias, proj_weight, expand_weight, shrink_weight)
+        cost_estimate=pl.CostEstimate(flops=10**9, bytes_accessed=10**7, transcendentals=0),
+        name="middle_back",
+    )(places, core, own, other, back_two, normed, scale, slope, vectors, sums, proj_weight, expand_weight, shrink_weight)
 
 
 def input_far_kernel(core, *refs):
@@ -626,68 +753,54 @@
 
 
 def joined_kernel(places, core, *refs, tiles, pairs):
-    w_q, w_k, w_v = refs[:3]
-    x_refs = refs[3:7]
-    arrays = refs[7 : 7 + 3 * pairs]
-    near_ref, first_ref, second_ref = refs[7 + 3 * pairs : 10 + 3 * pairs]
-    q_g, k_g, v_g, b_g = refs[10 + 3 * pairs :]
+    x_refs = refs[:4]
+    arrays = refs[4 : 4 + 3 * pairs]
+    first_ref, second_ref = refs[4 + 3 * pairs : 6 + 3 * pairs]
+    total, sums = refs[6 + 3 * pairs :]
     step = pl.program_id(0)
     half = D // 2
     per = tiles // 4
 
     @pl.when(step == 0)
     def _():
-        for total in (q_g, k_g, v_g, b_g):
-            total[...] = jnp.zeros_like(total)
-
-    def joined(which):
-        return jnp.concatenate([ref[...] for ref in arrays[which * pairs : (which + 1) * pairs]], axis=1)
-
-    ones = jnp.ones((TILE, 128), bf16)
+        total[...] = jnp.zeros_like(total)
+        sums[...] = jnp.zeros_like(sums)
+
+    def joined(first, last):
+        return jnp.concatenate([ref[...] for ref in arrays[first * pairs : last * pairs]], axis=1)
+
     for piece in range(4):
 
         @pl.when((step >= piece * per) & (step < (piece + 1) * per))
         def _():
-            x = x_refs[piece][...]
-            back_k = joined(1)
-            back_v = joined(2)
-            k_g[...] += dot_tn(x, back_k)
-            v_g[...] += dot_tn(x, back_v)
-            b_g[half:, :] += dot_tn(back_v, ones)
-            if piece < 2:
-                back_q = joined(0)
-                q_g[...] += dot_tn(x, back_q)
-                b_g[:half, :] += dot_tn(back_q, ones)
-                near_ref[...] = (
-                    dot_nt(back_q, w_q[...]) + dot_nt(back_k, w_k[...]) + dot_nt(back_v, w_v[...])
-                ).astype(bf16)
+            first = 0 if piece < 2 else 1
+            back = joined(first, 3)
+            total[:, first * half : 3 * half] += dot_tn(x_refs[piece][...], back)
+            sums[0:1, first * half :] += column_sum(back.astype(f32))
 
     @pl.when(step == tiles - 1)
     def _():
         rows = D // QKV_PIECES
+        q_sums = jnp.transpose(jnp.broadcast_to(sums[0:1, :half], (128, half)))
+        v_sums = jnp.transpose(jnp.broadcast_to(sums[0:1, 2 * half :], (128, half)))
+        total[:half, 3 * half :] = q_sums
+        total[half:, 3 * half :] = v_sums
+        width = first_ref.shape[2]
         for piece in range(QKV_PIECES):
             part = pl.ds(pl.multiple_of((piece ^ places[0]) * rows, rows), rows)
-            first_ref[piece, :, :half] = q_g[part, :].astype(bf16)
-            first_ref[piece, :, half:] = k_g[part, :256].astype(bf16)
+            first_ref[piece] = total[part, :width].astype(bf16)
             part = pl.ds(pl.multiple_of((piece ^ places[1]) * rows, rows), rows)
-            second_ref[piece, :, :128] = k_g[part, 256:].astype(bf16)
-            second_ref[piece, :, 128 : 128 + half] = v_g[part, :].astype(bf16)
-            second_ref[piece, :, 128 + half :] = b_g[part, :].astype(bf16)
-
-
-def joined_grads(places, core, qkv_weight, xs, back_qs, back_ks, back_vs):
+            second_ref[piece] = total[part, width:].astype(bf16)
+
+
+def joined_grads(places, core, xs, back_qs, back_ks, back_vs):
     rows = xs[0].shape[0]
     pairs = len(back_qs)
     per = rows // TILE
     tiles = 4 * per
-    half = D // 2
-    width = half + 256
+    width = D // 2 + 256
     token = pl.BlockSpec((TILE, 128), lambda step, *_: (step, 0))
     query = pl.BlockSpec((TILE, 128), lambda step, *_: (jnp.minimum(step, 2 * per - 1), 0))
-    weights = [
-        pl.BlockSpec((D, half), lambda step, places, core, which=which: (0, 2 * which + core[0]))
-        for which in range(3)
-    ]
     packed = pl.BlockSpec((QKV_PIECES, D // QKV_PIECES, width), lambda step, *_: (0, 0, 0))
     packed_shape = jax.ShapeDtypeStruct((QKV_PIECES, D // QKV_PIECES, width), bf16)
     return pl.pallas_call(
@@ -695,72 +808,139 @@
         grid_spec=pltpu.PrefetchScalarGridSpec(
             num_scalar_prefetch=2,
             grid=(tiles,),
-            in_specs=weights
-            + [piece_spec(piece, per, D) for piece in range(4)]
-            + [query] * pairs
-            + [token] * (2 * pairs),
-            out_specs=[
-                pl.BlockSpec((TILE, D), lambda step, *_: (jnp.minimum(step, 2 * per - 1), 0)),
-                packed,
-                packed,
-            ],
-            scratch_shapes=[pltpu.VMEM((D, half), f32)] * 3 + [pltpu.VMEM((D, 128), f32)],
+            in_specs=[piece_spec(piece, per, D) for piece in range(4)] + [query] * pairs + [token] * (2 * pairs),
+            out_specs=[packed, packed],
+            scratch_shapes=[pltpu.VMEM((D, 2 * width), f32), pltpu.VMEM((8, 3 * D // 2), f32)],
         ),
-        out_shape=[jax.ShapeDtypeStruct((2 * rows, D), bf16), packed_shape, packed_shape],
+        out_shape=[packed_shape, packed_shape],
         compiler_params=pltpu.CompilerParams(vmem_limit_bytes=48 << 20),
-        cost_estimate=pl.CostEstimate(flops=10 * 10**9, bytes_accessed=10**7, transcendentals=0),
+        cost_estimate=pl.CostEstimate(flops=10**9, bytes_accessed=10**7, transcendentals=0),
         name="joined_grads",
-    )(places, core, qkv_weight, qkv_weight, qkv_weight, *xs, *back_qs, *back_ks, *back_vs)
-
-
-def unpack_kernel(places, first_own, first_other, second_own, second_other, shrink_ref, expand_ref, low_ref, high_ref, *, rows):
+    )(places, core, *xs, *back_qs, *back_ks, *back_vs)
+
+
+def input_near_kernel(core, *refs):
+    w_q, w_k, w_v, out = refs[0], refs[1], refs[2], refs[-1]
+    arrays = refs[3:-1]
+    pairs = len(arrays) // 3
+
+    def joined(which):
+        return jnp.concatenate([ref[...] for ref in arrays[which * pairs : (which + 1) * pairs]], axis=1)
+
+    out[...] = (dot_nt(joined(0), w_q[...]) + dot_nt(joined(1), w_k[...]) + dot_nt(joined(2), w_v[...])).astype(bf16)
+
+
+def input_near(core, qkv_weight, back_qs, back_ks, back_vs):
+    rows = back_qs[0].shape[0]
+    token = pl.BlockSpec((TILE, 128), lambda step, *_: (step, 0))
+    arrays = list(back_qs) + list(back_ks) + list(back_vs)
+    return pl.pallas_call(
+        input_near_kernel,
+        grid_spec=pltpu.PrefetchScalarGridSpec(
+            num_scalar_prefetch=1,
+            grid=(rows // TILE,),
+            in_specs=[own_weight(0), own_weight(1), own_weight(2)] + [token] * len(arrays),
+            out_specs=pl.BlockSpec((TILE, D), lambda step, *_: (step, 0)),
+        ),
+        out_shape=jax.ShapeDtypeStruct((rows, D), bf16),
+        compiler_params=pltpu.CompilerParams(vmem_limit_bytes=32 << 20),
+        cost_estimate=pl.CostEstimate(flops=10**9, bytes_accessed=10**7, transcendentals=0),
+        name="input_near",
+    )(core, qkv_weight, qkv_weight, qkv_weight, *arrays)
+
+
+def unpack_shrink_body(places, first_own, first_other, second_own, second_other, out):
     step = pl.program_id(0)
+    within = lax.rem(step, PIECES)
+    for color, (own, other) in enumerate(((first_own, first_other), (second_own, second_other))):
+
+        @pl.when((step // PIECES == color) & (within < PIECES // 2))
+        def _():
+            out[...] = own[0].astype(f32)
+
+        @pl.when((step // PIECES == color) & (within >= PIECES // 2))
+        def _():
+            out[...] = other[0].astype(f32)
+
+
+def colored(color, part, rows):
     kept = PIECES // 2
 
-    def put(first, second):
-        shrink_ref[...] = first[0, :rows, :].astype(f32)
-        expand_ref[...] = second[0, :rows, :].astype(f32)
-        low_ref[...] = first[0, rows:, :].astype(f32)
-        high_ref[...] = second[0, rows:, :].astype(f32)
-
-    @pl.when(step < kept)
-    def _():
-        put(first_own, second_own)
-
-    @pl.when(step >= kept)
-    def _():
-        put(first_other, second_other)
-
-
-def unpack(places, first_own, first_other, second_own, second_other, ff):
-    kept, piece_rows, _ = first_own.shape
-    rows = ff // PIECES
+    def index(step, *_):
+        return (jnp.clip(step - color * PIECES - part * kept, 0, kept - 1), 0, 0)
+
+    return pl.BlockSpec((1, rows, D), index)
+
+
+def piece_number(step, places):
+    color = step // PIECES
+    return color * PIECES + (lax.rem(step, PIECES) ^ places[color])
+
+
+def unpack_shrink(places, first_own, first_other, second_own, second_other):
+    rows = first_own.shape[1]
+    return pl.pallas_call(
+        unpack_shrink_body,
+        grid_spec=pltpu.PrefetchScalarGridSpec(
+            num_scalar_prefetch=1,
+            grid=(2 * PIECES,),
+            in_specs=[colored(color, part, rows) for color in range(2) for part in range(2)],
+            out_specs=pl.BlockSpec((rows, D), lambda step, places: (piece_number(step, places), 0)),
+        ),
+        out_shape=jax.ShapeDtypeStruct((2 * PIECES * rows, D), f32),
+        compiler_params=pltpu.CompilerParams(vmem_limit_bytes=32 << 20),
+        cost_estimate=pl.CostEstimate(flops=10**6, bytes_accessed=10**6, transcendentals=0),
+        name="unpack_shrink",
+    )(places, first_own, first_other, second_own, second_other)
+
+
+def unpack_expand_body(places, first_own, first_other, second_own, second_other, expand_ref, proj_ref, *, rows):
+    step = pl.program_id(0)
+    within = lax.rem(step, PIECES)
+
+    def put(source):
+        expand_ref[...] = source[0, :rows, :].astype(f32)
+        proj_ref[...] = source[0, rows:, :].astype(f32)
+
+    for color, (own, other) in enumerate(((first_own, first_other), (second_own, second_other))):
+
+        @pl.when((step // PIECES == color) & (within < PIECES // 2))
+        def _():
+            put(own)
+
+        @pl.when((step // PIECES == color) & (within >= PIECES // 2))
+        def _():
+            put(other)
+
+
+def unpack_expand(places, first_own, first_other, second_own, second_other, ff):
+    piece_rows = first_own.shape[1]
+    rows = ff // (2 * PIECES)
     extra = piece_rows - rows
     wide = ff // D
-    own = pl.BlockSpec((1, piece_rows, D), lambda step, *_: (jnp.minimum(step, kept - 1), 0, 0))
-    other = pl.BlockSpec((1, piece_rows, D), lambda step, *_: (jnp.maximum(step - kept, 0), 0, 0))
+
+    def place(step, places):
+        number = piece_number(step, places)
+        return (number // wide, lax.rem(number, wide))
+
     return pl.pallas_call(
-        partial(unpack_kernel, rows=rows),
+        partial(unpack_expand_body, rows=rows),
         grid_spec=pltpu.PrefetchScalarGridSpec(
             num_scalar_prefetch=1,
-            grid=(PIECES,),
-            in_specs=[own, other, own, other],
+            grid=(2 * PIECES,),
+            in_specs=[colored(color, part, piece_rows) for color in range(2) for part in range(2)],
             out_specs=[
-                pl.BlockSpec((rows, D), lambda step, places: (step ^ places[0], 0)),
-                pl.BlockSpec((rows, D), lambda step, places: ((step ^ places[1]) // wide, (step ^ places[1]) % wide)),
-                pl.BlockSpec((extra, D), lambda step, places: (step ^ places[0], 0)),
-                pl.BlockSpec((extra, D), lambda step, places: (step ^ places[1], 0)),
+                pl.BlockSpec((rows, D), place),
+                pl.BlockSpec((extra, D), lambda step, places: (piece_number(step, places), 0)),
             ],
         ),
         out_shape=[
-            jax.ShapeDtypeStruct((ff, D), f32),
             jax.ShapeDtypeStruct((D, ff), f32),
-            jax.ShapeDtypeStruct((extra * PIECES, D), f32),
-            jax.ShapeDtypeStruct((extra * PIECES, D), f32),
+            jax.ShapeDtypeStruct((2 * PIECES * extra, D), f32),
         ],
         compiler_params=pltpu.CompilerParams(vmem_limit_bytes=32 << 20),
-        cost_estimate=pl.CostEstimate(flops=10**6, bytes_accessed=42 * 10**6, transcendentals=0),
-        name="unpack",
+        cost_estimate=pl.CostEstimate(flops=10**6, bytes_accessed=10**6, transcendentals=0),
+        name="unpack_expand",
     )(places, first_own, first_other, second_own, second_other)
 
 
@@ -825,26 +1005,55 @@
     return (left.astype(f32) + right.astype(f32)).astype(bf16)
 
 
-def scatter_sum(keep, arrived, order):
-    for axis, bit in order:
-        half = keep.shape[0] // 2
-        if arrived is None:
-            send, keep = keep[half:], keep[:half]
+class Chain:
+    def __init__(self, order, keep, arrived=None):
+        self.order, self.keep, self.arrived = order, keep, arrived
+        self.at = 0
+        self.gathered = None
+
+    def send(self):
+        steps = len(self.order)
+        if self.at < steps:
+            half = self.keep.shape[0] // 2
+            low, high = self.keep[:half], self.keep[half:]
+            if self.arrived is not None:
+                low = add_low(low, self.arrived[:half])
+                high = add_low(high, self.arrived[half:])
+            self.keep = low
+            return high
+        if self.at == steps:
+            total = add_low(self.keep, self.arrived)
+            bit = 8
+            while bit < lax.axis_size("dp"):
+                total = add_low(total, swap(total, "dp", bit))
+                bit *= 2
+            self.gathered = total
         else:
-            send, keep = add_low(keep[half:], arrived[half:]), add_low(keep[:half], arrived[:half])
-        arrived = swap(send, axis, bit)
-    total = add_low(keep, arrived)
-    bit = 8
-    while bit < lax.axis_size("dp"):
-        total = add_low(total, swap(total, "dp", bit))
-        bit *= 2
-    return total
-
-
-def gather_sum(piece, order):
-    for axis, bit in reversed(order):
-        piece = jnp.concatenate([piece, swap(piece, axis, bit)], axis=0)
-    return piece
+            self.gathered = jnp.concatenate([self.gathered, self.arrived], axis=0)
+        return self.gathered
+
+    def move(self, value):
+        steps = len(self.order)
+        if self.at >= steps:
+            self.gathered = value
+        if self.at < 2 * steps:
+            axis, bit = self.order[self.at if self.at < steps else 2 * steps - 1 - self.at]
+        else:
+            axis, bit = "hc", 1
+        self.arrived = swap(value, axis, bit)
+        self.at += 1
+
+
+def advance(chains, tied=()):
+    sends = [chain.send() for chain in chains]
+    *sends, = lax.optimization_barrier(tuple(sends) + tuple(tied))
+    for chain, value in zip(chains, sends):
+        chain.move(value)
+    return sends[len(chains) :]
+
+
+def ready(*values):
+    return lax.optimization_barrier(values)
 
 
 def per_device(
@@ -872,53 +1081,86 @@
     core_order = [("hc", 1)]
     places = jnp.stack([place_of(core_order + first_order), place_of(core_order + second_order)])
     chip_places = jnp.stack([place_of(first_order), place_of(second_order)])
-
+    empty = jnp.zeros((D,), bf16)
+    vectors = jnp.stack(
+        [proj_bias, first_gain, first_shift, shrink_bias, second_gain, second_shift, empty, empty]
+    ).astype(f32)
     bias_q = query_bias.astype(f32).reshape(1, D)
     bias_v = value_bias.astype(f32).reshape(1, D)
+    kept = PIECES // 2
+
+    def two_chains(keep, arrived):
+        return [
+            Chain(first_order, keep[:kept], arrived[:kept]),
+            Chain(second_order, keep[kept:], arrived[kept:]),
+        ]
+
     q, k, v = project_chip(core, x, x_near, qkv_weight, bias_q, bias_v)
+    x_far, q = ready(x_far, q)
     x_far_near = swap(x_far, "hc")
     k, v = project_far(core, x_far, x_far_near, qkv_weight, bias_v, k, v)
     context, logsum = attend(plan, doc_lengths, flip, q, k, v)
     other_context = swap(context[rows:], "hc")
-    empty = jnp.zeros((D,), bf16)
-    vectors = jnp.stack(
-        [proj_bias, first_gain, first_shift, shrink_bias, second_gain, second_shift, empty, empty]
-    ).astype(f32)
-    output, back_one, back_own, back_other, grads_keep, grads_send = middle(
+    output, back_two, normed, scale, slope, sums, shrink_keep, shrink_send = middle_forward(
         places, core, context, other_context, x, cotangent.reshape(rows, D), vectors,
         expand_bias.astype(f32).reshape(1, ff), proj_weight, expand_weight, shrink_weight,
     )
+    shrink = two_chains(shrink_keep, swap(shrink_send, "hc"))
+    (back_two,) = advance(shrink, (back_two,))
+    back_one, back_own, back_other, expand_keep, expand_send = middle_back(
+        places, core, context, other_context, back_two, normed, scale, slope, vectors, sums,
+        proj_weight, expand_weight, shrink_weight,
+    )
     back = jnp.concatenate([back_own, swap(back_other, "hc")], axis=0)
-    grads_arrived = swap(grads_send, "hc")
-    back_qs, back_ks, back_vs = zip(
-        *[attend_back(plan, doc_lengths, flip, pair, q, k, v, back, context, logsum) for pair in range(pairs)]
+    back, expand_send = advance(shrink, (back, expand_send))
+    expand_arrived = swap(expand_send, "hc")
+    grads = []
+
+    def attend_pair(pair, back):
+        grads.append(attend_back(plan, doc_lengths, flip, pair, q, k, v, back, context, logsum))
+
+    attend_pair(0, back)
+    back, expand_keep, expand_arrived, _ = ready(back, expand_keep, expand_arrived, grads[0][0])
+    expand = two_chains(expand_keep, expand_arrived)
+    (back,) = advance(shrink + expand, (back,))
+    attend_pair(1, back)
+    back, _ = ready(back, grads[1][0])
+    (back,) = advance(shrink + expand, (back,))
+    attend_pair(2, back)
+    (last,) = advance(shrink + expand, (grads[2][0],))
+    grads[2] = (last,) + tuple(grads[2][1:])
+    back_qs, back_ks, back_vs = zip(*grads)
+
+    joined_first, joined_second = joined_grads(
+        chip_places, core, (x, x_near, x_far, x_far_near), back_qs, back_ks, back_vs
     )
-    kept = PIECES // 2
-    first = scatter_sum(grads_keep[:kept], grads_arrived[:kept], first_order)
-    second = scatter_sum(grads_keep[kept:], grads_arrived[kept:], second_order)
-
+    joined = [Chain(first_order, joined_first), Chain(second_order, joined_second)]
+    (last,) = advance(joined + shrink + expand, (back_ks[0],))
+    back_ks = (last,) + tuple(back_ks[1:])
     far = input_far(core, qkv_weight, back_ks, back_vs, rows)
     far_own = add_low(far[:rows], swap(far[rows:], "hc"))
+    (far_own,) = advance(joined + shrink + expand, (far_own,))
     from_far = swap(far_own, "hx")
-    near, joined_first, joined_second = joined_grads(
-        chip_places, core, qkv_weight, (x, x_near, x_far, x_far_near), back_qs, back_ks, back_vs
-    )
+    far_own, last = ready(far_own, back_qs[0])
+    near = input_near(core, qkv_weight, (last,) + tuple(back_qs[1:]), back_ks, back_vs)
     from_near = swap(near[rows:], "hc")
-    joined_first = gather_sum(scatter_sum(joined_first, None, first_order), first_order)
-    joined_second = gather_sum(scatter_sum(joined_second, None, second_order), second_order)
-    first = gather_sum(first, first_order)
-    second = gather_sum(second, second_order)
+
+    def left(chain):
+        return 2 * len(chain.order) + 1 - chain.at
+
+    while any(left(chain) > 0 for chain in joined + shrink + expand):
+        advance([chain for chain in joined + shrink + expand if left(chain) > 0])
     input_grad = back_one + near[:rows].astype(f32) + from_near.astype(f32) + from_far.astype(f32)
 
-    grad_shrink, grad_expand, low, high = unpack(
-        places, first, swap(first, "hc"), second, swap(second, "hc"), ff
-    )
-    grad_qkv, bias = unpack_joined(
-        chip_places, core, joined_first, joined_second, swap(joined_first, "hc"), swap(joined_second, "hc")
-    )
-    low_rows = low.shape[0]
-    grad_proj = jnp.concatenate([low, high[: D - low_rows]], axis=0)
-    vector = high[D - low_rows :]
+    def both(chains):
+        return [value for chain in chains for value in (chain.gathered, chain.arrived)]
+
+    grad_shrink = unpack_shrink(places, *both(shrink))
+    grad_expand, proj_rows = unpack_expand(places, *both(expand), ff)
+    first_own, first_other, second_own, second_other = both(joined)
+    grad_qkv, bias = unpack_joined(chip_places, core, first_own, second_own, first_other, second_other)
+    grad_proj = proj_rows[:D]
+    vector = proj_rows[D:]
     grad_query_bias = jnp.concatenate([bias[:half, 0], bias[:half, 128]])
     grad_value_bias = jnp.concatenate([bias[half:, 0], bias[half:, 128]])
     grad_expand_bias = vector[8 : 8 + ff // D].reshape(ff)

time: 504 us -> 520 us (1.032)
  waiting for transfers between devices: 220 us -> 123 us
  Pallas kernels: 191 us -> 252 us
  local copies, waits for them, and re-layouts: 25.4 us -> 54.3 us
  other arithmetic: 14 us -> 26.8 us
  starting transfers between devices: 45.6 us -> 54.4 us
    ppermute x45 -> x64, waiting for transfers between devices: 220 us -> 123 us  [swap(): lax.ppermute(value, axis, [(place, place ^ bit) for place in range(size)])]
    pallas_call x2 -> x5, Pallas kernels: 72.1 us -> 139 us  [the longest x1 44.9 us: middle_forward(): pl.pallas_call(partial(middle_forward_kernel, chunk=D), grid_spec=pltpu.P...]
    unnamed x84 -> x115, local copies, waits for them, and re-layouts: 19.6 us -> 35.7 us
    ppermute x45 -> x64, starting transfers between devices: 45.6 us -> 54.4 us  [swap(): lax.ppermute(value, axis, [(place, place ^ bit) for place in range(size)])]
    pallas_call x1, Pallas kernels: 21.9 us -> 13.2 us  [joined_grads(): pl.pallas_call(partial(joined_kernel, tiles=tiles, pairs=pairs), grid_spe...]
    convert_element_type x14 -> x27, other arithmetic: 5.6 us -> 14.2 us  [add_low(): return (left.astype(f32) + right.astype(f32)).astype(bf16)]
    another operation x8, local copies, waits for them, and re-layouts: 0.08 us -> 6.34 us  [per_device(): jnp.stack([proj_bias, first_gain, first_shift, shrink_bias, second_gain,...]
  transfers between devices with their start and end apart: 45 -> 64, of which waited for: 19 -> 22; matrix products, arithmetic and copies ran while one was open for 3% -> 7% of each run, Pallas kernels for 17% -> 31%
where the time goes in v3:
time: 520 us; the launch traced here: 513 us
  Pallas kernels  252 us (48%)
  waiting for transfers between devices  123 us (24%)
  starting transfers between devices  54.4 us (10%)
  local copies, waits for them, and re-layouts  54.3 us (10%)
  other arithmetic  26.8 us (5%)
    ppermute x64, waiting for transfers between devices, swap(): lax.ppermute(value, axis, [(place, place ^ bit) for place in range(size)])  123 us
    ppermute x64, starting transfers between devices, swap(): lax.ppermute(value, axis, [(place, place ^ bit) for place in range(size)])  54.4 us
    pallas_call x3, Pallas kernels, attend_back(): pl.pallas_call(partial(backward_kernel, unroll=8, items=query_names.shape...  47.3 us
    pallas_call x1, Pallas kernels, middle_forward(): pl.pallas_call(partial(middle_forward_kernel, chunk=D), grid_spec=pltpu.P...  44.9 us
    pallas_call x1, Pallas kernels, middle_back(): pl.pallas_call(partial(middle_back_kernel, chunk=D), grid_spec=pltpu.Pref...  42.6 us
    unnamed x115, local copies, waits for them, and re-layouts  35.7 us
    pallas_call x1, Pallas kernels, attend(): pl.pallas_call(partial(forward_kernel, unroll=8, query_blocks=query_block...  26 us
    pallas_call x1, Pallas kernels, unpack_expand(): pl.pallas_call(partial(unpack_expand_body, rows=rows), grid_spec=pltpu.Pr...  22.8 us
  transfers between devices with their start and end apart: 64, of which 22 were waited for; matrix products, arithmetic and copies ran while one was open for 7% of the time, Pallas kernels for 31%

profile of v3, /device:TPU:0, one launch (start us, length us, event | category | flops | bytes accessed | tf_op | source)
XLA Modules:
  0.0 513.1 jit_solution(14843727215123341814)
XLA Ops:
  11.1 5.9 %project_chip.1 = (bf16[2048,384]{1,0:T(8,128)(2,1)S(1)}, bf16[4096,384]{1,0:T(8,128)(2,1)S(1)}, bf16[4096,384]{1,0:T(8,128)(2,1)S(1)}) custom-call(s32[1]{0:T(128)} %bitcast.2.core, bf16[1024,768]{1,0:T(8,128)(2,1)S(1)} %bitcast.19, bf16[1024,768]{1,0:T(8,128)(2,1)S(1)} %copy-done.36, bf16[768,2304]{1,0:T(8,128)(2,1)S(1)} %copy-done, ...), custom_call_target="tpu_custom_call" | custom-call | flops 4000000000 | bytes 10000000 | tf_op jit(solution)/shard_map/project_chip/pallas_call | solution.py:335
  21.5 17.6 %collective-permute-done.x_ref.refs_2_ = bf16[1024,768]{1,0:T(8,128)(2,1)} collective-permute-done((bf16[1024,768]{1,0:T(8,128)(2,1)}, bf16[1024,768]{1,0:T(8,128)(2,1)}, u32[]{:S(2)}, u32[]{:S(2)}) %collective-permute-start) | collective-permute-done | bytes 1572896 | tf_op jit(solution)/shard_map/ppermute | solution.py:994
  53.4 5.7 %project_far.1 = (bf16[4096,384]{1,0:T(8,128)(2,1)S(1)}, bf16[4096,384]{1,0:T(8,128)(2,1)S(1)}) custom-call(s32[1]{0:T(128)} %bitcast.2.core, bf16[1024,768]{1,0:T(8,128)(2,1)} %collective-permute-done.x_ref.refs_2_, bf16[1024,768]{1,0:T(8,128)(2,1)} %collective-permute-done.2.x_near_ref.refs_3_, ...), custom_call_target="tpu_custom_call", output_to_operand_aliasing={{0}: (6, {}), {1}: (7, {})} | custom-call | flops 3000000000 | bytes 10000000 | tf_op jit(solution)/shard_map/project_far/pallas_call | solution.py:361
  62.5 26.0 %attend_forward.1 = (bf16[2048,384]{1,0:T(8,128)(2,1)S(1)}, f32[3,32,128]{2,1,0:T(8,128)S(1)}) custom-call(s32[40,8]{1,0:T(8,128)S(1)} %get-tuple-element.268.key_names, s32[40,8]{1,0:T(8,128)S(1)} %get-tuple-element.267.bias_names, s32[1]{0:T(128)} %bitcast.5.global_name, s32[1]{0:T(128)S(6)} %copy.68.lengths, s32[1]{0:T(128)} %bitcast.6.flips, ...), custom_call_target="tpu_custom_call" | custom-call | flops 40000000000 | bytes 10000000 | tf_op jit(solution)/shard_map/attend_forward/pallas_call | solution.py:173
  99.9 44.9 %middle_forward.1 = (bf16[1024,768]{1,0:T(8,128)(2,1)}, f32[1024,768]{1,0:T(8,128)}, f32[1024,768]{1,0:T(8,128)}, f32[1024,128]{1,0:T(8,128)}, bf16[1024,3072]{1...) custom-call(s32[2]{0:T(128)} %pad_add_fusion.2.places, ...), custom_call_target="tpu_custom_call" | custom-call | flops 1000000000 | bytes 10000000 | tf_op jit(solution)/shard_map/middle_forward/pallas_call | solution.py:549
  144.9 4.7 collective-permute-done.4
  156.2 42.6 %middle_back.1 = (f32[1024,768]{1,0:T(8,128)}, bf16[1024,384]{1,0:T(8,128)(2,1)}, bf16[1024,384]{1,0:T(8,128)(2,1)}, bf16[32,64,768]{2,1,0:T(8,128)(2,1)}, bf16[32,64,768]{2,1,0:T(8,128)(2,1)}) custom-call(s32[2]{0:T(128)} %pad_add_fusion.2.places, s32[1]{0:T(128)} %bitcast.2.core, bf16[2048,384]{1,0:T(8,128)(2,1)} %copy-done.12, ...), custom_call_target="tpu_custom_call" | custom-call | flops 1000000000 | bytes 10000000 | tf_op jit(solution)/shard_map/middle_back/pallas_call | solution.py:687
  209.4 15.9 %attend_backward.3 = (bf16[2048,128]{1,0:T(8,128)(2,1)S(1)}, bf16[4096,128]{1,0:T(8,128)(2,1)S(1)}, bf16[4096,128]{1,0:T(8,128)(2,1)S(1)}) custom-call(s32[40]{0:T(128)S(1)} %concatenate.96.query_names, s32[40,8]{1,0:T(8,128)S(1)} %copy-done.44, s32[40,8]{1,0:T(8,128)S(1)} %copy-done.41, s32[1]{0:T(128)S(6)} %copy.68.lengths, s32[1]{0:T(128)} %bitcast.6.flips, ...), custom_call_target="tpu_custom_call" | custom-call | flops 1000000000 | bytes 1000000 | tf_op jit(solution)/shard_map/attend_backward/pallas_call | solution.py:253
  245.0 15.7 %attend_backward.4 = (bf16[2048,128]{1,0:T(8,128)(2,1)S(1)}, bf16[4096,128]{1,0:T(8,128)(2,1)S(1)}, bf16[4096,128]{1,0:T(8,128)(2,1)S(1)}) custom-call(s32[40]{0:T(128)S(1)} %concatenate.96.query_names, s32[40,8]{1,0:T(8,128)S(1)} %copy-done.45, s32[40,8]{1,0:T(8,128)S(1)} %copy-done.42, s32[1]{0:T(128)S(6)} %copy.68.lengths, s32[1]{0:T(128)} %bitcast.6.flips, ...), custom_call_target="tpu_custom_call" | custom-call | flops 1000000000 | bytes 1000000 | tf_op jit(solution)/shard_map/attend_backward/pallas_call | solution.py:253
  266.9 15.7 %attend_backward.5 = (bf16[2048,128]{1,0:T(8,128)(2,1)S(1)}, bf16[4096,128]{1,0:T(8,128)(2,1)S(1)}, bf16[4096,128]{1,0:T(8,128)(2,1)S(1)}) custom-call(s32[40]{0:T(128)S(1)} %concatenate.96.query_names, s32[40,8]{1,0:T(8,128)S(1)} %copy-done.45, s32[40,8]{1,0:T(8,128)S(1)} %copy-done.42, s32[1]{0:T(128)S(6)} %copy.68.lengths, s32[1]{0:T(128)} %bitcast.6.flips, ...), custom_call_target="tpu_custom_call" | custom-call | flops 1000000000 | bytes 1000000 | tf_op jit(solution)/shard_map/attend_backward/pallas_call | solution.py:253
  285.9 13.2 %joined_grads.1 = (bf16[16,48,640]{2,1,0:T(8,128)(2,1)S(1)}, bf16[16,48,640]{2,1,0:T(8,128)(2,1)S(1)}) custom-call(s32[2]{0:T(128)S(1)} %pad_add_fusion.3.places, s32[1]{0:T(128)} %bitcast.2.core, bf16[1024,768]{1,0:T(8,128)(2,1)} %bitcast.18, bf16[1024,768]{1,0:T(8,128)(2,1)} %copy-done.35, bf16[1024,768]{1,0:T(8,128)(2,1)} %collective-permute-done.x_ref.refs_2_, ...), custom_call_target="tpu_custom_call" | custom-call | flops 1000000000 | bytes 10000000 | tf_op jit(solution)/shard_map/joined_grads/pallas_call | solution.py:806
  302.7 4.9 collective-permute-done.20
  307.6 4.8 collective-permute-done.21
  323.3 9.9 %collective-permute-done.28 = bf16[1,64,768]{2,1,0:T(8,128)(2,1)S(1)} collective-permute-done((bf16[1,64,768]{2,1,0:T(8,128)(2,1)S(1)}, bf16[1,64,768]{2,1,0:T(8,128)(2,1)S(1)}, u32[]{:S(2)}, u32[]{:S(2)}) %collective-permute-start.28) | collective-permute-done | bytes 98336 | tf_op jit(solution)/shard_map/ppermute | solution.py:994
  333.3 5.7 %collective-permute-done.26 = bf16[2,48,768]{2,1,0:T(8,128)(2,1)S(1)} collective-permute-done((bf16[2,48,768]{2,1,0:T(8,128)(2,1)S(1)}, bf16[2,48,768]{2,1,0:T(8,128)(2,1)S(1)}, u32[]{:S(2)}, u32[]{:S(2)}) %collective-permute-start.26) | collective-permute-done | bytes 147488 | tf_op jit(solution)/shard_map/ppermute | solution.py:994
  345.5 8.4 %collective-permute-done.37 = bf16[1,64,768]{2,1,0:T(8,128)(2,1)S(1)} collective-permute-done((bf16[1,64,768]{2,1,0:T(8,128)(2,1)S(1)}, bf16[1,64,768]{2,1,0:T(8,128)(2,1)S(1)}, u32[]{:S(2)}, u32[]{:S(2)}) %collective-permute-start.37) | collective-permute-done | bytes 98336 | tf_op jit(solution)/shard_map/ppermute | solution.py:994
  366.3 5.3 %collective-permute-done.42 = bf16[2,64,768]{2,1,0:T(8,128)(2,1)S(1)} collective-permute-done((bf16[2,64,768]{2,1,0:T(8,128)(2,1)S(1)}, bf16[2,64,768]{2,1,0:T(8,128)(2,1)S(1)}, u32[]{:S(2)}, u32[]{:S(2)}) %collective-permute-start.42) | collective-permute-done | bytes 196640 | tf_op jit(solution)/shard_map/ppermute | solution.py:994
  390.1 19.0 %collective-permute-done.48 = bf16[1,48,640]{2,1,0:T(8,128)(2,1)S(1)} collective-permute-done((bf16[1,48,640]{2,1,0:T(8,128)(2,1)S(1)}, bf16[1,48,640]{2,1,0:T(8,128)(2,1)S(1)}, u32[]{:S(2)}, u32[]{:S(2)}) %collective-permute-start.48) | collective-permute-done | bytes 61472 | tf_op jit(solution)/shard_map/ppermute | solution.py:994
  416.9 6.1 %input_near.1 = bf16[2048,768]{1,0:T(8,128)(2,1)S(1)} custom-call(s32[1]{0:T(128)} %bitcast.2.core, bf16[768,2304]{1,0:T(8,128)(2,1)S(1)} %copy-done.1, bf16[768,2304]{1,0:T(8,128)(2,1)S(1)} %copy-done.1, bf16[768,2304]{1,0:T(8,128)(2,1)S(1)} %copy-done.1, bf16[2048,128]{1,0:T(8,128)(2,1)S(1)} %copy-done.33, ...), custom_call_target="tpu_custom_call" | custom-call | flops 1000000000 | bytes 10000000 | tf_op jit(solution)/shard_map/input_near/pallas_call | solution.py:837
  425.2 6.5 %collective-permute-done.55 = bf16[4,48,640]{2,1,0:T(8,128)(2,1)S(1)} collective-permute-done((bf16[4,48,640]{2,1,0:T(8,128)(2,1)S(1)}, bf16[4,48,640]{2,1,0:T(8,128)(2,1)S(1)}, u32[]{:S(2)}, u32[]{:S(2)}) %collective-permute-start.55) | collective-permute-done | bytes 245792 | tf_op jit(solution)/shard_map/ppermute | solution.py:994
  436.6 8.1 %collective-permute-done.56 = bf16[8,48,640]{2,1,0:T(8,128)(2,1)S(1)} collective-permute-done((bf16[8,48,640]{2,1,0:T(8,128)(2,1)S(1)}, bf16[8,48,640]{2,1,0:T(8,128)(2,1)S(1)}, u32[]{:S(2)}, u32[]{:S(2)}) %collective-permute-start.56) | collective-permute-done | bytes 491552 | tf_op jit(solution)/shard_map/ppermute | solution.py:994
  450.6 22.5 %unpack_shrink.1 = f32[3072,768]{1,0:T(8,128)} custom-call(s32[2]{0:T(128)S(1)} %copy-done.46, bf16[16,48,768]{2,1,0:T(8,128)(2,1)S(1)} %pad_maximum_fusion.3.first_own, bf16[16,48,768]{2,1,0:T(8,128)(2,1)S(1)} %collective-permute-done.62.first_other, bf16[16,48,768]{2,1,0:T(8,128)(2,1)S(1)} %pad_maximum_fusion.4.second_own, ...), custom_call_target="tpu_custom_call" | custom-call | flops 1000000 | bytes 1000000 | tf_op jit(solution)/shard_map/unpack_shrink/pallas_call | solution.py:882
  473.0 22.8 %unpack_expand.1 = (f32[768,3072]{1,0:T(8,128)}, f32[1024,768]{1,0:T(8,128)S(1)}) custom-call(s32[2]{0:T(128)S(1)} %copy-done.46, bf16[16,64,768]{2,1,0:T(8,128)(2,1)S(1)} %pad_maximum_fusion.1.first_own, bf16[16,64,768]{2,1,0:T(8,128)(2,1)S(1)} %collective-permute-done.60.first_other, bf16[16,64,768]{2,1,0:T(8,128)(2,1)S(1)} %pad_maximum_fusion.2.second_own, ...), custom_call_target="tpu_custom_call" | custom-call | flops 1000000 | bytes 1000000 | tf_op jit(solution)/shard_map/unpack_expand/pallas_call | solution.py:926
  500.5 10.6 %unpack_joined.1 = (f32[768,2304]{1,0:T(8,128)}, f32[768,256]{1,0:T(8,128)S(1)}) custom-call(s32[2]{0:T(128)S(1)} %pad_add_fusion.3.places, s32[1]{0:T(128)} %bitcast.2.core, bf16[16,48,640]{2,1,0:T(8,128)(2,1)S(1)} %pad_maximum_fusion.5.first_own, bf16[16,48,640]{2,1,0:T(8,128)(2,1)S(1)} %pad_maximum_fusion.6.second_own, ...), custom_call_target="tpu_custom_call" | custom-call | flops 1000000 | bytes 10000000 | tf_op jit(solution)/shard_map/unpack_joined/pallas_call | solution.py:974
  (330 shorter events, 167.8 us)
Async XLA Ops:
  1.2 37.9 %collective-permute-start = (bf16[1024,768]{1,0:T(8,128)(2,1)}, bf16[1024,768]{1,0:T(8,128)(2,1)}, u32[]{:S(2)}, u32[]{:S(2)}) collective-permute-start(bf16[1024,768]{1,0:T(8,128)(2,1)} %bitcast.16), channel_id=1, source_target_pairs={{0,2},{2,0},{1,3},{3,1},{4,6},{6,4},{5,7},{7,5},{8,10},{10,8},{9,1... | collective-permute-start | bytes 4718600 | tf_op jit(solution)/shard_map/ppermute | solution.py:994
  152.9 46.0 %collective-permute-start.5 = (bf16[8,48,768]{2,1,0:T(8,128)(2,1)}, bf16[8,48,768]{2,1,0:T(8,128)(2,1)}, u32[]{:S(2)}, u32[]{:S(2)}) collective-permute-start(bf16[8,48,768]{2,1,0:T(8,128)(2,1)} %get-tuple-element.137), channel_id=1, source_target_pairs={{0,4},{4,0},{8,12},{12,8},{16,20},{20,16},{24,28},{28,24},{1,5},{5... | collective-permute-start | bytes 1769480 | tf_op jit(solution)/shard_map/ppermute | solution.py:994
  154.7 45.8 %collective-permute-start.6 = (bf16[8,48,768]{2,1,0:T(8,128)(2,1)}, bf16[8,48,768]{2,1,0:T(8,128)(2,1)}, u32[]{:S(2)}, u32[]{:S(2)}) collective-permute-start(bf16[8,48,768]{2,1,0:T(8,128)(2,1)} %get-tuple-element.138), channel_id=1, source_target_pairs={{0,2},{2,0},{1,3},{3,1},{4,6},{6,4},{5,7},{7,5},{8,10},{10,8},{9,1... | collective-permute-start | bytes 1769480 | tf_op jit(solution)/shard_map/ppermute | solution.py:994
  203.9 23.2 %collective-permute-start.10 = (bf16[32,64,768]{2,1,0:T(8,128)(2,1)}, bf16[32,64,768]{2,1,0:T(8,128)(2,1)S(1)}, u32[]{:S(2)}, u32[]{:S(2)}) collective-permute-start(bf16[32,64,768]{2,1,0:T(8,128)(2,1)} %get-tuple-element.148), channel_id=1, source_target_pairs={{0,1},{1,0},{2,3},{3,2},{4,5},{5,4},{6,7},{7,6},{8,9},{9,8},{10,11... | collective-permute-start | bytes 9437192 | tf_op jit(solution)/shard_map/ppermute | solution.py:994
  204.4 20.9 %collective-permute-start.8 = (bf16[4,48,768]{2,1,0:T(8,128)(2,1)S(1)}, bf16[4,48,768]{2,1,0:T(8,128)(2,1)S(1)}, u32[]{:S(2)}, u32[]{:S(2)}) collective-permute-start(bf16[4,48,768]{2,1,0:T(8,128)(2,1)S(1)} %get-tuple-element.145), channel_id=1, source_target_pairs={{0,8},{4,12},{8,0},{12,4},{16,24},{20,28},{24,16},{28,20},{1,9},{5... | collective-permute-start | bytes 884744 | tf_op jit(solution)/shard_map/ppermute | solution.py:994
  206.0 20.3 %collective-permute-start.9 = (bf16[4,48,768]{2,1,0:T(8,128)(2,1)}, bf16[4,48,768]{2,1,0:T(8,128)(2,1)S(1)}, u32[]{:S(2)}, u32[]{:S(2)}) collective-permute-start(bf16[4,48,768]{2,1,0:T(8,128)(2,1)} %get-tuple-element.146), channel_id=1, source_target_pairs={{0,4},{4,0},{8,12},{12,8},{16,20},{20,16},{24,28},{28,24},{1,5},{5... | collective-permute-start | bytes 884744 | tf_op jit(solution)/shard_map/ppermute | solution.py:994
  229.6 31.3 %collective-permute-start.13 = (bf16[8,64,768]{2,1,0:T(8,128)(2,1)}, bf16[8,64,768]{2,1,0:T(8,128)(2,1)}, u32[]{:S(2)}, u32[]{:S(2)}) collective-permute-start(bf16[8,64,768]{2,1,0:T(8,128)(2,1)} %get-tuple-element.156), channel_id=1, source_target_pairs={{0,4},{4,0},{8,12},{12,8},{16,20},{20,16},{24,28},{28,24},{1,5},{5... | collective-permute-start | bytes 2359304 | tf_op jit(solution)/shard_map/ppermute | solution.py:994
  231.1 29.7 %collective-permute-start.11 = (bf16[2,48,768]{2,1,0:T(8,128)(2,1)}, bf16[2,48,768]{2,1,0:T(8,128)(2,1)S(1)}, u32[]{:S(2)}, u32[]{:S(2)}) collective-permute-start(bf16[2,48,768]{2,1,0:T(8,128)(2,1)} %get-tuple-element.154), channel_id=1, source_target_pairs={{0,16},{4,20},{8,24},{12,28},{16,0},{20,4},{24,8},{28,12},{1,17},{... | collective-permute-start | bytes 442376 | tf_op jit(solution)/shard_map/ppermute | solution.py:994
  233.8 27.0 %collective-permute-start.12 = (bf16[2,48,768]{2,1,0:T(8,128)(2,1)}, bf16[2,48,768]{2,1,0:T(8,128)(2,1)S(1)}, u32[]{:S(2)}, u32[]{:S(2)}) collective-permute-start(bf16[2,48,768]{2,1,0:T(8,128)(2,1)} %get-tuple-element.155), channel_id=1, source_target_pairs={{0,8},{4,12},{8,0},{12,4},{16,24},{20,28},{24,16},{28,20},{1,9},{5... | collective-permute-start | bytes 442376 | tf_op jit(solution)/shard_map/ppermute | solution.py:994
  234.2 28.4 %collective-permute-start.14 = (bf16[8,64,768]{2,1,0:T(8,128)(2,1)}, bf16[8,64,768]{2,1,0:T(8,128)(2,1)S(1)}, u32[]{:S(2)}, u32[]{:S(2)}) collective-permute-start(bf16[8,64,768]{2,1,0:T(8,128)(2,1)} %get-tuple-element.157), channel_id=1, source_target_pairs={{0,2},{2,0},{1,3},{3,1},{4,6},{6,4},{5,7},{7,5},{8,10},{10,8},{9,1... | collective-permute-start | bytes 2359304 | tf_op jit(solution)/shard_map/ppermute | solution.py:994
  262.9 21.7 %collective-permute-start.15 = (bf16[1,48,768]{2,1,0:T(8,128)(2,1)S(1)}, bf16[1,48,768]{2,1,0:T(8,128)(2,1)S(1)}, u32[]{:S(2)}, u32[]{:S(2)}) collective-permute-start(bf16[1,48,768]{2,1,0:T(8,128)(2,1)S(1)} %add_convert_fusion.43), channel_id=1, source_target_pairs={{0,2},{2,0},{1,3},{3,1},{4,6},{6,4},{5,7},{7,5},{8,10},{10,8},{9,1... | collective-permute-start | bytes 221192 | tf_op jit(solution)/shard_map/ppermute | solution.py:994
  264.4 20.1 %collective-permute-start.16 = (bf16[1,48,768]{2,1,0:T(8,128)(2,1)S(1)}, bf16[1,48,768]{2,1,0:T(8,128)(2,1)S(1)}, u32[]{:S(2)}, u32[]{:S(2)}) collective-permute-start(bf16[1,48,768]{2,1,0:T(8,128)(2,1)S(1)} %add_convert_fusion.42), channel_id=1, source_target_pairs={{0,16},{4,20},{8,24},{12,28},{16,0},{20,4},{24,8},{28,12},{1,17},{... | collective-permute-start | bytes 221192 | tf_op jit(solution)/shard_map/ppermute | solution.py:994
  316.8 22.5 %collective-permute-start.29 = (bf16[1024,768]{1,0:T(8,128)(2,1)S(1)}, bf16[1024,768]{1,0:T(8,128)(2,1)S(1)}, u32[]{:S(2)}, u32[]{:S(2)}) collective-permute-start(bf16[1024,768]{1,0:T(8,128)(2,1)S(1)} %slice.523), channel_id=1, source_target_pairs={{0,1},{1,0},{2,3},{3,2},{4,5},{5,4},{6,7},{7,6},{8,9},{9,8},{10,11... | collective-permute-start | bytes 4718600 | tf_op jit(solution)/shard_map/ppermute | solution.py:994
  317.7 21.3 %collective-permute-start.23 = (bf16[8,48,640]{2,1,0:T(8,128)(2,1)S(1)}, bf16[8,48,640]{2,1,0:T(8,128)(2,1)S(1)}, u32[]{:S(2)}, u32[]{:S(2)}) collective-permute-start(bf16[8,48,640]{2,1,0:T(8,128)(2,1)S(1)} %slice.413), channel_id=1, source_target_pairs={{0,4},{4,0},{8,12},{12,8},{16,20},{20,16},{24,28},{28,24},{1,5},{5... | collective-permute-start | bytes 1474568 | tf_op jit(solution)/shard_map/ppermute | solution.py:994
  319.1 20.0 %collective-permute-start.24 = (bf16[8,48,640]{2,1,0:T(8,128)(2,1)S(1)}, bf16[8,48,640]{2,1,0:T(8,128)(2,1)S(1)}, u32[]{:S(2)}, u32[]{:S(2)}) collective-permute-start(bf16[8,48,640]{2,1,0:T(8,128)(2,1)S(1)} %slice.414), channel_id=1, source_target_pairs={{0,2},{2,0},{1,3},{3,1},{4,6},{6,4},{5,7},{7,5},{8,10},{10,8},{9,1... | collective-permute-start | bytes 1474568 | tf_op jit(solution)/shard_map/ppermute | solution.py:994
  387.2 22.0 %collective-permute-start.50 = (bf16[8,64,768]{2,1,0:T(8,128)(2,1)S(1)}, bf16[8,64,768]{2,1,0:T(8,128)(2,1)S(1)}, u32[]{:S(2)}, u32[]{:S(2)}) collective-permute-start(bf16[8,64,768]{2,1,0:T(8,128)(2,1)S(1)} %pad_maximum_fusion.7), channel_id=1, source_target_pairs={{0,4},{4,0},{8,12},{12,8},{16,20},{20,16},{24,28},{28,24},{1,5},{5... | collective-permute-start | bytes 2359304 | tf_op jit(solution)/shard_map/ppermute | solution.py:994
  387.3 22.1 %collective-permute-start.51 = (bf16[8,64,768]{2,1,0:T(8,128)(2,1)S(1)}, bf16[8,64,768]{2,1,0:T(8,128)(2,1)S(1)}, u32[]{:S(2)}, u32[]{:S(2)}) collective-permute-start(bf16[8,64,768]{2,1,0:T(8,128)(2,1)S(1)} %pad_maximum_fusion.8), channel_id=1, source_target_pairs={{0,2},{2,0},{1,3},{3,1},{4,6},{6,4},{5,7},{7,5},{8,10},{10,8},{9,1... | collective-permute-start | bytes 2359304 | tf_op jit(solution)/shard_map/ppermute | solution.py:994
  388.0 21.2 %collective-permute-start.48 = (bf16[1,48,640]{2,1,0:T(8,128)(2,1)S(1)}, bf16[1,48,640]{2,1,0:T(8,128)(2,1)S(1)}, u32[]{:S(2)}, u32[]{:S(2)}) collective-permute-start(bf16[1,48,640]{2,1,0:T(8,128)(2,1)S(1)} %add_convert_fusion.47), channel_id=1, source_target_pairs={{0,2},{2,0},{1,3},{3,1},{4,6},{6,4},{5,7},{7,5},{8,10},{10,8},{9,1... | collective-permute-start | bytes 184328 | tf_op jit(solution)/shard_map/ppermute | solution.py:994
  389.4 47.3 %collective-permute-start.31 = (bf16[1024,768]{1,0:T(8,128)(2,1)S(1)}, bf16[1024,768]{1,0:T(8,128)(2,1)S(1)}, u32[]{:S(2)}, u32[]{:S(2)}) collective-permute-start(bf16[1024,768]{1,0:T(8,128)(2,1)S(1)} %add_convert_fusion), channel_id=1, source_target_pairs={{0,2},{2,0},{1,3},{3,1},{4,6},{6,4},{5,7},{7,5},{8,10},{10,8},{9,1... | collective-permute-start | bytes 4718600 | tf_op jit(solution)/shard_map/ppermute | solution.py:994
  423.1 24.4 %collective-permute-start.30 = (bf16[1024,768]{1,0:T(8,128)(2,1)S(1)}, bf16[1024,768]{1,0:T(8,128)(2,1)S(1)}, u32[]{:S(2)}, u32[]{:S(2)}) collective-permute-start(bf16[1024,768]{1,0:T(8,128)(2,1)S(1)} %slice.525), channel_id=1, source_target_pairs={{0,1},{1,0},{2,3},{3,2},{4,5},{5,4},{6,7},{7,6},{8,9},{9,8},{10,11... | collective-permute-start | bytes 4718600 | tf_op jit(solution)/shard_map/ppermute | solution.py:994
  436.6 36.4 %collective-permute-start.60 = (bf16[16,64,768]{2,1,0:T(8,128)(2,1)S(1)}, bf16[16,64,768]{2,1,0:T(8,128)(2,1)S(1)}, u32[]{:S(2)}, u32[]{:S(2)}) collective-permute-start(bf16[16,64,768]{2,1,0:T(8,128)(2,1)S(1)} %pad_maximum_fusion.1.first_own), channel_id=1, source_target_pairs={{0,1},{1,0},{2,3},{3,2},{4,5},{5,4},{6,7},{7,6},{8,9},{9,8},{10,11... | collective-permute-start | bytes 4718600 | tf_op jit(solution)/shard_map/ppermute | solution.py:994
  444.8 28.3 %collective-permute-start.61 = (bf16[16,64,768]{2,1,0:T(8,128)(2,1)S(1)}, bf16[16,64,768]{2,1,0:T(8,128)(2,1)S(1)}, u32[]{:S(2)}, u32[]{:S(2)}) collective-permute-start(bf16[16,64,768]{2,1,0:T(8,128)(2,1)S(1)} %pad_maximum_fusion.2.second_own), channel_id=1, source_target_pairs={{0,1},{1,0},{2,3},{3,2},{4,5},{5,4},{6,7},{7,6},{8,9},{9,8},{10,11... | collective-permute-start | bytes 4718600 | tf_op jit(solution)/shard_map/ppermute | solution.py:994
  447.5 53.0 %collective-permute-start.58 = (bf16[16,48,640]{2,1,0:T(8,128)(2,1)S(1)}, bf16[16,48,640]{2,1,0:T(8,128)(2,1)}, u32[]{:S(2)}, u32[]{:S(2)}) collective-permute-start(bf16[16,48,640]{2,1,0:T(8,128)(2,1)S(1)} %pad_maximum_fusion.5.first_own), channel_id=1, source_target_pairs={{0,1},{1,0},{2,3},{3,2},{4,5},{5,4},{6,7},{7,6},{8,9},{9,8},{10,11... | collective-permute-start | bytes 2949128 | tf_op jit(solution)/shard_map/ppermute | solution.py:994
  448.1 52.5 %collective-permute-start.59 = (bf16[16,48,640]{2,1,0:T(8,128)(2,1)S(1)}, bf16[16,48,640]{2,1,0:T(8,128)(2,1)}, u32[]{:S(2)}, u32[]{:S(2)}) collective-permute-start(bf16[16,48,640]{2,1,0:T(8,128)(2,1)S(1)} %pad_maximum_fusion.6.second_own), channel_id=1, source_target_pairs={{0,1},{1,0},{2,3},{3,2},{4,5},{5,4},{6,7},{7,6},{8,9},{9,8},{10,11... | collective-permute-start | bytes 2949128 | tf_op jit(solution)/shard_map/ppermute | solution.py:994
  (97 other events, 778.6 us)
